TPU v7x, 128 devices: a whole 4x4x4 slice. The times are simulated.
128 devices in a mesh: rep: 4 (over y), dom: 32 (over x, z, core).
Axes of the slice: x: 4, y: 4, z: 4, core: 2. Of those that a mesh axis runs over, the one named last changes fastest.
Arguments:
- features: bfloat16 [65536, 128], P('dom'), may hold values from -6 to 6
- proj_weight: bfloat16 [128, 256], replicated, may hold values from -0.5 to 0.5
- bias: float32 [256], replicated, may hold values from -3 to 3
- cotangent: bfloat16 [65536, 256], P('dom'), may hold values from -6 to 6
- send_rows: int32 [32, 32, 128], P('dom'), may hold values from 0 to 2047
- send_count: int32 [32, 32], P('dom'), may hold values from 32 to 128, as said below
- hub_blocks: int32 [8], replicated, may hold values from 0 to 511, as said below
- tile_dst: int32 [4, 32, 384], P('rep', 'dom'), may hold values from 0 to 15, as said below
- tile_src: int32 [4, 32, 384], P('rep', 'dom'), may hold values from 0 to 55
- tile_weight: bfloat16 [4, 32, 384, 128, 128], P('rep', 'dom'), may hold values from 0.0019989014 to 0.019897461
Outputs:
- output: bfloat16 [65536, 256], P('dom')
- grad_x: float32 [65536, 128], P('dom')
- grad_w: float32 [128, 256], replicated
Inputs may be any that keep to these rules, and one draw needn't show every extreme that they name: `send_count`: for every owner one peer's count is exactly 128 and another's exactly 32. `hub_blocks`: distinct block numbers; the first and the last block are always among them. On every device the pairs (tile_dst, tile_src) of its 384 tiles are distinct.
All inputs are finite; a program needn't handle non-finite values.
Results may differ from a plain program's by a relative error of at most 0.0061.
Values may be sent and summed in bfloat16 or wider, within the bound.
No kernel may reach another device: no remote copies, remote signals or barrier semaphores. Data moves between devices by JAX's collectives and lax.ppermute only.
A program may use at most 128 MiB of HBM per device.

v0:
```python
import math

import jax
import jax.numpy as jnp
from jax import lax
from jax.sharding import PartitionSpec as P

group_size = 16


def from_root(block, axis, holder):
    block = jnp.where(lax.axis_index(axis) == holder, block, jnp.zeros_like(block))
    return lax.psum(block, axis)


def activate(summed, bias, cotangent):
    pre = summed + bias
    activated, pullback = jax.vjp(jax.nn.gelu, pre)
    pre_grad = pullback(cotangent.astype(jnp.float32))[0]
    return (activated.astype(jnp.bfloat16), pre_grad.astype(jnp.bfloat16))


def shards(
    features,
    proj_weight,
    bias,
    cotangent,
    send_rows,
    send_count,
    hub_blocks,
    tile_dst,
    tile_src,
    tile_weight,
):
    row_count = features.shape[0]
    hid_width = proj_weight.shape[1]
    block_size = tile_weight.shape[-1]
    local_blocks = row_count // block_size
    dom_size = lax.axis_size("dom")
    dom_here = lax.axis_index("dom")
    targets = send_rows[0]
    counts = send_count[0]
    slot_total = targets.shape[1]
    live_slots = jnp.arange(slot_total, dtype=jnp.int32)[None, :] < counts[:, None]
    projected = jnp.dot(features, proj_weight, preferred_element_type=jnp.float32).astype(
        jnp.bfloat16
    )
    outgoing = jnp.where(live_slots[:, :, None], projected[targets], jnp.zeros((), jnp.bfloat16))
    remote = lax.all_to_all(outgoing, "dom", split_axis=0, concat_axis=0, tiled=True)
    hub_owner = hub_blocks // local_blocks
    hub_local = hub_blocks % local_blocks
    hub_count = hub_blocks.shape[0]
    proj_blocks = projected.reshape(local_blocks, block_size, hid_width)

    def fetch_hub(hub_index, held):
        hub_piece = lax.dynamic_index_in_dim(proj_blocks, hub_local[hub_index], 0, keepdims=False)
        received = from_root(hub_piece, "dom", hub_owner[hub_index])
        return lax.dynamic_update_index_in_dim(held, received, hub_index, 0)

    hub_data = lax.fori_loop(
        0, hub_count, fetch_hub, jnp.zeros((hub_count, block_size, hid_width), jnp.bfloat16)
    )
    blocks = jnp.concatenate([proj_blocks, remote, hub_data], 0)
    buffer_blocks = blocks.shape[0]
    dst_groups = tile_dst[0, 0].reshape(-1, group_size)
    src_groups = tile_src[0, 0].reshape(-1, group_size)
    weight_groups = tile_weight[0, 0].reshape(-1, group_size, block_size, block_size)

    def forward_step(totals, tile_group):
        dst_index, src_index, weights_here = tile_group
        products = jnp.einsum(
            "tij,tjh->tih", weights_here, blocks[src_index], preferred_element_type=jnp.float32
        )
        return (totals.at[dst_index].add(products), None)

    partial_sum, _ = lax.scan(
        forward_step,
        jnp.zeros((local_blocks, block_size, hid_width), jnp.float32),
        (dst_groups, src_groups, weight_groups),
    )
    partial_sum = partial_sum.reshape(row_count, hid_width)
    totals = lax.psum(partial_sum, "rep")
    output, pre_grad = activate(totals, bias, cotangent)
    grad_blocks = pre_grad.reshape(local_blocks, block_size, hid_width)

    def backward_step(totals, tile_group):
        dst_index, src_index, weights_here = tile_group
        products = jnp.einsum(
            "tij,tih->tjh", weights_here, grad_blocks[dst_index], preferred_element_type=jnp.float32
        )
        return (totals.at[src_index].add(products), None)

    source_grads, _ = lax.scan(
        backward_step,
        jnp.zeros((buffer_blocks, block_size, hid_width), jnp.float32),
        (dst_groups, src_groups, weight_groups),
    )
    flattened = source_grads.reshape(buffer_blocks * block_size, hid_width)
    remote_end = row_count + dom_size * slot_total
    local_part = flattened[:row_count]
    remote_grad = flattened[row_count:remote_end].reshape(dom_size, slot_total, hid_width)
    hub_grad = flattened[remote_end:].reshape(hub_count, block_size, hid_width)
    returned = lax.all_to_all(remote_grad, "dom", split_axis=0, concat_axis=0, tiled=True)
    returned = jnp.where(live_slots[:, :, None], returned, 0.0)
    local_part = local_part + jax.ops.segment_sum(
        returned.reshape(-1, hid_width), targets.reshape(-1), num_segments=row_count
    )
    hub_total = lax.psum(hub_grad, ("rep", "dom"))
    summed = lax.psum(local_part, "rep").reshape(local_blocks, block_size, hid_width)
    owned_part = jnp.where((hub_owner == dom_here)[:, None, None], hub_total, 0.0)
    summed = summed.at[hub_local].add(owned_part)
    dproj_b = summed.reshape(row_count, hid_width).astype(jnp.bfloat16)
    grad_x = jnp.dot(dproj_b, proj_weight.T, preferred_element_type=jnp.float32)
    weight_part = jnp.dot(features.T, dproj_b, preferred_element_type=jnp.float32)
    grad_w = lax.psum(weight_part, "dom") * (1.0 / math.sqrt(row_count * dom_size))
    return (output, grad_x, grad_w)


def solution(mesh):
    in_specs = (
        P("dom", None),
        P(),
        P(),
        P("dom", None),
        P("dom", None, None),
        P("dom", None),
        P(),
        P("rep", "dom", None),
        P("rep", "dom", None),
        P("rep", "dom", None, None, None),
    )
    out_specs = (P("dom", None), P("dom", None), P())
    return jax.shard_map(shards, mesh=mesh, in_specs=in_specs, out_specs=out_specs, check_vma=False)
```

profile of v0, /device:TPU:1, one launch (start us, length us, event | category | flops | bytes accessed | tf_op | source)
XLA Modules:
  0.0 1736.9 jit_solution(6575844088541602051)
XLA Ops:
  10.8 16.9 gather_fusion.2
  30.7 9.6 all-to-all-start
  40.6 805.5 %while.33 = (s32[]{:T(128)}, bf16[8,128,256]{2,1,0:T(8,128)(2,1)S(1)}, s32[8]{0:T(128)S(1)}, s32[8]{0:T(128)S(1)}, bf16[16,128,256]{2,1,0:T(8,128)(2,1)S(1)}, /*index=5*/s32[]{:T(128)}, s32[]{:T(128)}, s32[]{:T(128)}, u32[]{:T(128)}) while((s32[]{:T(128)}, bf16[8,128,256]{2,1,0:T(8,128)(2,1)S(1)}, s32[8]{0:T(128)S(1)}, s32[8]{0:T(128)S(1)}, ...), condition=%wide.region_2.3_spmd, body=%wide.region_0.2_spmd.sunk | while | flops 65544 | bytes 655597 | solution.py:60
  45.1 102.6 %all-reduce.14.cloned.1.call-done = bf16[1,128,256]{2,1,0:T(8,128)(2,1)} async-done(((bf16[1,128,256]{2,1,0:T(8,128)(2,1)}), bf16[1,128,256]{2,1,0:T(8,128)(2,1)}) %all-reduce.14.cloned.1.call-update) | async-done | bytes 65552 | tf_op jit(solution)/shard_map/while/body/eval_jaxpr/psum | solution.py:13
  152.9 94.4 %all-reduce.14.cloned.1.call-done = bf16[1,128,256]{2,1,0:T(8,128)(2,1)} async-done(((bf16[1,128,256]{2,1,0:T(8,128)(2,1)}), bf16[1,128,256]{2,1,0:T(8,128)(2,1)}) %all-reduce.14.cloned.1.call-update) | async-done | bytes 65552 | tf_op jit(solution)/shard_map/while/body/eval_jaxpr/psum | solution.py:13
  252.6 94.4 %all-reduce.14.cloned.1.call-done = bf16[1,128,256]{2,1,0:T(8,128)(2,1)} async-done(((bf16[1,128,256]{2,1,0:T(8,128)(2,1)}), bf16[1,128,256]{2,1,0:T(8,128)(2,1)}) %all-reduce.14.cloned.1.call-update) | async-done | bytes 65552 | tf_op jit(solution)/shard_map/while/body/eval_jaxpr/psum | solution.py:13
  352.3 94.3 %all-reduce.14.cloned.1.call-done = bf16[1,128,256]{2,1,0:T(8,128)(2,1)} async-done(((bf16[1,128,256]{2,1,0:T(8,128)(2,1)}), bf16[1,128,256]{2,1,0:T(8,128)(2,1)}) %all-reduce.14.cloned.1.call-update) | async-done | bytes 65552 | tf_op jit(solution)/shard_map/while/body/eval_jaxpr/psum | solution.py:13
  451.9 94.3 %all-reduce.14.cloned.1.call-done = bf16[1,128,256]{2,1,0:T(8,128)(2,1)} async-done(((bf16[1,128,256]{2,1,0:T(8,128)(2,1)}), bf16[1,128,256]{2,1,0:T(8,128)(2,1)}) %all-reduce.14.cloned.1.call-update) | async-done | bytes 65552 | tf_op jit(solution)/shard_map/while/body/eval_jaxpr/psum | solution.py:13
  551.5 94.3 %all-reduce.14.cloned.1.call-done = bf16[1,128,256]{2,1,0:T(8,128)(2,1)} async-done(((bf16[1,128,256]{2,1,0:T(8,128)(2,1)}), bf16[1,128,256]{2,1,0:T(8,128)(2,1)}) %all-reduce.14.cloned.1.call-update) | async-done | bytes 65552 | tf_op jit(solution)/shard_map/while/body/eval_jaxpr/psum | solution.py:13
  651.1 94.4 %all-reduce.14.cloned.1.call-done = bf16[1,128,256]{2,1,0:T(8,128)(2,1)} async-done(((bf16[1,128,256]{2,1,0:T(8,128)(2,1)}), bf16[1,128,256]{2,1,0:T(8,128)(2,1)}) %all-reduce.14.cloned.1.call-update) | async-done | bytes 65552 | tf_op jit(solution)/shard_map/while/body/eval_jaxpr/psum | solution.py:13
  750.8 94.4 %all-reduce.14.cloned.1.call-done = bf16[1,128,256]{2,1,0:T(8,128)(2,1)} async-done(((bf16[1,128,256]{2,1,0:T(8,128)(2,1)}), bf16[1,128,256]{2,1,0:T(8,128)(2,1)}) %all-reduce.14.cloned.1.call-update) | async-done | bytes 65552 | tf_op jit(solution)/shard_map/while/body/eval_jaxpr/psum | solution.py:13
  850.9 236.4 %while.34 = (s32[]{:T(128)}, f32[16,128,256]{2,1,0:T(8,128)}, s32[24,16]{1,0:T(8,128)S(1)}, bf16[24,16,128,128]{3,2,1,0:T(8,128)(2,1)}, s32[24,16]{1,0:T(8,128)S(1)}, /*index=5*/bf16[56,128,256]{2,1,0:T(8,128)(2,1)}, s32[]{:T(128)}) while((s32[]{:T(128)}, f32[16,128,256]{2,1,0:T(8,128)}, s32[24,16]{1,0:T(8,128)S(1)}, ...), condition=%wide.region_5.6_spmd, body=%wide.region_3.5_spmd.sunk | while | flops 134743136 | bytes 12063261 | solution.py:76
  974.4 4.5 scatter_fusion
  1087.4 16.1 copy.16
  1103.5 40.8 %all-reduce.6.cloned.1.call-done = f32[2048,256]{1,0:T(8,128)} async-done(((f32[2048,256]{1,0:T(8,128)}), f32[2048,256]{1,0:T(8,128)}) %all-reduce.6.cloned.1.call-update) | async-done | bytes 2097168 | tf_op jit(solution)/shard_map/psum | solution.py:82
  1144.3 4.6 fusion.18
  1152.7 221.3 %while.35 = (s32[]{:T(128)}, f32[56,128,256]{2,1,0:T(8,128)}, s32[24,16]{1,0:T(8,128)S(1)}, bf16[24,16,128,128]{2,3,1,0:T(8,128)(2,1)}, s32[24,16]{1,0:T(8,128)S(1)}, /*index=5*/bf16[16,128,256]{2,1,0:T(8,128)(2,1)}, s32[]{:T(128)}) while((s32[]{:T(128)}, f32[56,128,256]{2,1,0:T(8,128)}, s32[24,16]{1,0:T(8,128)S(1)}, ...), condition=%wide.region_9.10_spmd, body=%wide.region_7.9_spmd.sunk | while | flops 134743136 | bytes 12063261 | solution.py:93
  1157.4 4.5 scatter_fusion.1
  1166.5 4.6 scatter_fusion.1
  1175.8 4.5 scatter_fusion.1
  1185.0 4.5 scatter_fusion.1
  1194.2 4.6 scatter_fusion.1
  1203.4 4.6 scatter_fusion.1
  1212.7 4.6 scatter_fusion.1
  1222.0 4.6 scatter_fusion.1
  1231.3 4.6 scatter_fusion.1
  1240.5 4.6 scatter_fusion.1
  1249.7 4.6 scatter_fusion.1
  1258.9 4.5 scatter_fusion.1
  1268.1 4.5 scatter_fusion.1
  1277.3 4.6 scatter_fusion.1
  1286.5 4.5 scatter_fusion.1
  1295.7 4.6 scatter_fusion.1
  1305.0 4.5 scatter_fusion.1
  1314.1 4.5 scatter_fusion.1
  1323.3 4.5 scatter_fusion.1
  1332.5 4.5 scatter_fusion.1
  1341.6 4.6 scatter_fusion.1
  1350.9 4.6 scatter_fusion.1
  1360.1 4.6 scatter_fusion.1
  1369.4 4.6 scatter_fusion.1
  1374.0 4.6 slice.16
  1378.6 7.2 all-to-all-start.1
  1390.0 49.2 %all-to-all-done.1 = f32[32,128,256]{2,1,0:T(8,128)} async-done(((f32[32,128,256]{2,1,0:T(8,128)}), f32[32,128,256]{2,1,0:T(8,128)}, u32[]{:S(2)}, u32[]{:S(2)}) %all-to-all-start.1) | async-done | bytes 4194336 | tf_op jit(solution)/shard_map/all_to_all | solution.py:103
  1443.2 23.8 %scatter_fusion.2 = f32[2048,256]{1,0:T(8,128)S(1)} fusion(f32[2048,256]{1,0:T(8,128)S(1)} %bitcast.88, s32[4096]{0:T(1024)S(1)} %bitcast.99, f32[4096,256]{1,0:T(8,128)} %bitcast.95), kind=kCustom, calls=%fused_computation.5 | custom fusion | flops 1048576 | bytes 12599296 | tf_op jit(solution)/shard_map/scatter-add | solution.py:105
  1468.4 94.7 %all-reduce.10.cloned.1.call-done = f32[8,128,256]{2,1,0:T(8,128)} async-done(((f32[8,128,256]{2,1,0:T(8,128)}), f32[8,128,256]{2,1,0:T(8,128)}) %all-reduce.10.cloned.1.call-update) | async-done | bytes 1048592 | tf_op jit(solution)/shard_map/psum | solution.py:108
  1564.4 57.6 %all-reduce.8.cloned.1.call-done = f32[16,128,256]{2,1,0:T(8,128)} async-done(((f32[16,128,256]{2,1,0:T(8,128)}), f32[16,128,256]{2,1,0:T(8,128)}) %all-reduce.8.cloned.1.call-update) | async-done | bytes 2097168 | tf_op jit(solution)/shard_map/psum | solution.py:109
  1629.6 98.1 %all-reduce.12.cloned.1.call-done = f32[128,256]{0,1:T(8,128)} async-done(((f32[128,256]{0,1:T(8,128)}), f32[128,256]{0,1:T(8,128)}) %all-reduce.12.cloned.1.call-update) | async-done | bytes 131088 | tf_op jit(solution)/shard_map/psum | solution.py:115
  (314 shorter events, 399.2 us)
Async XLA Ops:
  8.0 1.5 copy-start
  30.7 9.7 copy-start.8
  30.7 9.7 copy-start.5
  30.7 9.7 copy-start.6
  30.7 815.4 %all-to-all-start = ((bf16[32,128,256]{2,1,0:T(8,128)(2,1)}), bf16[32,128,256]{2,1,0:T(8,128)(2,1)}, u32[]{:S(2)}, u32[]{:S(2)}) async-start(bf16[32,128,256]{2,1,0:T(8,128)(2,1)} %broadcast_select_fusion.1), calls=%async_computation | async-start | bytes 4194304 | tf_op jit(solution)/shard_map/all_to_all | solution.py:49
  40.6 107.1 %all-reduce.14.cloned.1.call-start = ((), (), s32[]{:S(2)}) async-start(), calls=%async_computation.6 | async-start | bytes 131072 | tf_op jit(solution)/shard_map/while/body/eval_jaxpr/psum | solution.py:13
  148.5 98.9 %all-reduce.14.cloned.1.call-start = ((), (), s32[]{:S(2)}) async-start(), calls=%async_computation.6 | async-start | bytes 131072 | tf_op jit(solution)/shard_map/while/body/eval_jaxpr/psum | solution.py:13
  248.2 98.9 %all-reduce.14.cloned.1.call-start = ((), (), s32[]{:S(2)}) async-start(), calls=%async_computation.6 | async-start | bytes 131072 | tf_op jit(solution)/shard_map/while/body/eval_jaxpr/psum | solution.py:13
  347.9 98.7 %all-reduce.14.cloned.1.call-start = ((), (), s32[]{:S(2)}) async-start(), calls=%async_computation.6 | async-start | bytes 131072 | tf_op jit(solution)/shard_map/while/body/eval_jaxpr/psum | solution.py:13
  447.5 98.7 %all-reduce.14.cloned.1.call-start = ((), (), s32[]{:S(2)}) async-start(), calls=%async_computation.6 | async-start | bytes 131072 | tf_op jit(solution)/shard_map/while/body/eval_jaxpr/psum | solution.py:13
  547.1 98.7 %all-reduce.14.cloned.1.call-start = ((), (), s32[]{:S(2)}) async-start(), calls=%async_computation.6 | async-start | bytes 131072 | tf_op jit(solution)/shard_map/while/body/eval_jaxpr/psum | solution.py:13
  646.7 98.9 %all-reduce.14.cloned.1.call-start = ((), (), s32[]{:S(2)}) async-start(), calls=%async_computation.6 | async-start | bytes 131072 | tf_op jit(solution)/shard_map/while/body/eval_jaxpr/psum | solution.py:13
  746.4 98.9 %all-reduce.14.cloned.1.call-start = ((), (), s32[]{:S(2)}) async-start(), calls=%async_computation.6 | async-start | bytes 131072 | tf_op jit(solution)/shard_map/while/body/eval_jaxpr/psum | solution.py:13
  846.1 298.2 %all-reduce.6.cloned.1.call-start = ((), (), s32[]{:S(2)}) async-start(), calls=%async_computation.2 | async-start | bytes 4194304 | tf_op jit(solution)/shard_map/psum | solution.py:82
  1087.4 57.0 %copy-start.2 = (bf16[2048,256]{1,0:T(8,128)(2,1)S(1)}, bf16[2048,256]{1,0:T(8,128)(2,1)}, u32[]{:S(2)}) copy-start(bf16[2048,256]{1,0:T(8,128)(2,1)} %param.19) | copy-start | bytes 3145732
  1087.4 57.0 %copy-start.7 = (f32[256]{0:T(256)S(1)}, f32[256]{0:T(256)}, u32[]{:S(2)}) copy-start(f32[256]{0:T(256)} %param.18) | copy-start | bytes 3076
  1378.6 60.6 %all-to-all-start.1 = ((f32[32,128,256]{2,1,0:T(8,128)}), f32[32,128,256]{2,1,0:T(8,128)}, u32[]{:S(2)}, u32[]{:S(2)}) async-start(f32[32,128,256]{2,1,0:T(8,128)} %slice.16), calls=%async_computation.1 | async-start | bytes 8388608 | tf_op jit(solution)/shard_map/all_to_all | solution.py:103
  1385.8 177.2 %all-reduce.10.cloned.1.call-start = ((), (), s32[]{:S(2)}) async-start(), calls=%async_computation.4 | async-start | bytes 2097152 | tf_op jit(solution)/shard_map/psum | solution.py:108
  1388.2 233.8 %all-reduce.8.cloned.1.call-start = ((), (), s32[]{:S(2)}) async-start(), calls=%async_computation.3 | async-start | bytes 4194304 | tf_op jit(solution)/shard_map/psum | solution.py:109
  1390.0 53.2 %copy-start.4 = (s32[1,32,128]{2,1,0:T(8,128)S(1)}, s32[1,32,128]{2,1,0:T(8,128)}, u32[]{:S(2)}) copy-start(s32[1,32,128]{2,1,0:T(8,128)} %param.20) | copy-start | bytes 49156
  1467.0 1.3 copy-start.1
  1468.3 259.3 %all-reduce.12.cloned.1.call-start = ((), (), s32[]{:S(2)}) async-start(), calls=%async_computation.5 | async-start | bytes 262144 | tf_op jit(solution)/shard_map/psum | solution.py:115
  1625.3 2.9 copy-start.3
Sparse Core Ops, SparseCore 0:
  45.3 102.3 all-reduce.13
  153.2 94.1 all-reduce.13
  252.9 94.1 all-reduce.13
  352.5 94.1 all-reduce.13
  452.1 94.1 all-reduce.13
  551.6 94.1 all-reduce.13
  651.4 94.1 all-reduce.13
  751.1 94.1 all-reduce.13
Sparse Core Ops, SparseCore 1:
  1087.4 56.8 all-reduce.5
  1392.4 170.6 all-reduce.9
  1565.3 56.7 all-reduce.7
  1628.3 99.4 all-reduce.11
where the time goes:
time: 1740 us
  waiting for transfers between devices  1100 us (63%)
  other arithmetic  268 us (15%)
  local copies, waits for them, and re-layouts  220 us (13%)
  matrix products  90.4 us (5%)
  loops' own time  21.5 us (1%)
    psum x8, waiting for transfers between devices, from_root(): return lax.psum(block, axis)  763 us
    scatter-add x24, other arithmetic, backward_step(): return (totals.at[src_index].add(products), None)  109 us
    scatter-add x24, other arithmetic, forward_step(): return (totals.at[dst_index].add(products), None)  106 us
    psum x1, waiting for transfers between devices, shards(): lax.psum(weight_part, 'dom') * (1.0 / math.sqrt(row_count * dom_size))  98.1 us
    psum x1, waiting for transfers between devices, shards(): hub_total = lax.psum(hub_grad, ('rep', 'dom'))  94.7 us
    gather x24, local copies, waits for them, and re-layouts, forward_step(): blocks[src_index]  86.9 us
    gather x24, local copies, waits for them, and re-layouts, backward_step(): grad_blocks[dst_index]  67.9 us
    psum x1, waiting for transfers between devices, shards(): lax.psum(local_part, 'rep').reshape(local_blocks, block_size, hid_width)  57.6 us
  transfers between devices with their start and end apart: 14, of which 13 were waited for; matrix products, arithmetic and copies ran while one was open for 4% of the time, Pallas kernels for 0%

commit v1 on v0

v1 whole, which is shorter than its diff:
```python
import functools
import math

import jax
import jax.numpy as jnp
from jax import lax
from jax.experimental import pallas as pl
from jax.experimental.pallas import tpu as pltpu
from jax.sharding import PartitionSpec as P

F32 = jnp.float32
BF16 = jnp.bfloat16
BLK = 128
N_REP = 4
N_DOM = 32
FIN = 128
HID = 256
ROWS = 2048
LOCAL = ROWS // BLK
HUBS = 8
BLOCKS = LOCAL + N_DOM + HUBS
TILES = 384
GROUP = 16
HUB_ROWS = HUBS * BLK // N_DOM
QUARTER = ROWS // N_REP
QB = LOCAL // N_REP
FQ = FIN // N_REP
MSG = FQ + 16
LO = 256
VMEM_LIMIT = 48 * 1024 * 1024

VM = pl.BlockSpec(memory_space=pltpu.VMEM)
SM = pl.BlockSpec(memory_space=pltpu.SMEM)
PARAMS = pltpu.CompilerParams(vmem_limit_bytes=VMEM_LIMIT)


def dot(a, b):
    return jnp.dot(a, b, preferred_element_type=F32)


def halves(x):
    high = x.astype(BF16)
    return high, (x - high.astype(F32)).astype(BF16)


def column(row):
    return jnp.broadcast_to(row, (BLK, BLK)).T


def low_onehot(col):
    low = jnp.where(col < 0, -1, col & (LO - 1))
    lane = lax.broadcasted_iota(jnp.int32, (BLK, BLK), 1)
    return jnp.concatenate(
        [jnp.where(low == lane + k * BLK, 1.0, 0.0) for k in range(LO // BLK)], axis=1
    ).astype(BF16)


def gather_kernel(index_ref, feat_ref, out_ref):
    def step(p, carry):
        col = column(index_ref[pl.ds(p, 1), :])
        hot = low_onehot(col)
        high = lax.shift_right_arithmetic(col, 8)
        total = jnp.zeros((BLK, FIN), F32)
        for pair in range(ROWS // LO // 2):
            left = feat_ref[pl.ds(2 * pair * LO, LO), :]
            right = feat_ref[pl.ds((2 * pair + 1) * LO, LO), :]
            got = dot(hot, jnp.concatenate([left, right], axis=1))
            total = jnp.where(high == 2 * pair, got[:, :FIN], total)
            total = jnp.where(high == 2 * pair + 1, got[:, FIN:], total)
        out_ref[pl.ds(p, 1), pl.ds(0, BLK), :] = total.astype(BF16)[None]
        return carry

    lax.fori_loop(0, N_DOM, step, 0)


def gather_rows(index, features):
    return pl.pallas_call(
        gather_kernel,
        out_shape=jax.ShapeDtypeStruct((N_DOM, BLK + HUB_ROWS, FIN), BF16),
        in_specs=[VM, VM],
        out_specs=VM,
        compiler_params=PARAMS,
        cost_estimate=pl.CostEstimate(flops=4 * 10**9, bytes_accessed=2 * 10**6, transcendentals=0),
        name="gather_rows",
    )(index, features)


def forward_kernel(
    dst_ref, src_ref, rep_ref, feat_ref, recv_ref, w_ref, own_ref, s1_ref, s2_ref, s3_ref, xs, acc
):
    step = pl.program_id(0)

    @pl.when(step == 0)
    def _():
        xs[pl.ds(0, LOCAL)] = feat_ref[...]
        xs[pl.ds(LOCAL, N_DOM)] = recv_ref[:, pl.ds(0, BLK), :]
        per_hub = BLK // HUB_ROWS
        for p in range(N_DOM):
            xs[LOCAL + N_DOM + p // per_hub, pl.ds((p % per_hub) * HUB_ROWS, HUB_ROWS), :] = recv_ref[
                p, pl.ds(BLK, HUB_ROWS), :
            ]
        acc[...] = jnp.zeros_like(acc)

    for base in range(0, GROUP, 4):
        found = []
        for k in range(base, base + 4):
            t = step * GROUP + k
            found.append((dst_ref[t], dot(w_ref[k], xs[src_ref[t]])))
        for d, value in found:
            acc[d] += value

    @pl.when(step == pl.num_programs(0) - 1)
    def _():
        rep = rep_ref[0]
        own_ref[...] = acc[pl.ds(rep * QB, QB)]
        for k, ref in ((1, s1_ref), (2, s2_ref), (3, s3_ref)):
            ref[...] = acc[pl.ds(lax.rem(rep + k, N_REP) * QB, QB)].astype(BF16)


def forward_tiles(dst, src, rep, features, received, weights):
    quarter = (QB, BLK, FIN)
    whole = lambda shape: pl.BlockSpec(shape, lambda i: (0,) * len(shape))
    return pl.pallas_call(
        forward_kernel,
        grid=(TILES // GROUP,),
        out_shape=[jax.ShapeDtypeStruct(quarter, F32)] + [jax.ShapeDtypeStruct(quarter, BF16)] * 3,
        in_specs=[
            SM,
            SM,
            SM,
            whole((LOCAL, BLK, FIN)),
            whole((N_DOM, BLK + HUB_ROWS, FIN)),
            pl.BlockSpec((GROUP, BLK, BLK), lambda i: (i, 0, 0)),
        ],
        out_specs=[whole(quarter)] * 4,
        scratch_shapes=[pltpu.VMEM((BLOCKS, BLK, FIN), BF16), pltpu.VMEM((LOCAL, BLK, FIN), F32)],
        compiler_params=PARAMS,
        cost_estimate=pl.CostEstimate(flops=4 * 10**9, bytes_accessed=14 * 10**6, transcendentals=0),
        name="forward_tiles",
    )(dst, src, rep, features, received, weights)


def middle_kernel(own_ref, a_ref, b_ref, c_ref, w_ref, bias_ref, cot_ref, out_ref, y_ref, gw_ref):
    zx = (own_ref[...] + a_ref[...].astype(F32)) + (b_ref[...].astype(F32) + c_ref[...].astype(F32))
    zx = zx.reshape(QUARTER, FIN)
    weight = w_ref[...]
    zh, zl = halves(zx)
    pre = dot(zh, weight) + dot(zl, weight) + bias_ref[...]
    root = math.sqrt(2.0 / math.pi)
    square = pre * pre
    bent = jnp.tanh(root * (pre + 0.044715 * (square * pre)))
    cdf = 0.5 * (1.0 + bent)
    out_ref[...] = (pre * cdf).astype(BF16)
    slope = cdf + (0.5 * pre) * ((1.0 - bent * bent) * (root * (1.0 + (3 * 0.044715) * square)))
    pre_grad = (cot_ref[...].astype(F32) * slope).astype(BF16)
    yt = lax.dot_general(weight, pre_grad, (((1,), (1,)), ((), ())), preferred_element_type=F32)
    yt = yt.astype(BF16)
    for k in range(QB):
        y_ref[k] = yt[:, k * BLK : (k + 1) * BLK]
    th, tl = halves(zx.T)
    gw = dot(th, pre_grad) + dot(tl, pre_grad)
    for part, piece in enumerate(halves(gw)):
        for c in range(16):
            g, side = c // 2, c % 2
            gw_ref[part * 16 + c] = piece[g * 16 : (g + 1) * 16, side * BLK : (side + 1) * BLK]


def middle(rep, own, a, b, c, weight, bias, cotangent):
    whole = lambda shape: pl.BlockSpec(shape, lambda i, rep_ref: (0,) * len(shape))
    quarter = (QB, BLK, FIN)
    return pl.pallas_call(
        lambda rep_ref, *refs: middle_kernel(*refs),
        grid_spec=pltpu.PrefetchScalarGridSpec(
            num_scalar_prefetch=1,
            grid=(1,),
            in_specs=[whole(quarter)] * 4
            + [
                whole((FIN, HID)),
                whole((1, HID)),
                pl.BlockSpec((QUARTER, HID), lambda i, rep_ref: (rep_ref[0], 0)),
            ],
            out_specs=[whole((QUARTER, HID)), whole((QB, FIN, BLK)), whole((32, 16, BLK))],
        ),
        out_shape=[
            jax.ShapeDtypeStruct((QUARTER, HID), BF16),
            jax.ShapeDtypeStruct((QB, FIN, BLK), BF16),
            jax.ShapeDtypeStruct((32, 16, BLK), BF16),
        ],
        compiler_params=PARAMS,
        name="middle",
    )(rep, own, a, b, c, weight, bias, cotangent)


def backward_kernel(
    dst_ref, src_ref, rep_ref, y0, y1, y2, y3, gw_ref, w_ref, msg_ref, own_ref, s1, s2, s3, ys, acc
):
    step = pl.program_id(0)
    rep = rep_ref[0]

    @pl.when(step == 0)
    def _():
        for k, ref in enumerate((y0, y1, y2, y3)):
            ys[pl.ds(lax.rem(rep + N_REP - k, N_REP) * QB, QB)] = ref[...]
        acc[...] = jnp.zeros_like(acc)

    for base in range(0, GROUP, 4):
        found = []
        for k in range(base, base + 4):
            t = step * GROUP + k
            found.append((src_ref[t], dot(ys[dst_ref[t]], w_ref[k])))
        for s, value in found:
            acc[s] += value

    @pl.when(step == pl.num_programs(0) - 1)
    def _():
        for q in range(N_REP):
            rows = pl.ds(q * FQ, FQ)
            msg_ref[q, :, pl.ds(0, FQ), :] = acc[pl.ds(LOCAL, N_DOM), rows, :].astype(BF16)
            for m in range(16):
                piece = acc[LOCAL + N_DOM + m // 2, pl.ds(q * FQ + (m % 2) * 16, 16), :]
                msg_ref[q, 2 * m, pl.ds(FQ, 16), :] = piece.astype(BF16)
                if m < 8:
                    msg_ref[q, 2 * m + 1, pl.ds(FQ, 16), :] = gw_ref[q * 8 + m]
                else:
                    msg_ref[q, 2 * m + 1, pl.ds(FQ, 16), :] = jnp.zeros((16, BLK), BF16)
        def rows_of(k):
            start = pl.multiple_of(lax.rem(rep + k, N_REP) * FQ, FQ)
            return acc[pl.ds(0, LOCAL), pl.ds(start, FQ), :]
        own_ref[...] = rows_of(0)
        for k, ref in ((1, s1), (2, s2), (3, s3)):
            ref[...] = rows_of(k).astype(BF16)


def backward_tiles(dst, src, rep, ys, gw, weights):
    whole = lambda shape: pl.BlockSpec(shape, lambda i: (0,) * len(shape))
    part = (LOCAL, FQ, BLK)
    return pl.pallas_call(
        backward_kernel,
        grid=(TILES // GROUP,),
        out_shape=[
            jax.ShapeDtypeStruct((N_REP, N_DOM, MSG, BLK), BF16),
            jax.ShapeDtypeStruct(part, F32),
        ]
        + [jax.ShapeDtypeStruct(part, BF16)] * 3,
        in_specs=[SM, SM, SM]
        + [whole((QB, FIN, BLK))] * 4
        + [whole((32, 16, BLK)), pl.BlockSpec((GROUP, BLK, BLK), lambda i: (i, 0, 0))],
        out_specs=[whole((N_REP, N_DOM, MSG, BLK))] + [whole(part)] * 4,
        scratch_shapes=[pltpu.VMEM((LOCAL, FIN, BLK), BF16), pltpu.VMEM((BLOCKS, FIN, BLK), F32)],
        compiler_params=PARAMS,
        cost_estimate=pl.CostEstimate(flops=4 * 10**9, bytes_accessed=14 * 10**6, transcendentals=0),
        name="backward_tiles",
    )(dst, src, rep, *ys, gw, weights)


def scatter_kernel(index_ref, recv_ref, own_ref, a_ref, b_ref, c_ref, out_ref, acc):
    chunks = ROWS // LO
    acc[...] = jnp.zeros_like(acc)

    def step(i, carry):
        hots, sides = [], []
        for j in range(2):
            p = 2 * i + j
            row = index_ref[pl.ds(p, 1), :]
            hots.append(low_onehot(column(row)))
            total = recv_ref[p, pl.ds(0, FQ), :].astype(F32)
            for r in range(1, N_REP):
                total = total + recv_ref[r * N_DOM + p, pl.ds(0, FQ), :].astype(F32)
            high = lax.shift_right_arithmetic(row, 8)
            here = [jnp.where(high == c, total, 0.0) for c in range(chunks)]
            pieces = [halves(h) for h in here]
            sides.append(jnp.concatenate([h for h, _ in pieces] + [l for _, l in pieces], axis=0))
        acc[...] += dot(jnp.concatenate(sides, axis=1), jnp.concatenate(hots, axis=0))
        return carry

    lax.fori_loop(0, N_DOM // 2, step, 0)
    for b in range(LOCAL):
        c, side = b // 2, b % 2
        lanes = pl.ds(side * BLK, BLK)
        here = acc[pl.ds(c * FQ, FQ), lanes] + acc[pl.ds((chunks + c) * FQ, FQ), lanes]
        near = own_ref[b] + a_ref[b].astype(F32) + b_ref[b].astype(F32) + c_ref[b].astype(F32)
        out_ref[b] = here + near


def scatter_rows(index, received, own, a, b, c):
    return pl.pallas_call(
        scatter_kernel,
        out_shape=jax.ShapeDtypeStruct((LOCAL, FQ, BLK), F32),
        in_specs=[VM] * 6,
        out_specs=VM,
        scratch_shapes=[pltpu.VMEM((2 * FIN * 2, LO), F32)],
        compiler_params=PARAMS,
        cost_estimate=pl.CostEstimate(flops=4 * 10**9, bytes_accessed=4 * 10**6, transcendentals=0),
        name="scatter_rows",
    )(index, received, own, a, b, c)


def hub_kernel(dom_ref, hub_ref, part_ref, shared_ref, out_ref):
    out_ref[pl.ds(0, LOCAL * FQ), :] = part_ref[...].reshape(LOCAL * FQ, BLK)
    for h in range(HUBS):
        block = hub_ref[h]

        @pl.when(lax.shift_right_logical(block, 4) == dom_ref[0])
        def _():
            start = pl.multiple_of((block & (LOCAL - 1)) * FQ, FQ)
            for k in range(2):
                out_ref[pl.ds(start + k * 16, 16), :] += shared_ref[4 * h + 2 * k]

    for m in range(8):
        out_ref[pl.ds(LOCAL * FQ + m * 16, 16), :] = shared_ref[2 * m + 1]


def add_hubs(dom, hubs, part, shared):
    return pl.pallas_call(
        hub_kernel,
        out_shape=jax.ShapeDtypeStruct((LOCAL * FQ + 128, BLK), F32),
        in_specs=[SM, SM, VM, VM],
        out_specs=VM,
        compiler_params=PARAMS,
        name="add_hubs",
    )(dom, hubs, part, shared)


def final_kernel(rep_ref, m0, m1, m2, m3, gx_ref, gw_ref, blocks, chunks, *, scale):
    rep = rep_ref[0]
    for k, ref in enumerate((m0, m1, m2, m3)):
        q = lax.rem(rep + N_REP - k, N_REP)
        start = pl.multiple_of(q * FQ, FQ)
        blocks[:, pl.ds(start, FQ), :] = ref[pl.ds(0, LOCAL * FQ), :].reshape(LOCAL, FQ, BLK)
        chunks[pl.ds(q * 8, 8)] = ref[pl.ds(LOCAL * FQ, 128), :].reshape(8, 16, BLK)
    for b in range(LOCAL):
        gx_ref[pl.ds(b * BLK, BLK), :] = blocks[b].T
    for c in range(16):
        g, side = c // 2, c % 2
        gw_ref[pl.ds(g * 16, 16), pl.ds(side * BLK, BLK)] = (chunks[c] + chunks[16 + c]) * scale


def finish(rep, parts, scale):
    return pl.pallas_call(
        functools.partial(final_kernel, scale=scale),
        out_shape=[
            jax.ShapeDtypeStruct((ROWS, FIN), F32),
            jax.ShapeDtypeStruct((FIN, HID), F32),
        ],
        in_specs=[SM] + [VM] * 4,
        out_specs=[VM, VM],
        scratch_shapes=[pltpu.VMEM((LOCAL, FIN, BLK), F32), pltpu.VMEM((32, 16, BLK), F32)],
        compiler_params=PARAMS,
        name="finish",
    )(rep, *parts)


def place_kernel(rep_ref, o0, o1, o2, o3, out_ref):
    for k, ref in enumerate((o0, o1, o2, o3)):
        start = pl.multiple_of(lax.rem(rep_ref[0] + N_REP - k, N_REP) * QUARTER, QUARTER)
        out_ref[pl.ds(start, QUARTER), :] = ref[...]


def place_output(rep, parts):
    return pl.pallas_call(
        place_kernel,
        out_shape=jax.ShapeDtypeStruct((ROWS, HID), BF16),
        in_specs=[SM] + [VM] * 4,
        out_specs=VM,
        compiler_params=PARAMS,
        name="place_output",
    )(rep, *parts)


def turn(value, k):
    return lax.ppermute(value, "rep", [(i, (i + k) % N_REP) for i in range(N_REP)])


def around(value):
    return [value] + [turn(value, k) for k in (1, 2, 3)]


def swap(value, axes):
    return lax.all_to_all(value, axes, split_axis=0, concat_axis=0, tiled=True)


def shards(
    features,
    proj_weight,
    bias,
    cotangent,
    send_rows,
    send_count,
    hub_blocks,
    tile_dst,
    tile_src,
    tile_weight,
):
    dom_here = lax.axis_index("dom")
    rep = lax.axis_index("rep").astype(jnp.int32).reshape(1)
    dom = dom_here.astype(jnp.int32).reshape(1)
    slots = jnp.arange(BLK, dtype=jnp.int32)[None, :]
    index = jnp.where(slots < send_count[0][:, None], send_rows[0], -1)
    blocks = features.reshape(LOCAL, BLK, FIN)
    dst, src, weights = tile_dst[0, 0], tile_src[0, 0], tile_weight[0, 0]

    hub_owner = hub_blocks // LOCAL
    mine = (hub_owner == dom_here)[:, None, None]
    hub_rows = jnp.where(mine, blocks[hub_blocks % LOCAL], jnp.zeros((), BF16))
    spread = swap(hub_rows.reshape(N_DOM, HUB_ROWS, FIN), "dom")
    listed = gather_rows(index, features)
    holder = hub_owner[dom_here // (BLK // HUB_ROWS)]
    piece = lax.dynamic_index_in_dim(spread, holder, 0, keepdims=True)
    piece = jnp.broadcast_to(piece, (N_DOM, HUB_ROWS, FIN))
    outgoing = lax.dynamic_update_slice(listed, piece, (0, BLK, 0))
    received = swap(outgoing, "dom")

    own, s1, s2, s3 = forward_tiles(dst, src, rep, blocks, received, weights)
    a, b, c = turn(s1, 1), turn(s2, 2), turn(s3, 3)
    out_part, y_part, gw_part = middle(
        rep, own, a, b, c, proj_weight, bias.reshape(1, HID), cotangent
    )
    ys = around(y_part)
    message, own, s1, s2, s3 = backward_tiles(dst, src, rep, ys, gw_part, weights)
    returned = swap(message.reshape(N_REP * N_DOM, MSG, BLK), ("rep", "dom"))
    a, b, c = turn(s1, 1), turn(s2, 2), turn(s3, 3)
    output = place_output(rep, around(out_part))

    chunk = jnp.sum(returned[:, FQ:, :].astype(F32), axis=0)
    shared = swap(jnp.broadcast_to(chunk[None], (N_DOM, 16, BLK)), "dom")
    part = scatter_rows(index, returned, own, a, b, c)
    whole = add_hubs(dom, hub_blocks, part, shared)
    grad_x, grad_w = finish(rep, around(whole), 1.0 / math.sqrt(ROWS * N_DOM))
    return (output, grad_x, grad_w)


def solution(mesh):
    in_specs = (
        P("dom", None),
        P(),
        P(),
        P("dom", None),
        P("dom", None, None),
        P("dom", None),
        P(),
        P("rep", "dom", None),
        P("rep", "dom", None),
        P("rep", "dom", None, None, None),
    )
    out_specs = (P("dom", None), P("dom", None), P())
    return jax.shard_map(shards, mesh=mesh, in_specs=in_specs, out_specs=out_specs, check_vma=False)
```

time: 1740 us -> 191 us (0.11)
  waiting for transfers between devices: 1100 us -> 74.9 us
  other arithmetic: 268 us -> 2.45 us
  local copies, waits for them, and re-layouts: 220 us -> 3.89 us
  matrix products: 90.4 us -> 0 us
  Pallas kernels: 0 us -> 55.8 us
  starting transfers between devices: 17 us -> 49.7 us
  loops' own time: 21.5 us -> 0 us
    psum x12 -> x0, waiting for transfers between devices: 1050 us -> none  [the longest x8 763 us: from_root(): return lax.psum(block, axis)]
    scatter-add x50 -> x0, other arithmetic: 242 us -> none  [the longest x24 109 us: backward_step(): return (totals.at[src_index].add(products), None)]
    gather x49 -> x1, local copies, waits for them, and re-layouts: 172 us -> 1.64 us  [shards(): hub_rows = jnp.where(mine, blocks[hub_blocks % LOCAL], jnp.zeros((), BF16))]
    dot_general x51 -> x0, matrix products: 90.4 us -> none  [the longest x24 43.3 us: backward_step(): jnp.einsum('tij,tih->tjh', weights_here, grad_blocks[dst_index], preferre...]
    pallas_call x0 -> x8, Pallas kernels: none -> 55.8 us  [the longest x1 18.9 us: backward_tiles(): pl.pallas_call(backward_kernel, grid=(TILES // GROUP,), out_shape=[jax.Sh...]
    ppermute x0 -> x15, waiting for transfers between devices: none -> 32.7 us  [turn(): lax.ppermute(value, 'rep', [(i, (i + k) % N_REP) for i in range(N_REP)])]
    another operation x3 -> x0, loops' own time: 21.5 us -> none  [the longest x1 20.8 us: shards(): lax.fori_loop(0, hub_count, fetch_hub, jnp.zeros((hub_count, block_size,...]
    ppermute x0 -> x15, starting transfers between devices: none -> 20.5 us  [turn(): lax.ppermute(value, 'rep', [(i, (i + k) % N_REP) for i in range(N_REP)])]
  transfers between devices with their start and end apart: 14 -> 19, of which waited for: 13 -> 10; matrix products, arithmetic and copies ran while one was open for 4% -> 1% of each run, Pallas kernels for 0% -> 9%
where the time goes in v1:
time: 191 us; the launch traced here: 190 us
  waiting for transfers between devices  74.9 us (39%)
  Pallas kernels  55.8 us (29%)
  starting transfers between devices  49.7 us (26%)
  local copies, waits for them, and re-layouts  3.89 us (2%)
  between operations  2.79 us (1%)
  other arithmetic  2.45 us (1%)
    all_to_all x4, waiting for transfers between devices, swap(): return lax.all_to_all(value, axes, split_axis=0, concat_axis=0, tiled=True)  42.2 us
    ppermute x15, waiting for transfers between devices, turn(): lax.ppermute(value, 'rep', [(i, (i + k) % N_REP) for i in range(N_REP)])  32.7 us
    all_to_all x4, starting transfers between devices, swap(): return lax.all_to_all(value, axes, split_axis=0, concat_axis=0, tiled=True)  29.2 us
    ppermute x15, starting transfers between devices, turn(): lax.ppermute(value, 'rep', [(i, (i + k) % N_REP) for i in range(N_REP)])  20.5 us
    pallas_call x1, Pallas kernels, backward_tiles(): pl.pallas_call(backward_kernel, grid=(TILES // GROUP,), out_shape=[jax.Sh...  18.9 us
    pallas_call x1, Pallas kernels, forward_tiles(): pl.pallas_call(forward_kernel, grid=(TILES // GROUP,), out_shape=[jax.Sha...  17.6 us
    pallas_call x1, Pallas kernels, gather_rows(): pl.pallas_call(gather_kernel, out_shape=jax.ShapeDtypeStruct((N_DOM, BLK...  9.98 us
    pallas_call x1, Pallas kernels, scatter_rows(): pl.pallas_call(scatter_kernel, out_shape=jax.ShapeDtypeStruct((LOCAL, FQ,...  5.28 us
  transfers between devices with their start and end apart: 19, of which 10 were waited for; matrix products, arithmetic and copies ran while one was open for 1% of the time, Pallas kernels for 9%

profile of v1, /device:TPU:1, one launch (start us, length us, event | category | flops | bytes accessed | tf_op | source)
XLA Modules:
  0.0 189.6 jit_solution(6911304236950850887)
XLA Ops:
  0.7 0.7 compare_select_fusion
  1.4 0.7 broadcast_compare_fusion
  2.1 0.1 broadcast_in_dim.39
  2.1 0.1 broadcast_in_dim.40
  2.2 1.6 gather_fusion
  3.9 0.8 broadcast_select_fusion
  4.7 9.4 %all-to-all-start = ((bf16[32,32,128]{2,1,0:T(8,128)(2,1)}), bf16[32,32,128]{2,1,0:T(8,128)(2,1)S(1)}, u32[]{:S(2)}, u32[]{:S(2)}) async-start(bf16[32,32,128]{2,1,0:T(8,128)(2,1)} %broadcast_select_fusion), calls=%async_computation | async-start | bytes 524288 | tf_op jit(solution)/shard_map/all_to_all | solution.py:379
  14.1 0.6 dynamic_slice.7
  16.7 0.1 bitcast_select_fusion.index_ref
  16.8 10.0 %gather_rows.1 = bf16[32,160,128]{2,1,0:T(8,128)(2,1)} custom-call(s32[32,128]{1,0:T(8,128)S(1)} %bitcast_select_fusion.index_ref, bf16[2048,128]{1,0:T(8,128)(2,1)S(1)} %copy-done.1), custom_call_target="tpu_custom_call" | custom-call | flops 4000000000 | bytes 2000000 | tf_op jit(solution)/shard_map/gather_rows/pallas_call | solution.py:77
  26.7 0.7 broadcast_dynamic-update-slice_fusion
  27.5 7.5 %all-to-all-start.1 = ((bf16[32,160,128]{2,1,0:T(8,128)(2,1)}), bf16[32,160,128]{2,1,0:T(8,128)(2,1)S(1)}, u32[]{:S(2)}, u32[]{:S(2)}) async-start(bf16[32,160,128]{2,1,0:T(8,128)(2,1)} %broadcast_dynamic-update-slice_fusion), calls=%async_computation.1 | async-start | bytes 2621440 | tf_op jit(solution)/shard_map/all_to_all | solution.py:379
  35.1 19.7 %all-to-all-done.1.recv_ref = bf16[32,160,128]{2,1,0:T(8,128)(2,1)S(1)} async-done(((bf16[32,160,128]{2,1,0:T(8,128)(2,1)}), bf16[32,160,128]{2,1,0:T(8,128)(2,1)S(1)}, u32[]{:S(2)}, u32[]{:S(2)}) %all-to-all-start.1) | async-done | bytes 1310752 | tf_op jit(solution)/shard_map/all_to_all | solution.py:379
  54.8 17.6 %forward_tiles.1 = (f32[4,128,128]{2,1,0:T(8,128)S(1)}, bf16[4,128,128]{2,1,0:T(8,128)(2,1)S(1)}, bf16[4,128,128]{2,1,0:T(8,128)(2,1)S(1)}, bf16[4,128,128]{2,1,0:T(8,128)(2,1)S(1)}) custom-call(s32[384]{0:T(512)S(1)} %reduce.dst_ref, s32[384]{0:T(512)S(1)} %reduce.1.src_ref, s32[1]{0:T(128)} %bitcast.rep_ref, bf16[16,128,128]{2,1,0:T(8,128)(2,1)S(1)} %bitcast.14, ...), custom_call_target="tpu_custom_call" | custom-call | flops 4000000000 | bytes 14000000 | tf_op jit(solution)/shard_map/forward_tiles/pallas_call | solution.py:123
  72.4 1.3 collective-permute-start
  73.7 2.6 %collective-permute-start.1 = (bf16[4,128,128]{2,1,0:T(8,128)(2,1)S(1)}, bf16[4,128,128]{2,1,0:T(8,128)(2,1)S(1)}, u32[]{:S(2)}, u32[]{:S(2)}) collective-permute-start(bf16[4,128,128]{2,1,0:T(8,128)(2,1)S(1)} %get-tuple-element.19), channel_id=1, source_target_pairs={{0,64},{32,96},{64,0},{96,32},{1,65},{33,97},{65,1},{97,33},{2,66}... | collective-permute-start | bytes 393224 | tf_op jit(solution)/shard_map/ppermute | solution.py:371
  76.4 1.1 collective-permute-start.2
  77.4 1.0 collective-permute-done.refs_1_
  78.5 3.9 %collective-permute-done.1.refs_2_ = bf16[4,128,128]{2,1,0:T(8,128)(2,1)S(1)} collective-permute-done((bf16[4,128,128]{2,1,0:T(8,128)(2,1)S(1)}, bf16[4,128,128]{2,1,0:T(8,128)(2,1)S(1)}, u32[]{:S(2)}, u32[]{:S(2)}) %collective-permute-start.1) | collective-permute-done | bytes 131104 | tf_op jit(solution)/shard_map/ppermute | solution.py:371
  82.4 1.0 middle.1
  83.4 1.0 collective-permute-start.6
  84.4 2.2 %collective-permute-start.7 = (bf16[4,128,128]{2,1,0:T(8,128)(2,1)S(1)}, bf16[4,128,128]{2,1,0:T(8,128)(2,1)S(1)}, u32[]{:S(2)}, u32[]{:S(2)}) collective-permute-start(bf16[4,128,128]{2,1,0:T(8,128)(2,1)S(1)} %get-tuple-element.22.y0), channel_id=1, source_target_pairs={{0,64},{32,96},{64,0},{96,32},{1,65},{33,97},{65,1},{97,33},{2,66}... | collective-permute-start | bytes 393224 | tf_op jit(solution)/shard_map/ppermute | solution.py:371
  86.6 0.9 collective-permute-start.8
  87.5 0.9 collective-permute-done.6.y1
  88.5 3.1 %collective-permute-done.7.y2 = bf16[4,128,128]{2,1,0:T(8,128)(2,1)S(1)} collective-permute-done((bf16[4,128,128]{2,1,0:T(8,128)(2,1)S(1)}, bf16[4,128,128]{2,1,0:T(8,128)(2,1)S(1)}, u32[]{:S(2)}, u32[]{:S(2)}) %collective-permute-start.7) | collective-permute-done | bytes 131104 | tf_op jit(solution)/shard_map/ppermute | solution.py:371
  91.6 18.9 %backward_tiles.1 = (bf16[4,32,48,128]{3,2,1,0:T(8,128)(2,1)}, f32[16,32,128]{2,1,0:T(8,128)S(1)}, bf16[16,32,128]{2,1,0:T(8,128)(2,1)S(1)}, bf16[16,32,128]{2,1,0:T(8,128)(2,1)S(1)}, bf16[16,32,128]{2,1,0:T(8,128)(2,1)S(1)}) custom-call(s32[384]{0:T(512)S(1)} %reduce.dst_ref, s32[384]{0:T(512)S(1)} %reduce.1.src_ref, s32[1]{0:T(128)} %bitcast.rep_ref, ...), custom_call_target="tpu_custom_call" | custom-call | flops 4000000000 | bytes 14000000 | tf_op jit(solution)/shard_map/backward_tiles/pallas_call | solution.py:237
  110.5 7.5 %all-to-all-start.2 = ((bf16[128,48,128]{2,1,0:T(8,128)(2,1)}), bf16[128,48,128]{2,1,0:T(8,128)(2,1)S(1)}, u32[]{:S(2)}, u32[]{:S(2)}) async-start(bf16[128,48,128]{2,1,0:T(8,128)(2,1)} %bitcast.10), calls=%async_computation.2 | async-start | bytes 3145728 | tf_op jit(solution)/shard_map/all_to_all | solution.py:379
  117.9 1.5 collective-permute-start.3
  119.4 2.4 %collective-permute-start.10 = (bf16[16,32,128]{2,1,0:T(8,128)(2,1)S(1)}, bf16[16,32,128]{2,1,0:T(8,128)(2,1)S(1)}, u32[]{:S(2)}, u32[]{:S(2)}) collective-permute-start(bf16[16,32,128]{2,1,0:T(8,128)(2,1)S(1)} %get-tuple-element.27), channel_id=1, source_target_pairs={{0,64},{32,96},{64,0},{96,32},{1,65},{33,97},{65,1},{97,33},{2,66}... | collective-permute-start | bytes 393224 | tf_op jit(solution)/shard_map/ppermute | solution.py:371
  121.9 1.1 collective-permute-start.11
  123.0 0.3 collective-permute-start.9
  123.3 19.3 %all-to-all-done.2.recv_ref = bf16[128,48,128]{2,1,0:T(8,128)(2,1)S(1)} async-done(((bf16[128,48,128]{2,1,0:T(8,128)(2,1)}), bf16[128,48,128]{2,1,0:T(8,128)(2,1)S(1)}, u32[]{:S(2)}, u32[]{:S(2)}) %all-to-all-start.2) | async-done | bytes 1572896 | tf_op jit(solution)/shard_map/all_to_all | solution.py:379
  142.7 0.1 convert_reduce_fusion
  142.8 0.7 broadcast_in_dim.46
  143.5 4.8 %all-to-all-start.3 = ((f32[32,16,128]{2,1,0:T(8,128)}), f32[32,16,128]{2,1,0:T(8,128)S(1)}, u32[]{:S(2)}, u32[]{:S(2)}) async-start(f32[32,16,128]{2,1,0:T(8,128)} %broadcast_in_dim.46), calls=%async_computation.3 | async-start | bytes 524288 | tf_op jit(solution)/shard_map/all_to_all | solution.py:379
  148.3 0.6 collective-permute-done.9.a_ref
  148.9 5.3 %scatter_rows.1.part_ref = f32[16,32,128]{2,1,0:T(8,128)S(1)} custom-call(s32[32,128]{1,0:T(8,128)S(1)} %bitcast_select_fusion.index_ref, bf16[128,48,128]{2,1,0:T(8,128)(2,1)S(1)} %all-to-all-done.2.recv_ref, f32[16,32,128]{2,1,0:T(8,128)S(1)} %get-tuple-element.25.own_ref, bf16[16,32,128]{2,1,0:T(8,128)(2,1)S(1)} %collective-permute-done.9.a_ref, ...), custom_call_target="tpu_custom_call" | custom-call | flops 4000000000 | bytes 4000000 | tf_op jit(solution)/shard_map/scatter_rows/pallas_call | solution.py:286
  154.2 3.2 %all-to-all-done.3.shared_ref = f32[32,16,128]{2,1,0:T(8,128)S(1)} async-done(((f32[32,16,128]{2,1,0:T(8,128)}), f32[32,16,128]{2,1,0:T(8,128)S(1)}, u32[]{:S(2)}, u32[]{:S(2)}) %all-to-all-start.3) | async-done | bytes 262176 | tf_op jit(solution)/shard_map/all_to_all | solution.py:379
  157.4 0.6 add_hubs.1.m0
  158.0 0.4 collective-permute-start.12
  158.4 1.7 collective-permute-start.13
  160.1 0.8 collective-permute-start.14
  160.9 2.2 %collective-permute-start.4 = (bf16[512,256]{1,0:T(8,128)(2,1)S(1)}, bf16[512,256]{1,0:T(8,128)(2,1)S(1)}, u32[]{:S(2)}, u32[]{:S(2)}) collective-permute-start(bf16[512,256]{1,0:T(8,128)(2,1)S(1)} %get-tuple-element.21.o0), channel_id=1, source_target_pairs={{0,64},{32,96},{64,0},{96,32},{1,65},{33,97},{65,1},{97,33},{2,66}... | collective-permute-start | bytes 786440 | tf_op jit(solution)/shard_map/ppermute | solution.py:371
  163.1 0.8 collective-permute-start.5
  164.0 16.5 %collective-permute-done.4.o2 = bf16[512,256]{1,0:T(8,128)(2,1)S(1)} collective-permute-done((bf16[512,256]{1,0:T(8,128)(2,1)S(1)}, bf16[512,256]{1,0:T(8,128)(2,1)S(1)}, u32[]{:S(2)}, u32[]{:S(2)}) %collective-permute-start.4) | collective-permute-done | bytes 262176 | tf_op jit(solution)/shard_map/ppermute | solution.py:371
  180.4 6.6 %collective-permute-done.5.o3 = bf16[512,256]{1,0:T(8,128)(2,1)S(1)} collective-permute-done((bf16[512,256]{1,0:T(8,128)(2,1)S(1)}, bf16[512,256]{1,0:T(8,128)(2,1)S(1)}, u32[]{:S(2)}, u32[]{:S(2)}) %collective-permute-start.5) | collective-permute-done | bytes 262176 | tf_op jit(solution)/shard_map/ppermute | solution.py:371
  187.0 1.0 place_output.1
  188.1 1.5 finish.1
  (31 shorter events, 0.1 us)
Async XLA Ops:
  0.6 16.1 %copy-start.1 = (bf16[2048,128]{1,0:T(8,128)(2,1)S(1)}, bf16[2048,128]{1,0:T(8,128)(2,1)}, u32[]{:S(2)}) copy-start(bf16[2048,128]{1,0:T(8,128)(2,1)} %feat_ref.1) | copy-start | bytes 1572868
  0.6 16.0 %copy-start.8 = (s32[1,32]{1,0:T(1,128)S(1)}, s32[1,32]{1,0:T(1,128)}, u32[]{:S(2)}) copy-start(s32[1,32]{1,0:T(1,128)} %param.15) | copy-start | bytes 388
  0.7 16.0 %copy-start.5 = (s32[1,32,128]{2,1,0:T(8,128)S(1)}, s32[1,32,128]{2,1,0:T(8,128)}, u32[]{:S(2)}) copy-start(s32[1,32,128]{2,1,0:T(8,128)} %param.14) | copy-start | bytes 49156
  4.7 22.1 %all-to-all-start = ((bf16[32,32,128]{2,1,0:T(8,128)(2,1)}), bf16[32,32,128]{2,1,0:T(8,128)(2,1)S(1)}, u32[]{:S(2)}, u32[]{:S(2)}) async-start(bf16[32,32,128]{2,1,0:T(8,128)(2,1)} %broadcast_select_fusion), calls=%async_computation | async-start | bytes 524288 | tf_op jit(solution)/shard_map/all_to_all | solution.py:379
  27.5 7.5 %copy-start.6 = (s32[1,1,384]{2,1,0:T(1,128)S(1)}, s32[1,1,384]{2,1,0:T(1,128)}, u32[]{:S(2)}) copy-start(s32[1,1,384]{2,1,0:T(1,128)} %param.17) | copy-start | bytes 4612
  27.5 7.6 %copy-start.7 = (s32[1,1,384]{2,1,0:T(1,128)S(1)}, s32[1,1,384]{2,1,0:T(1,128)}, u32[]{:S(2)}) copy-start(s32[1,1,384]{2,1,0:T(1,128)} %param.18) | copy-start | bytes 4612
  27.5 27.3 %all-to-all-start.1 = ((bf16[32,160,128]{2,1,0:T(8,128)(2,1)}), bf16[32,160,128]{2,1,0:T(8,128)(2,1)S(1)}, u32[]{:S(2)}, u32[]{:S(2)}) async-start(bf16[32,160,128]{2,1,0:T(8,128)(2,1)} %broadcast_dynamic-update-slice_fusion), calls=%async_computation.1 | async-start | bytes 2621440 | tf_op jit(solution)/shard_map/all_to_all | solution.py:379
  54.8 27.6 %copy-start = (bf16[2048,256]{1,0:T(8,128)(2,1)S(1)}, bf16[2048,256]{1,0:T(8,128)(2,1)}, u32[]{:S(2)}) copy-start(bf16[2048,256]{1,0:T(8,128)(2,1)} %refs_6_.1) | copy-start | bytes 3145732
  54.8 27.6 %copy-start.2 = (bf16[128,256]{1,0:T(8,128)(2,1)S(1)}, bf16[128,256]{1,0:T(8,128)(2,1)}, u32[]{:S(2)}) copy-start(bf16[128,256]{1,0:T(8,128)(2,1)} %refs_4_.1) | copy-start | bytes 196612
  54.8 27.6 %copy-start.4 = (f32[256]{0:T(256)S(1)}, f32[256]{0:T(256)}, u32[]{:S(2)}) copy-start(f32[256]{0:T(256)} %param.12) | copy-start | bytes 3076
  72.4 6.1 %collective-permute-start = (bf16[4,128,128]{2,1,0:T(8,128)(2,1)S(1)}, bf16[4,128,128]{2,1,0:T(8,128)(2,1)S(1)}, u32[]{:S(2)}, u32[]{:S(2)}) collective-permute-start(bf16[4,128,128]{2,1,0:T(8,128)(2,1)S(1)} %get-tuple-element.18), channel_id=1, source_target_pairs={{0,32},{32,64},{64,96},{96,0},{1,33},{33,65},{65,97},{97,1},{2,34}... | collective-permute-start | bytes 393224 | tf_op jit(solution)/shard_map/ppermute | solution.py:371
  73.7 8.7 %collective-permute-start.1 = (bf16[4,128,128]{2,1,0:T(8,128)(2,1)S(1)}, bf16[4,128,128]{2,1,0:T(8,128)(2,1)S(1)}, u32[]{:S(2)}, u32[]{:S(2)}) collective-permute-start(bf16[4,128,128]{2,1,0:T(8,128)(2,1)S(1)} %get-tuple-element.19), channel_id=1, source_target_pairs={{0,64},{32,96},{64,0},{96,32},{1,65},{33,97},{65,1},{97,33},{2,66}... | collective-permute-start | bytes 393224 | tf_op jit(solution)/shard_map/ppermute | solution.py:371
  76.4 6.1 %collective-permute-start.2 = (bf16[4,128,128]{2,1,0:T(8,128)(2,1)S(1)}, bf16[4,128,128]{2,1,0:T(8,128)(2,1)S(1)}, u32[]{:S(2)}, u32[]{:S(2)}) collective-permute-start(bf16[4,128,128]{2,1,0:T(8,128)(2,1)S(1)} %get-tuple-element.20), channel_id=1, source_target_pairs={{0,96},{32,0},{64,32},{96,64},{1,97},{33,1},{65,33},{97,65},{2,98}... | collective-permute-start | bytes 393224 | tf_op jit(solution)/shard_map/ppermute | solution.py:371
  83.4 5.1 %collective-permute-start.6 = (bf16[4,128,128]{2,1,0:T(8,128)(2,1)S(1)}, bf16[4,128,128]{2,1,0:T(8,128)(2,1)S(1)}, u32[]{:S(2)}, u32[]{:S(2)}) collective-permute-start(bf16[4,128,128]{2,1,0:T(8,128)(2,1)S(1)} %get-tuple-element.22.y0), channel_id=1, source_target_pairs={{0,32},{32,64},{64,96},{96,0},{1,33},{33,65},{65,97},{97,1},{2,34}... | collective-permute-start | bytes 393224 | tf_op jit(solution)/shard_map/ppermute | solution.py:371
  84.4 7.2 %collective-permute-start.7 = (bf16[4,128,128]{2,1,0:T(8,128)(2,1)S(1)}, bf16[4,128,128]{2,1,0:T(8,128)(2,1)S(1)}, u32[]{:S(2)}, u32[]{:S(2)}) collective-permute-start(bf16[4,128,128]{2,1,0:T(8,128)(2,1)S(1)} %get-tuple-element.22.y0), channel_id=1, source_target_pairs={{0,64},{32,96},{64,0},{96,32},{1,65},{33,97},{65,1},{97,33},{2,66}... | collective-permute-start | bytes 393224 | tf_op jit(solution)/shard_map/ppermute | solution.py:371
  86.6 4.9 %collective-permute-start.8 = (bf16[4,128,128]{2,1,0:T(8,128)(2,1)S(1)}, bf16[4,128,128]{2,1,0:T(8,128)(2,1)S(1)}, u32[]{:S(2)}, u32[]{:S(2)}) collective-permute-start(bf16[4,128,128]{2,1,0:T(8,128)(2,1)S(1)} %get-tuple-element.22.y0), channel_id=1, source_target_pairs={{0,96},{32,0},{64,32},{96,64},{1,97},{33,1},{65,33},{97,65},{2,98}... | collective-permute-start | bytes 393224 | tf_op jit(solution)/shard_map/ppermute | solution.py:371
  110.5 32.2 %all-to-all-start.2 = ((bf16[128,48,128]{2,1,0:T(8,128)(2,1)}), bf16[128,48,128]{2,1,0:T(8,128)(2,1)S(1)}, u32[]{:S(2)}, u32[]{:S(2)}) async-start(bf16[128,48,128]{2,1,0:T(8,128)(2,1)} %bitcast.10), calls=%async_computation.2 | async-start | bytes 3145728 | tf_op jit(solution)/shard_map/all_to_all | solution.py:379
  117.9 45.2 %collective-permute-start.3 = (bf16[512,256]{1,0:T(8,128)(2,1)S(1)}, bf16[512,256]{1,0:T(8,128)(2,1)S(1)}, u32[]{:S(2)}, u32[]{:S(2)}) collective-permute-start(bf16[512,256]{1,0:T(8,128)(2,1)S(1)} %get-tuple-element.21.o0), channel_id=1, source_target_pairs={{0,32},{32,64},{64,96},{96,0},{1,33},{33,65},{65,97},{97,1},{2,34}... | collective-permute-start | bytes 786440 | tf_op jit(solution)/shard_map/ppermute | solution.py:371
  119.4 28.9 %collective-permute-start.10 = (bf16[16,32,128]{2,1,0:T(8,128)(2,1)S(1)}, bf16[16,32,128]{2,1,0:T(8,128)(2,1)S(1)}, u32[]{:S(2)}, u32[]{:S(2)}) collective-permute-start(bf16[16,32,128]{2,1,0:T(8,128)(2,1)S(1)} %get-tuple-element.27), channel_id=1, source_target_pairs={{0,64},{32,96},{64,0},{96,32},{1,65},{33,97},{65,1},{97,33},{2,66}... | collective-permute-start | bytes 393224 | tf_op jit(solution)/shard_map/ppermute | solution.py:371
  121.9 26.4 %collective-permute-start.11 = (bf16[16,32,128]{2,1,0:T(8,128)(2,1)S(1)}, bf16[16,32,128]{2,1,0:T(8,128)(2,1)S(1)}, u32[]{:S(2)}, u32[]{:S(2)}) collective-permute-start(bf16[16,32,128]{2,1,0:T(8,128)(2,1)S(1)} %get-tuple-element.28), channel_id=1, source_target_pairs={{0,96},{32,0},{64,32},{96,64},{1,97},{33,1},{65,33},{97,65},{2,98}... | collective-permute-start | bytes 393224 | tf_op jit(solution)/shard_map/ppermute | solution.py:371
  123.0 25.9 %collective-permute-start.9 = (bf16[16,32,128]{2,1,0:T(8,128)(2,1)S(1)}, bf16[16,32,128]{2,1,0:T(8,128)(2,1)S(1)}, u32[]{:S(2)}, u32[]{:S(2)}) collective-permute-start(bf16[16,32,128]{2,1,0:T(8,128)(2,1)S(1)} %get-tuple-element.26), channel_id=1, source_target_pairs={{0,32},{32,64},{64,96},{96,0},{1,33},{33,65},{65,97},{97,1},{2,34}... | collective-permute-start | bytes 393224 | tf_op jit(solution)/shard_map/ppermute | solution.py:371
  143.5 13.9 %all-to-all-start.3 = ((f32[32,16,128]{2,1,0:T(8,128)}), f32[32,16,128]{2,1,0:T(8,128)S(1)}, u32[]{:S(2)}, u32[]{:S(2)}) async-start(f32[32,16,128]{2,1,0:T(8,128)} %broadcast_in_dim.46), calls=%async_computation.3 | async-start | bytes 524288 | tf_op jit(solution)/shard_map/all_to_all | solution.py:379
  148.9 8.4 %copy-start.3 = (s32[8]{0:T(128)S(1)}, s32[8]{0:T(128)}, u32[]{:S(2)}) copy-start(s32[8]{0:T(128)} %hub_ref.1) | copy-start | bytes 100
  158.0 30.1 %collective-permute-start.12 = (f32[640,128]{1,0:T(8,128)S(1)}, f32[640,128]{1,0:T(8,128)S(1)}, u32[]{:S(2)}, u32[]{:S(2)}) collective-permute-start(f32[640,128]{1,0:T(8,128)S(1)} %add_hubs.1.m0), channel_id=1, source_target_pairs={{0,32},{32,64},{64,96},{96,0},{1,33},{33,65},{65,97},{97,1},{2,34}... | collective-permute-start | bytes 983048 | tf_op jit(solution)/shard_map/ppermute | solution.py:371
  158.4 29.6 %collective-permute-start.13 = (f32[640,128]{1,0:T(8,128)S(1)}, f32[640,128]{1,0:T(8,128)S(1)}, u32[]{:S(2)}, u32[]{:S(2)}) collective-permute-start(f32[640,128]{1,0:T(8,128)S(1)} %add_hubs.1.m0), channel_id=1, source_target_pairs={{0,64},{32,96},{64,0},{96,32},{1,65},{33,97},{65,1},{97,33},{2,66}... | collective-permute-start | bytes 983048 | tf_op jit(solution)/shard_map/ppermute | solution.py:371
  160.1 28.0 %collective-permute-start.14 = (f32[640,128]{1,0:T(8,128)S(1)}, f32[640,128]{1,0:T(8,128)S(1)}, u32[]{:S(2)}, u32[]{:S(2)}) collective-permute-start(f32[640,128]{1,0:T(8,128)S(1)} %add_hubs.1.m0), channel_id=1, source_target_pairs={{0,96},{32,0},{64,32},{96,64},{1,97},{33,1},{65,33},{97,65},{2,98}... | collective-permute-start | bytes 983048 | tf_op jit(solution)/shard_map/ppermute | solution.py:371
  160.9 19.5 %collective-permute-start.4 = (bf16[512,256]{1,0:T(8,128)(2,1)S(1)}, bf16[512,256]{1,0:T(8,128)(2,1)S(1)}, u32[]{:S(2)}, u32[]{:S(2)}) collective-permute-start(bf16[512,256]{1,0:T(8,128)(2,1)S(1)} %get-tuple-element.21.o0), channel_id=1, source_target_pairs={{0,64},{32,96},{64,0},{96,32},{1,65},{33,97},{65,1},{97,33},{2,66}... | collective-permute-start | bytes 786440 | tf_op jit(solution)/shard_map/ppermute | solution.py:371
  163.1 23.9 %collective-permute-start.5 = (bf16[512,256]{1,0:T(8,128)(2,1)S(1)}, bf16[512,256]{1,0:T(8,128)(2,1)S(1)}, u32[]{:S(2)}, u32[]{:S(2)}) collective-permute-start(bf16[512,256]{1,0:T(8,128)(2,1)S(1)} %get-tuple-element.21.o0), channel_id=1, source_target_pairs={{0,96},{32,0},{64,32},{96,64},{1,97},{33,1},{65,33},{97,65},{2,98}... | collective-permute-start | bytes 786440 | tf_op jit(solution)/shard_map/ppermute | solution.py:371

commit v2 on v1

v2 whole, which is shorter than its diff:
```python
import functools
import math

import jax
import jax.numpy as jnp
from jax import lax
from jax.experimental import pallas as pl
from jax.experimental.pallas import tpu as pltpu
from jax.sharding import PartitionSpec as P

F32 = jnp.float32
BF16 = jnp.bfloat16
BLK = 128
N_REP = 4
N_DOM = 32
FIN = 128
HID = 256
ROWS = 2048
LOCAL = ROWS // BLK
HUBS = 8
BLOCKS = LOCAL + N_DOM + HUBS
TILES = 384
REMOTE = N_DOM
PAIRED_HUBS = HUBS // N_REP
CHUNK = 32
FWD_SLOTS = 512
BWD_SLOTS = 512
QUARTER = ROWS // N_REP
QB = LOCAL // N_REP
FQ = FIN // N_REP
GW_ROWS = FQ * HID // BLK
FOLD = HUBS * FQ
LO = 256
VMEM_LIMIT = 24 * 1024 * 1024

VM = pl.BlockSpec(memory_space=pltpu.VMEM)
SM = pl.BlockSpec(memory_space=pltpu.SMEM)
PARAMS = pltpu.CompilerParams(vmem_limit_bytes=VMEM_LIMIT)
TILE_PARAMS = pltpu.CompilerParams(vmem_limit_bytes=VMEM_LIMIT)


def dot(a, b):
    return jnp.dot(a, b, preferred_element_type=F32)


def halves(x):
    high = x.astype(BF16)
    return high, (x - high.astype(F32)).astype(BF16)


def column(row):
    return jnp.broadcast_to(row, (BLK, BLK)).T


def low_onehot(col):
    low = jnp.where(col < 0, -1, col & (LO - 1))
    lane = lax.broadcasted_iota(jnp.int32, (BLK, BLK), 1)
    return jnp.concatenate(
        [jnp.where(low == lane + k * BLK, 1.0, 0.0) for k in range(LO // BLK)], axis=1
    ).astype(BF16)


def sort_tiles(bucket, operand, empty, edges, out_of, slots):
    sub = lax.broadcasted_iota(jnp.int32, (BLK, BLK), 0)
    lane = lax.broadcasted_iota(jnp.int32, (BLK, BLK), 1)
    line = lane[:1]
    parts = len(bucket)
    cols = [column(b) for b in bucket]
    hots = [jnp.where(c == lane, 1.0, 0.0) for c in cols]
    counts = sum(jnp.sum(h, axis=0, keepdims=True) for h in hots).astype(jnp.int32)
    padded = (counts + 1) & -2
    before = jnp.where(sub < lane, column(padded).astype(F32), 0.0)
    starts = jnp.sum(before, axis=0, keepdims=True).astype(jnp.int32)
    first = jnp.zeros((1, BLK), jnp.int32)
    low = 0
    for n, high in enumerate(edges):
        inside = (line >= low) & (line < high)
        size = jnp.sum(jnp.where(inside, padded, 0).astype(F32), axis=1, keepdims=True).astype(jnp.int32)
        gap = ((size + CHUNK - 1) & -CHUNK) - size
        starts = starts + jnp.where(line >= high, gap, 0)
        total = (size + CHUNK - 1) // CHUNK
        first = first + jnp.where(line > n, total, 0)
        low = high
    begin, end = column(starts), column(starts + padded)
    places = []
    for i in range(parts):
        rank = jnp.sum(jnp.where(hots[i] > 0.0, starts.astype(F32), 0.0), axis=1, keepdims=True)
        for j in range(i + 1):
            same = jnp.broadcast_to(bucket[j], (BLK, BLK)) == cols[i]
            if j == i:
                same = same & (lane < sub)
            rank = rank + jnp.sum(jnp.where(same, 1.0, 0.0), axis=1, keepdims=True)
        places.append(jnp.broadcast_to(rank.astype(jnp.int32), (BLK, BLK)))
    shifted = [column(o - empty).astype(F32) for o in operand]
    tiles, blocks, outs = [], [], []
    for s in range(slots // BLK):
        here = lane + s * BLK
        tile = jnp.zeros((1, BLK), F32)
        block = jnp.zeros((1, BLK), F32)
        for i in range(parts):
            hit = places[i] == here
            tile = tile + jnp.sum(jnp.where(hit, (sub + i * BLK).astype(F32), 0.0), axis=0, keepdims=True)
            block = block + jnp.sum(jnp.where(hit, shifted[i], 0.0), axis=0, keepdims=True)
        inside = (begin <= here) & (here < end)
        out = jnp.sum(jnp.where(inside, out_of(sub).astype(F32), 0.0), axis=0, keepdims=True)
        tiles.append(tile.astype(jnp.int32))
        blocks.append(block.astype(jnp.int32) + empty)
        outs.append(out.astype(jnp.int32))
    return tiles, blocks, outs, first


def order_kernel(dst_ref, src_ref, fwd_ref, bwd_ref):
    parts = TILES // BLK
    dst = [dst_ref[pl.ds(i, 1), :] for i in range(parts)]
    src = [src_ref[pl.ds(i, 1), :] for i in range(parts)]
    bucket = [jnp.where(s < LOCAL, d, d + LOCAL) for d, s in zip(dst, src)]
    operand = [jnp.where(s < LOCAL, s, s - LOCAL) for s in src]
    empty = REMOTE + HUBS
    found = sort_tiles(bucket, operand, empty, (LOCAL, 2 * LOCAL), lambda b: b & (LOCAL - 1), FWD_SLOTS)
    for n, rows in enumerate(found[:3]):
        for s, row in enumerate(rows):
            fwd_ref[n, pl.ds(s, 1), :] = row
    fwd_ref[3, pl.ds(0, 1), :] = found[3]
    far = REMOTE + HUBS
    bucket = [jnp.where(s < LOCAL, s + far, s - LOCAL) for s in src]
    found = sort_tiles(
        bucket, dst, LOCAL, (far, far + LOCAL), lambda b: jnp.where(b < far, b, b - far), BWD_SLOTS
    )
    for n, rows in enumerate(found[:3]):
        for s, row in enumerate(rows):
            bwd_ref[n, pl.ds(s, 1), :] = row
    bwd_ref[3, pl.ds(0, 1), :] = found[3]


def order_tiles(dst, src):
    return pl.pallas_call(
        order_kernel,
        out_shape=[
            jax.ShapeDtypeStruct((4, FWD_SLOTS // BLK, BLK), jnp.int32),
            jax.ShapeDtypeStruct((4, BWD_SLOTS // BLK, BLK), jnp.int32),
        ],
        in_specs=[VM, VM],
        out_specs=[VM, VM],
        compiler_params=PARAMS,
        name="order_tiles",
    )(dst, src)


def run_class(plan_ref, number, product, acc):
    def chunk(i, carry):
        row, col = i // (BLK // CHUNK), lax.rem(i, BLK // CHUNK) * CHUNK
        found = []
        for k in range(0, CHUNK, 2):
            one = (plan_ref[0, row, col + k], plan_ref[1, row, col + k])
            two = (plan_ref[0, row, col + k + 1], plan_ref[1, row, col + k + 1])
            found.append((plan_ref[2, row, col + k], product(one, two)))
        for d, value in found:
            acc[d] += value
        return carry

    lax.fori_loop(plan_ref[3, 0, number], plan_ref[3, 0, number + 1], chunk, 0)


PEERS = 4


def gather_kernel(rows_ref, count_ref, feat_ref, out_ref):
    slot = lax.broadcasted_iota(jnp.int32, (1, BLK), 1)

    def step(i, carry):
        cols = []
        for j in range(PEERS):
            p = PEERS * i + j
            row = jnp.where(slot < count_ref[0, p], rows_ref[pl.ds(p, 1), :], -1)
            cols.append(column(row))
        hot = jnp.concatenate([low_onehot(c) for c in cols], axis=0)
        high = lax.shift_right_arithmetic(jnp.concatenate(cols, axis=0), 8)
        total = jnp.zeros((PEERS * BLK, FIN), F32)
        for pair in range(ROWS // LO // 2):
            left = feat_ref[pl.ds(2 * pair * LO, LO), :]
            right = feat_ref[pl.ds((2 * pair + 1) * LO, LO), :]
            got = dot(hot, jnp.concatenate([left, right], axis=1))
            total = jnp.where(high == 2 * pair, got[:, :FIN], total)
            total = jnp.where(high == 2 * pair + 1, got[:, FIN:], total)
        out_ref[pl.ds(PEERS * i, PEERS)] = total.astype(BF16).reshape(PEERS, BLK, FIN)
        return carry

    lax.fori_loop(0, N_DOM // PEERS, step, 0)


def gather_rows(rows, counts, features):
    return pl.pallas_call(
        gather_kernel,
        out_shape=jax.ShapeDtypeStruct((N_DOM, BLK, FIN), BF16),
        in_specs=[VM, SM, VM],
        out_specs=VM,
        compiler_params=PARAMS,
        cost_estimate=pl.CostEstimate(flops=4 * 10**9, bytes_accessed=2 * 10**6, transcendentals=0),
        name="gather_rows",
    )(rows, counts, features)


def hub_pick_kernel(hub_ref, place_ref, feat_ref, out_ref):
    for k in range(PAIRED_HUBS):
        block = hub_ref[place_ref[0] * PAIRED_HUBS + k]
        mine = lax.shift_right_logical(block, 4) == place_ref[1]

        @pl.when(mine)
        def _():
            out_ref[k] = feat_ref[block & (LOCAL - 1)]

        @pl.when(jnp.logical_not(mine))
        def _():
            out_ref[k] = jnp.zeros((BLK, FIN), BF16)


def pick_hubs(hubs, place, features):
    return pl.pallas_call(
        hub_pick_kernel,
        out_shape=jax.ShapeDtypeStruct((PAIRED_HUBS, BLK, FIN), BF16),
        in_specs=[SM, SM, VM],
        out_specs=VM,
        compiler_params=PARAMS,
        name="pick_hubs",
    )(hubs, place, features)


def forward_product(w_ref, xs):
    def product(one, two):
        left = jnp.concatenate([w_ref[one[0]], w_ref[two[0]]], axis=1)
        return dot(left, jnp.concatenate([xs[one[1]], xs[two[1]]], axis=0))

    return product


def forward_near_kernel(plan_ref, feat_ref, w_ref, acc_ref, xs):
    xs[pl.ds(0, LOCAL)] = feat_ref[...]
    xs[REMOTE + HUBS] = jnp.zeros((BLK, FIN), BF16)
    acc_ref[...] = jnp.zeros_like(acc_ref)
    run_class(plan_ref, 0, forward_product(w_ref, xs), acc_ref)


def forward_near(plan, features, weights):
    return pl.pallas_call(
        forward_near_kernel,
        out_shape=jax.ShapeDtypeStruct((LOCAL, BLK, FIN), F32),
        in_specs=[SM, VM, VM],
        out_specs=VM,
        scratch_shapes=[pltpu.VMEM((REMOTE + HUBS + 1, BLK, FIN), BF16)],
        compiler_params=TILE_PARAMS,
        cost_estimate=pl.CostEstimate(flops=10**9, bytes_accessed=14 * 10**6, transcendentals=0),
        name="forward_near",
    )(plan, features, weights)


def forward_far_kernel(
    plan_ref, rep_ref, near_ref, recv_ref, h0, h1, h2, h3, w_ref, own_ref, s1_ref, s2_ref, s3_ref, xs, acc
):
    rep = rep_ref[0]
    xs[pl.ds(0, REMOTE)] = recv_ref[...]
    for k, ref in enumerate((h0, h1, h2, h3)):
        first = lax.rem(rep + N_REP - k, N_REP) * PAIRED_HUBS
        xs[pl.ds(REMOTE + first, PAIRED_HUBS)] = ref[...]
    xs[REMOTE + HUBS] = jnp.zeros((BLK, FIN), BF16)
    acc[...] = near_ref[...]
    run_class(plan_ref, 1, forward_product(w_ref, xs), acc)
    own_ref[...] = acc[pl.ds(rep * QB, QB)]
    for k, ref in ((1, s1_ref), (2, s2_ref), (3, s3_ref)):
        ref[...] = acc[pl.ds(lax.rem(rep + k, N_REP) * QB, QB)].astype(BF16)


def forward_far(plan, rep, near, received, hubs, weights):
    quarter = (QB, BLK, FIN)
    return pl.pallas_call(
        forward_far_kernel,
        out_shape=[jax.ShapeDtypeStruct(quarter, F32)] + [jax.ShapeDtypeStruct(quarter, BF16)] * 3,
        in_specs=[SM, SM] + [VM] * 7,
        out_specs=[VM] * 4,
        scratch_shapes=[
            pltpu.VMEM((REMOTE + HUBS + 1, BLK, FIN), BF16),
            pltpu.VMEM((LOCAL, BLK, FIN), F32),
        ],
        compiler_params=TILE_PARAMS,
        cost_estimate=pl.CostEstimate(flops=4 * 10**9, bytes_accessed=14 * 10**6, transcendentals=0),
        name="forward_far",
    )(plan, rep, near, received, *hubs, weights)


def middle_kernel(
    rep_ref, own_ref, a_ref, b_ref, c_ref, w_ref, bias_ref, cot_ref, out_ref, y_ref, g0, g1, g2, g3, gw
):
    zx = (own_ref[...] + a_ref[...].astype(F32)) + (b_ref[...].astype(F32) + c_ref[...].astype(F32))
    zx = zx.reshape(QUARTER, FIN)
    weight = w_ref[...]
    zh, zl = halves(zx)
    pre = dot(zh, weight) + dot(zl, weight) + bias_ref[...]
    root = math.sqrt(2.0 / math.pi)
    square = pre * pre
    bent = jnp.tanh(root * (pre + 0.044715 * (square * pre)))
    cdf = 0.5 * (1.0 + bent)
    out_ref[...] = (pre * cdf).astype(BF16)
    slope = cdf + (0.5 * pre) * ((1.0 - bent * bent) * (root * (1.0 + (3 * 0.044715) * square)))
    pre_grad = (cot_ref[...].astype(F32) * slope).astype(BF16)
    yt = lax.dot_general(weight, pre_grad, (((1,), (1,)), ((), ())), preferred_element_type=F32)
    yt = yt.astype(BF16)
    for k in range(QB):
        y_ref[k] = yt[:, k * BLK : (k + 1) * BLK]
    th, tl = halves(zx.T)
    gw[...] = dot(th, pre_grad) + dot(tl, pre_grad)
    for k, ref in enumerate((g0, g1, g2, g3)):
        start = pl.multiple_of(lax.rem(rep_ref[0] + k, N_REP) * FQ, FQ)
        rows = gw[pl.ds(start, FQ), :]
        high, low = halves(jnp.concatenate([rows[:, :BLK], rows[:, BLK:]], axis=0))
        ref[pl.ds(0, GW_ROWS), :] = high
        ref[pl.ds(GW_ROWS, GW_ROWS), :] = low


def middle(rep, own, a, b, c, weight, bias, cotangent):
    whole = lambda shape: pl.BlockSpec(shape, lambda i, rep_ref: (0,) * len(shape))
    quarter = (QB, BLK, FIN)
    gw_shape = (2 * GW_ROWS, BLK)
    return pl.pallas_call(
        middle_kernel,
        grid_spec=pltpu.PrefetchScalarGridSpec(
            num_scalar_prefetch=1,
            grid=(1,),
            in_specs=[whole(quarter)] * 4
            + [
                whole((FIN, HID)),
                whole((1, HID)),
                pl.BlockSpec((QUARTER, HID), lambda i, rep_ref: (rep_ref[0], 0)),
            ],
            out_specs=[whole((QUARTER, HID)), whole((QB, FIN, BLK))] + [whole(gw_shape)] * 4,
            scratch_shapes=[pltpu.VMEM((FIN, HID), F32)],
        ),
        out_shape=[
            jax.ShapeDtypeStruct((QUARTER, HID), BF16),
            jax.ShapeDtypeStruct((QB, FIN, BLK), BF16),
        ]
        + [jax.ShapeDtypeStruct(gw_shape, BF16)] * 4,
        compiler_params=PARAMS,
        name="middle",
    )(rep, own, a, b, c, weight, bias, cotangent)


def backward_product(w_ref, ys):
    def product(one, two):
        left = jnp.concatenate([ys[one[1]], ys[two[1]]], axis=1)
        return dot(left, jnp.concatenate([w_ref[one[0]], w_ref[two[0]]], axis=0))

    return product


def load_ys(rep, refs, ys):
    for k, ref in enumerate(refs):
        ys[pl.ds(lax.rem(rep + N_REP - k, N_REP) * QB, QB)] = ref[...]
    ys[LOCAL] = jnp.zeros((FIN, BLK), BF16)


def backward_far_kernel(
    plan_ref, rep_ref, y0, y1, y2, y3, g0, g1, g2, g3, w_ref, msg_ref, f0, f1, f2, f3, ys, acc
):
    rep = rep_ref[0]
    load_ys(rep, (y0, y1, y2, y3), ys)
    acc[...] = jnp.zeros_like(acc)
    run_class(plan_ref, 0, backward_product(w_ref, ys), acc)
    for q in range(N_REP):
        msg_ref[q] = acc[pl.ds(0, REMOTE), pl.ds(q * FQ, FQ), :].astype(BF16)
    for k, (ref, gw) in enumerate(((f0, g0), (f1, g1), (f2, g2), (f3, g3))):
        start = pl.multiple_of(lax.rem(rep + k, N_REP) * FQ, FQ)
        rows = acc[pl.ds(REMOTE, HUBS), pl.ds(start, FQ), :].reshape(FOLD, BLK)
        ref[pl.ds(0, FOLD), :] = rows.astype(BF16)
        ref[pl.ds(FOLD, 2 * GW_ROWS), :] = gw[...]


def backward_far(plan, rep, ys, gws, weights):
    fold = (FOLD + 2 * GW_ROWS, BLK)
    return pl.pallas_call(
        backward_far_kernel,
        out_shape=[jax.ShapeDtypeStruct((N_REP, N_DOM, FQ, BLK), BF16)]
        + [jax.ShapeDtypeStruct(fold, BF16)] * 4,
        in_specs=[SM, SM] + [VM] * 9,
        out_specs=[VM] * 5,
        scratch_shapes=[
            pltpu.VMEM((LOCAL + 1, FIN, BLK), BF16),
            pltpu.VMEM((REMOTE + HUBS, FIN, BLK), F32),
        ],
        compiler_params=TILE_PARAMS,
        cost_estimate=pl.CostEstimate(flops=4 * 10**9, bytes_accessed=14 * 10**6, transcendentals=0),
        name="backward_far",
    )(plan, rep, *ys, *gws, weights)


def backward_near_kernel(plan_ref, rep_ref, y0, y1, y2, y3, w_ref, own_ref, s1, s2, s3, ys, acc):
    rep = rep_ref[0]
    load_ys(rep, (y0, y1, y2, y3), ys)
    acc[...] = jnp.zeros_like(acc)
    run_class(plan_ref, 1, backward_product(w_ref, ys), acc)

    def rows_of(k):
        start = pl.multiple_of(lax.rem(rep + k, N_REP) * FQ, FQ)
        return acc[:, pl.ds(start, FQ), :]

    own_ref[...] = rows_of(0)
    for k, ref in ((1, s1), (2, s2), (3, s3)):
        ref[...] = rows_of(k).astype(BF16)


def backward_near(plan, rep, ys, weights):
    part = (LOCAL, FQ, BLK)
    return pl.pallas_call(
        backward_near_kernel,
        out_shape=[jax.ShapeDtypeStruct(part, F32)] + [jax.ShapeDtypeStruct(part, BF16)] * 3,
        in_specs=[SM, SM] + [VM] * 5,
        out_specs=[VM] * 4,
        scratch_shapes=[
            pltpu.VMEM((LOCAL + 1, FIN, BLK), BF16),
            pltpu.VMEM((LOCAL, FIN, BLK), F32),
        ],
        compiler_params=TILE_PARAMS,
        cost_estimate=pl.CostEstimate(flops=10**9, bytes_accessed=14 * 10**6, transcendentals=0),
        name="backward_near",
    )(plan, rep, *ys, weights)


SCATTER_PEERS = 8


def fold_kernel(*refs):
    out_ref = refs[-1]
    total = refs[0][...].astype(F32)
    for ref in refs[1:-1]:
        total = total + ref[...].astype(F32)
    out_ref[pl.ds(0, FOLD), :] = total[:FOLD].astype(BF16)
    high, low = halves(total[FOLD : FOLD + GW_ROWS] + total[FOLD + GW_ROWS :])
    out_ref[pl.ds(FOLD, GW_ROWS), :] = high
    out_ref[pl.ds(FOLD + GW_ROWS, GW_ROWS), :] = low


def fold(parts):
    return pl.pallas_call(
        fold_kernel,
        out_shape=jax.ShapeDtypeStruct(parts[0].shape, BF16),
        in_specs=[VM] * len(parts),
        out_specs=VM,
        compiler_params=PARAMS,
        name="fold",
    )(*parts)


def scatter_kernel(
    place_ref, hub_ref, count_ref, rows_ref, recv_ref, own_ref, a_ref, b_ref, c_ref, f0, f1, out_ref, acc, part
):
    chunks = ROWS // LO
    slot = lax.broadcasted_iota(jnp.int32, (1, BLK), 1)
    acc[...] = jnp.zeros_like(acc)

    def step(i, carry):
        hots, sides = [], []
        for j in range(SCATTER_PEERS):
            p = SCATTER_PEERS * i + j
            row = jnp.where(slot < count_ref[0, p], rows_ref[pl.ds(p, 1), :], -1)
            hots.append(low_onehot(column(row)))
            total = recv_ref[p].astype(F32)
            for r in range(1, N_REP):
                total = total + recv_ref[r * N_DOM + p].astype(F32)
            high = lax.shift_right_arithmetic(row, 8)
            pieces = [halves(jnp.where(high == c, total, 0.0)) for c in range(chunks)]
            sides.append(jnp.concatenate([h for h, _ in pieces] + [l for _, l in pieces], axis=0))
        acc[...] += dot(jnp.concatenate(sides, axis=1), jnp.concatenate(hots, axis=0))
        return carry

    lax.fori_loop(0, N_DOM // SCATTER_PEERS, step, 0)
    for b in range(LOCAL):
        c, side = b // 2, b % 2
        lanes = pl.ds(side * BLK, BLK)
        here = acc[pl.ds(c * FQ, FQ), lanes] + acc[pl.ds((chunks + c) * FQ, FQ), lanes]
        near = own_ref[b] + a_ref[b].astype(F32) + b_ref[b].astype(F32) + c_ref[b].astype(F32)
        part[b] = here + near
    for h in range(HUBS):
        block = hub_ref[h]

        @pl.when(lax.shift_right_logical(block, 4) == place_ref[1])
        def _():
            rows = pl.ds(h * FQ, FQ)
            part[block & (LOCAL - 1)] += f0[rows, :].astype(F32) + f1[rows, :].astype(F32)

    out_ref[pl.ds(0, LOCAL * FQ), :] = part[...].reshape(LOCAL * FQ, BLK).astype(BF16)
    total = f0[pl.ds(FOLD, 2 * GW_ROWS), :].astype(F32) + f1[pl.ds(FOLD, 2 * GW_ROWS), :].astype(F32)
    high, low = halves(total[:GW_ROWS] + total[GW_ROWS:])
    out_ref[pl.ds(LOCAL * FQ, GW_ROWS), :] = high
    out_ref[pl.ds(LOCAL * FQ + GW_ROWS, GW_ROWS), :] = low


def scatter_rows(place, hubs, counts, rows, received, own, a, b, c, f0, f1):
    return pl.pallas_call(
        scatter_kernel,
        out_shape=jax.ShapeDtypeStruct((LOCAL * FQ + 2 * GW_ROWS, BLK), BF16),
        in_specs=[SM] * 3 + [VM] * 8,
        out_specs=VM,
        scratch_shapes=[pltpu.VMEM((2 * FIN * 2, LO), F32), pltpu.VMEM((LOCAL, FQ, BLK), F32)],
        compiler_params=PARAMS,
        cost_estimate=pl.CostEstimate(flops=4 * 10**9, bytes_accessed=4 * 10**6, transcendentals=0),
        name="scatter_rows",
    )(place, hubs, counts, rows, received, own, a, b, c, f0, f1)


def final_kernel(rep_ref, m0, m1, m2, m3, gx_ref, gw_ref, blocks, *, scale):
    rep = rep_ref[0]
    for k, ref in enumerate((m0, m1, m2, m3)):
        q = lax.rem(rep + N_REP - k, N_REP)
        start = pl.multiple_of(q * FQ, FQ)
        rows = ref[pl.ds(0, LOCAL * FQ), :].astype(F32)
        blocks[:, pl.ds(start, FQ), :] = rows.reshape(LOCAL, FQ, BLK)
        high = ref[pl.ds(LOCAL * FQ, GW_ROWS), :].astype(F32)
        gw = (high + ref[pl.ds(LOCAL * FQ + GW_ROWS, GW_ROWS), :].astype(F32)) * scale
        gw_ref[pl.ds(start, FQ), :] = jnp.concatenate([gw[:FQ], gw[FQ:]], axis=1)
    for b in range(LOCAL):
        gx_ref[pl.ds(b * BLK, BLK), :] = blocks[b].T


def finish(rep, parts, scale):
    return pl.pallas_call(
        functools.partial(final_kernel, scale=scale),
        out_shape=[
            jax.ShapeDtypeStruct((ROWS, FIN), F32),
            jax.ShapeDtypeStruct((FIN, HID), F32),
        ],
        in_specs=[SM] + [VM] * 4,
        out_specs=[VM, VM],
        scratch_shapes=[pltpu.VMEM((LOCAL, FIN, BLK), F32)],
        compiler_params=PARAMS,
        name="finish",
    )(rep, *parts)


def place_kernel(rep_ref, o0, o1, o2, o3, out_ref):
    for k, ref in enumerate((o0, o1, o2, o3)):
        start = pl.multiple_of(lax.rem(rep_ref[0] + N_REP - k, N_REP) * QUARTER, QUARTER)
        out_ref[pl.ds(start, QUARTER), :] = ref[...]


def place_output(rep, parts):
    return pl.pallas_call(
        place_kernel,
        out_shape=jax.ShapeDtypeStruct((ROWS, HID), BF16),
        in_specs=[SM] + [VM] * 4,
        out_specs=VM,
        compiler_params=PARAMS,
        name="place_output",
    )(rep, *parts)


def turn(value, k):
    return lax.ppermute(value, "rep", [(i, (i + k) % N_REP) for i in range(N_REP)])


def around(value):
    return [value] + [turn(value, k) for k in (1, 2, 3)]


def chips(x, z, core):
    pairs = []
    for i in range(N_DOM):
        to_x, to_z, to_core = (i // 8 + x) % 4, (i // 2 + z) % 4, (i + core) % 2
        pairs.append((i, (to_x * 4 + to_z) * 2 + to_core))
    return pairs


def over_chips(value, axis):
    if axis == "x":
        return [value] + [lax.ppermute(value, "dom", chips(k, 0, 0)) for k in (1, 2, 3)]
    return [value] + [lax.ppermute(value, "dom", chips(0, k, 0)) for k in (1, 2, 3)]


def over_cores(value):
    return [value, lax.ppermute(value, "dom", chips(0, 0, 1))]


def total(parts):
    return functools.reduce(lambda a, b: a + b, parts)


def swap(value, axes):
    return lax.all_to_all(value, axes, split_axis=0, concat_axis=0, tiled=True)


def shards(
    features,
    proj_weight,
    bias,
    cotangent,
    send_rows,
    send_count,
    hub_blocks,
    tile_dst,
    tile_src,
    tile_weight,
):
    rep = lax.axis_index("rep").astype(jnp.int32)
    dom = lax.axis_index("dom").astype(jnp.int32)
    place = jnp.stack([rep, dom])
    blocks = features.reshape(LOCAL, BLK, FIN)
    weights = tile_weight[0, 0]
    rows = send_rows[0]

    listed = gather_rows(rows, send_count, features)
    received = swap(listed, "dom")
    hub = pick_hubs(hub_blocks, place, blocks)
    hub = total(over_cores(hub))
    hub = total(over_chips(hub, "x"))
    hub = total(over_chips(hub, "z"))
    hubs = around(hub)
    fwd, bwd = order_tiles(
        tile_dst[0, 0].reshape(TILES // BLK, BLK), tile_src[0, 0].reshape(TILES // BLK, BLK)
    )
    near = forward_near(fwd, blocks, weights)
    own, s1, s2, s3 = forward_far(fwd, place, near, received, hubs, weights)
    a, b, c = turn(s1, 1), turn(s2, 2), turn(s3, 3)
    out_part, y_part, *gws = middle(
        place, own, a, b, c, proj_weight, bias.reshape(1, HID), cotangent
    )
    ys = around(y_part)
    out_part, ys = lax.optimization_barrier((out_part, ys))
    outs = around(out_part)
    message, *folds = backward_far(bwd, place, ys, gws, weights)
    returned = swap(message.reshape(N_REP * N_DOM, FQ, BLK), ("rep", "dom"))
    shared = fold([folds[0]] + [turn(folds[k], k) for k in (1, 2, 3)])
    shared = fold(over_chips(shared, "z"))
    shared = fold(over_chips(shared, "x"))
    f0, f1 = over_cores(shared)
    own, s1, s2, s3 = backward_near(bwd, place, ys, weights)
    a, b, c = turn(s1, 1), turn(s2, 2), turn(s3, 3)
    output = place_output(place, outs)
    returned, output = lax.optimization_barrier((returned, output))

    part = scatter_rows(place, hub_blocks, send_count, rows, returned, own, a, b, c, f0, f1)
    grad_x, grad_w = finish(place, around(part), 1.0 / math.sqrt(ROWS * N_DOM))
    return (output, grad_x, grad_w)


def solution(mesh):
    in_specs = (
        P("dom", None),
        P(),
        P(),
        P("dom", None),
        P("dom", None, None),
        P("dom", None),
        P(),
        P("rep", "dom", None),
        P("rep", "dom", None),
        P("rep", "dom", None, None, None),
    )
    out_specs = (P("dom", None), P("dom", None), P())
    return jax.shard_map(shards, mesh=mesh, in_specs=in_specs, out_specs=out_specs, check_vma=False)
```

time: 191 us -> 173 us (0.906)
  waiting for transfers between devices: 74.9 us -> 49.8 us
  Pallas kernels: 55.8 us -> 32.6 us
  starting transfers between devices: 49.7 us -> 70.3 us
  local copies, waits for them, and re-layouts: 3.89 us -> 17.4 us
  other arithmetic: 2.45 us -> 0.17 us
    all_to_all x4 -> x2, waiting for transfers between devices: 42.2 us -> 0.01 us  [swap(): return lax.all_to_all(value, axes, split_axis=0, concat_axis=0, tiled=True)]
    pallas_call x6 -> x12, Pallas kernels: 53.3 us -> 29 us  [the longest x1 6.7 us: backward_far(): pl.pallas_call(backward_far_kernel, out_shape=[jax.ShapeDtypeStruct((N_RE...]
    ppermute x0 -> x14, starting transfers between devices: none -> 24.2 us  [the longest x6 10.2 us: over_chips(): lax.ppermute(value, 'dom', chips(0, k, 0))]
    unnamed x18 -> x32, local copies, waits for them, and re-layouts: 0.04 us -> 17.4 us
    ppermute x0 -> x14, waiting for transfers between devices: none -> 16.8 us  [the longest x6 10.7 us: over_chips(): lax.ppermute(value, 'dom', chips(k, 0, 0))]
    all_to_all x4 -> x2, starting transfers between devices: 29.2 us -> 21 us  [swap(): return lax.all_to_all(value, axes, split_axis=0, concat_axis=0, tiled=True)]
    ppermute x15 -> x21, starting transfers between devices: 20.5 us -> 25.1 us  [turn(): lax.ppermute(value, 'rep', [(i, (i + k) % N_REP) for i in range(N_REP)])]
    ppermute x15 -> x21, waiting for transfers between devices: 32.7 us -> 33 us  [turn(): lax.ppermute(value, 'rep', [(i, (i + k) % N_REP) for i in range(N_REP)])]
  transfers between devices with their start and end apart: 19 -> 37, of which waited for: 10 -> 16; matrix products, arithmetic and copies ran while one was open for 1% -> 0% of each run, Pallas kernels for 9% -> 5%
where the time goes in v2:
time: 173 us; the launch traced here: 171 us
  starting transfers between devices  70.3 us (41%)
  waiting for transfers between devices  49.8 us (29%)
  Pallas kernels  32.6 us (19%)
  local copies, waits for them, and re-layouts  17.4 us (10%)
    ppermute x21, waiting for transfers between devices, turn(): lax.ppermute(value, 'rep', [(i, (i + k) % N_REP) for i in range(N_REP)])  33 us
    ppermute x21, starting transfers between devices, turn(): lax.ppermute(value, 'rep', [(i, (i + k) % N_REP) for i in range(N_REP)])  25.1 us
    all_to_all x2, starting transfers between devices, swap(): return lax.all_to_all(value, axes, split_axis=0, concat_axis=0, tiled=True)  21 us
    unnamed x32, local copies, waits for them, and re-layouts  17.4 us
    ppermute x6, waiting for transfers between devices, over_chips(): lax.ppermute(value, 'dom', chips(k, 0, 0))  10.7 us
    ppermute x6, starting transfers between devices, over_chips(): lax.ppermute(value, 'dom', chips(0, k, 0))  10.2 us
    ppermute x6, starting transfers between devices, over_chips(): lax.ppermute(value, 'dom', chips(k, 0, 0))  9.89 us
    pallas_call x1, Pallas kernels, backward_far(): pl.pallas_call(backward_far_kernel, out_shape=[jax.ShapeDtypeStruct((N_RE...  6.7 us
  transfers between devices with their start and end apart: 37, of which 16 were waited for; matrix products, arithmetic and copies ran while one was open for 0% of the time, Pallas kernels for 5%

profile of v2, /device:TPU:1, one launch (start us, length us, event | category | flops | bytes accessed | tf_op | source)
XLA Modules:
  0.0 171.2 jit_solution(5498544493034823049)
XLA Ops:
  3.1 5.5 %gather_rows.1 = bf16[32,128,128]{2,1,0:T(8,128)(2,1)} custom-call(s32[32,128]{1,0:T(8,128)S(1)} %bitcast.18, s32[1,32]{1,0:T(1,128)S(1)} %copy-done.12, bf16[2048,128]{1,0:T(8,128)(2,1)S(1)} %copy-done.4), custom_call_target="tpu_custom_call" | custom-call | flops 4000000000 | bytes 2000000 | tf_op jit(solution)/shard_map/gather_rows/pallas_call | solution.py:192
  8.5 9.4 %all-to-all-start = ((bf16[32,128,128]{2,1,0:T(8,128)(2,1)}), bf16[32,128,128]{2,1,0:T(8,128)(2,1)S(1)}, u32[]{:S(2)}, u32[]{:S(2)}) async-start(bf16[32,128,128]{2,1,0:T(8,128)(2,1)} %gather_rows.1), calls=%async_computation | async-start | bytes 2097152 | tf_op jit(solution)/shard_map/all_to_all | solution.py:585
  20.0 1.5 collective-permute-start.1
  21.5 2.4 %collective-permute-start.2 = (bf16[2,128,128]{2,1,0:T(8,128)(2,1)S(1)}, bf16[2,128,128]{2,1,0:T(8,128)(2,1)S(1)}, u32[]{:S(2)}, u32[]{:S(2)}) collective-permute-start(bf16[2,128,128]{2,1,0:T(8,128)(2,1)S(1)} %add.21), channel_id=1, source_target_pairs={{0,16},{1,17},{2,18},{3,19},{4,20},{5,21},{6,22},{7,23},{8,24},{9,... | collective-permute-start | bytes 196616 | tf_op jit(solution)/shard_map/ppermute | solution.py:572
  25.1 9.1 %collective-permute-done.1 = bf16[2,128,128]{2,1,0:T(8,128)(2,1)S(1)} collective-permute-done((bf16[2,128,128]{2,1,0:T(8,128)(2,1)S(1)}, bf16[2,128,128]{2,1,0:T(8,128)(2,1)S(1)}, u32[]{:S(2)}, u32[]{:S(2)}) %collective-permute-start.1) | collective-permute-done | bytes 65568 | tf_op jit(solution)/shard_map/ppermute | solution.py:572
  34.1 1.7 collective-permute-done.2
  35.8 1.3 collective-permute-start.4
  37.1 2.4 %collective-permute-start.5 = (bf16[2,128,128]{2,1,0:T(8,128)(2,1)S(1)}, bf16[2,128,128]{2,1,0:T(8,128)(2,1)S(1)}, u32[]{:S(2)}, u32[]{:S(2)}) collective-permute-start(bf16[2,128,128]{2,1,0:T(8,128)(2,1)S(1)} %add_add_fusion.1), channel_id=1, source_target_pairs={{0,4},{1,5},{2,6},{3,7},{4,0},{5,1},{6,2},{7,3},{8,12},{9,13},{10,... | collective-permute-start | bytes 196616 | tf_op jit(solution)/shard_map/ppermute | solution.py:573
  40.7 1.2 order_tiles.1
  41.9 1.5 collective-permute-done.6
  43.4 1.4 collective-permute-start.7
  44.8 2.6 %collective-permute-start.8 = (bf16[2,128,128]{2,1,0:T(8,128)(2,1)S(1)}, bf16[2,128,128]{2,1,0:T(8,128)(2,1)S(1)}, u32[]{:S(2)}, u32[]{:S(2)}) collective-permute-start(bf16[2,128,128]{2,1,0:T(8,128)(2,1)S(1)} %add_add_fusion.h0), channel_id=1, source_target_pairs={{0,64},{32,96},{64,0},{96,32},{1,65},{33,97},{65,1},{97,33},{2,66}... | collective-permute-start | bytes 196616 | tf_op jit(solution)/shard_map/ppermute | solution.py:555
  48.5 4.6 %copy-done = bf16[1,1,384,128,128]{4,3,2,1,0:T(8,128)(2,1)S(1)} copy-done((bf16[1,1,384,128,128]{4,3,2,1,0:T(8,128)(2,1)S(1)}, bf16[1,1,384,128,128]{4,3,2,1,0:T(8,128)(2,1)}, u32[]{:S(2)}) %copy-start) | copy-done | bytes 12582936
  53.0 2.6 %forward_near.1.near_ref = f32[16,128,128]{2,1,0:T(8,128)S(1)} custom-call(s32[4,4,128]{2,1,0:T(4,128)S(1)} %get-tuple-element.34.plan_ref, bf16[16,128,128]{2,1,0:T(8,128)(2,1)S(1)} %bitcast.14, bf16[384,128,128]{2,1,0:T(8,128)(2,1)S(1)} %bitcast.9), custom_call_target="tpu_custom_call" | custom-call | flops 1000000000 | bytes 14000000 | tf_op jit(solution)/shard_map/forward_near/pallas_call | solution.py:244
  55.7 4.6 %copy-done.1 = bf16[1,1,384,128,128]{4,3,2,1,0:T(8,128)(2,1)S(1)} copy-done((bf16[1,1,384,128,128]{4,3,2,1,0:T(8,128)(2,1)S(1)}, bf16[1,1,384,128,128]{4,3,2,1,0:T(8,128)(2,1)}, u32[]{:S(2)}) %copy-start.1) | copy-done | bytes 12582936
  60.3 5.1 %forward_far.1 = (f32[4,128,128]{2,1,0:T(8,128)S(1)}, bf16[4,128,128]{2,1,0:T(8,128)(2,1)S(1)}, bf16[4,128,128]{2,1,0:T(8,128)(2,1)S(1)}, bf16[4,128,128]{2,1,0:T(8,128)(2,1)S(1)}) custom-call(s32[4,4,128]{2,1,0:T(4,128)S(1)} %get-tuple-element.34.plan_ref, s32[2]{0:T(128)S(1)} %pad_add_fusion.place_ref.rep_ref, f32[16,128,128]{2,1,0:T(8,128)S(1)} %forward_near.1.near_ref, ...), custom_call_target="tpu_custom_call" | custom-call | flops 4000000000 | bytes 14000000 | tf_op jit(solution)/shard_map/forward_far/pallas_call | solution.py:274
  65.8 1.2 collective-permute-start.11
  67.1 1.2 collective-permute-start.12
  68.3 3.4 %collective-permute-done.10.a_ref = bf16[4,128,128]{2,1,0:T(8,128)(2,1)S(1)} collective-permute-done((bf16[4,128,128]{2,1,0:T(8,128)(2,1)S(1)}, bf16[4,128,128]{2,1,0:T(8,128)(2,1)S(1)}, u32[]{:S(2)}, u32[]{:S(2)}) %collective-permute-start.10) | collective-permute-done | bytes 131104 | tf_op jit(solution)/shard_map/ppermute | solution.py:555
  72.5 1.2 copy-done.6
  73.7 1.5 middle.1
  75.8 3.0 %collective-permute-start.14 = (bf16[4,128,128]{2,1,0:T(8,128)(2,1)S(1)}, bf16[4,128,128]{2,1,0:T(8,128)(2,1)S(1)}, u32[]{:S(2)}, u32[]{:S(2)}) collective-permute-start(bf16[4,128,128]{2,1,0:T(8,128)(2,1)S(1)} %get-tuple-element.41.y0), channel_id=1, source_target_pairs={{0,64},{32,96},{64,0},{96,32},{1,65},{33,97},{65,1},{97,33},{2,66}... | collective-permute-start | bytes 393224 | tf_op jit(solution)/shard_map/ppermute | solution.py:555
  78.8 1.6 collective-permute-done.13.y1
  80.4 2.2 %collective-permute-done.14.y2 = bf16[4,128,128]{2,1,0:T(8,128)(2,1)S(1)} collective-permute-done((bf16[4,128,128]{2,1,0:T(8,128)(2,1)S(1)}, bf16[4,128,128]{2,1,0:T(8,128)(2,1)S(1)}, u32[]{:S(2)}, u32[]{:S(2)}) %collective-permute-start.14) | collective-permute-done | bytes 131104 | tf_op jit(solution)/shard_map/ppermute | solution.py:555
  82.6 6.7 %backward_far.1 = (bf16[4,32,32,128]{3,2,1,0:T(8,128)(2,1)}, bf16[384,128]{1,0:T(8,128)(2,1)S(1)}, bf16[384,128]{1,0:T(8,128)(2,1)S(1)}, bf16[384,128]{1,0:T(8,128)(2,1)S(1)}, bf16[384,128]{1,0:T(8,128)(2,1)S(1)}) custom-call(s32[4,4,128]{2,1,0:T(4,128)S(1)} %get-tuple-element.33.plan_ref, s32[2]{0:T(128)S(1)} %pad_add_fusion.place_ref.rep_ref, ...), custom_call_target="tpu_custom_call" | custom-call | flops 4000000000 | bytes 14000000 | tf_op jit(solution)/shard_map/backward_far/pallas_call | solution.py:378
  89.3 11.6 %all-to-all-start.1 = ((bf16[128,32,128]{2,1,0:T(8,128)(2,1)}), bf16[128,32,128]{2,1,0:T(8,128)(2,1)S(1)}, u32[]{:S(2)}, u32[]{:S(2)}) async-start(bf16[128,32,128]{2,1,0:T(8,128)(2,1)} %bitcast.6), calls=%async_computation.1 | async-start | bytes 2097152 | tf_op jit(solution)/shard_map/all_to_all | solution.py:585
  100.9 1.5 collective-permute-start.16
  102.3 1.2 collective-permute-start.22
  103.5 1.5 collective-permute-start.23
  105.1 1.8 %collective-permute-start.24 = (bf16[384,128]{1,0:T(8,128)(2,1)S(1)}, bf16[384,128]{1,0:T(8,128)(2,1)S(1)}, u32[]{:S(2)}, u32[]{:S(2)}) collective-permute-start(bf16[384,128]{1,0:T(8,128)(2,1)S(1)} %get-tuple-element.60), channel_id=1, source_target_pairs={{0,96},{32,0},{64,32},{96,64},{1,97},{33,1},{65,33},{97,65},{2,98}... | collective-permute-start | bytes 294920 | tf_op jit(solution)/shard_map/ppermute | solution.py:555
  106.8 15.9 %collective-permute-done.22.refs_1_ = bf16[384,128]{1,0:T(8,128)(2,1)S(1)} collective-permute-done((bf16[384,128]{1,0:T(8,128)(2,1)S(1)}, bf16[384,128]{1,0:T(8,128)(2,1)S(1)}, u32[]{:S(2)}, u32[]{:S(2)}) %collective-permute-start.22) | collective-permute-done | bytes 98336 | tf_op jit(solution)/shard_map/ppermute | solution.py:555
  122.7 2.2 %collective-permute-done.23.refs_2_ = bf16[384,128]{1,0:T(8,128)(2,1)S(1)} collective-permute-done((bf16[384,128]{1,0:T(8,128)(2,1)S(1)}, bf16[384,128]{1,0:T(8,128)(2,1)S(1)}, u32[]{:S(2)}, u32[]{:S(2)}) %collective-permute-start.23) | collective-permute-done | bytes 98336 | tf_op jit(solution)/shard_map/ppermute | solution.py:555
  125.0 1.5 collective-permute-start.25
  126.6 2.9 %collective-permute-start.26 = (bf16[384,128]{1,0:T(8,128)(2,1)S(1)}, bf16[384,128]{1,0:T(8,128)(2,1)S(1)}, u32[]{:S(2)}, u32[]{:S(2)}) collective-permute-start(bf16[384,128]{1,0:T(8,128)(2,1)S(1)} %fold.3.refs_0_), channel_id=1, source_target_pairs={{0,4},{1,5},{2,6},{3,7},{4,0},{5,1},{6,2},{7,3},{8,12},{9,13},{10,... | collective-permute-start | bytes 294920 | tf_op jit(solution)/shard_map/ppermute | solution.py:573
  130.5 3.0 %collective-permute-done.26.refs_2_ = bf16[384,128]{1,0:T(8,128)(2,1)S(1)} collective-permute-done((bf16[384,128]{1,0:T(8,128)(2,1)S(1)}, bf16[384,128]{1,0:T(8,128)(2,1)S(1)}, u32[]{:S(2)}, u32[]{:S(2)}) %collective-permute-start.26) | collective-permute-done | bytes 98336 | tf_op jit(solution)/shard_map/ppermute | solution.py:573
  134.2 1.3 collective-permute-start.28
  135.4 2.4 %collective-permute-start.29 = (bf16[384,128]{1,0:T(8,128)(2,1)S(1)}, bf16[384,128]{1,0:T(8,128)(2,1)S(1)}, u32[]{:S(2)}, u32[]{:S(2)}) collective-permute-start(bf16[384,128]{1,0:T(8,128)(2,1)S(1)} %fold.4.refs_0_), channel_id=1, source_target_pairs={{0,16},{1,17},{2,18},{3,19},{4,20},{5,21},{6,22},{7,23},{8,24},{9,... | collective-permute-start | bytes 294920 | tf_op jit(solution)/shard_map/ppermute | solution.py:572
  137.8 1.2 collective-permute-start.30
  139.0 4.6 %copy-done.3 = bf16[1,1,384,128,128]{4,3,2,1,0:T(8,128)(2,1)S(1)} copy-done((bf16[1,1,384,128,128]{4,3,2,1,0:T(8,128)(2,1)S(1)}, bf16[1,1,384,128,128]{4,3,2,1,0:T(8,128)(2,1)}, u32[]{:S(2)}) %copy-start.3) | copy-done | bytes 12582936
  143.6 2.7 %backward_near.1 = (f32[16,32,128]{2,1,0:T(8,128)S(1)}, bf16[16,32,128]{2,1,0:T(8,128)(2,1)S(1)}, bf16[16,32,128]{2,1,0:T(8,128)(2,1)S(1)}, bf16[16,32,128]{2,1,0:T(8,128)(2,1)S(1)}) custom-call(s32[4,4,128]{2,1,0:T(4,128)S(1)} %get-tuple-element.33.plan_ref, s32[2]{0:T(128)S(1)} %pad_add_fusion.place_ref.rep_ref, ...), custom_call_target="tpu_custom_call" | custom-call | flops 1000000000 | bytes 14000000 | tf_op jit(solution)/shard_map/backward_near/pallas_call | solution.py:411
  146.4 2.6 %collective-permute-start.20 = (bf16[16,32,128]{2,1,0:T(8,128)(2,1)S(1)}, bf16[16,32,128]{2,1,0:T(8,128)(2,1)S(1)}, u32[]{:S(2)}, u32[]{:S(2)}) collective-permute-start(bf16[16,32,128]{2,1,0:T(8,128)(2,1)S(1)} %get-tuple-element.55), channel_id=1, source_target_pairs={{0,64},{32,96},{64,0},{96,32},{1,65},{33,97},{65,1},{97,33},{2,66}... | collective-permute-start | bytes 393224 | tf_op jit(solution)/shard_map/ppermute | solution.py:555
  149.0 2.0 %collective-permute-start.21 = (bf16[16,32,128]{2,1,0:T(8,128)(2,1)S(1)}, bf16[16,32,128]{2,1,0:T(8,128)(2,1)S(1)}, u32[]{:S(2)}, u32[]{:S(2)}) collective-permute-start(bf16[16,32,128]{2,1,0:T(8,128)(2,1)S(1)} %get-tuple-element.56), channel_id=1, source_target_pairs={{0,96},{32,0},{64,32},{96,64},{1,97},{33,1},{65,33},{97,65},{2,98}... | collective-permute-start | bytes 393224 | tf_op jit(solution)/shard_map/ppermute | solution.py:555
  151.1 3.8 %collective-permute-start.31 = (bf16[384,128]{1,0:T(8,128)(2,1)S(1)}, bf16[384,128]{1,0:T(8,128)(2,1)S(1)}, u32[]{:S(2)}, u32[]{:S(2)}) collective-permute-start(bf16[384,128]{1,0:T(8,128)(2,1)S(1)} %fold.5.f0), channel_id=1, source_target_pairs={{0,1},{1,0},{2,3},{3,2},{4,5},{5,4},{6,7},{7,6},{8,9},{9,8},{10,11... | collective-permute-start | bytes 294920 | tf_op jit(solution)/shard_map/ppermute | solution.py:577
  154.9 1.6 place_output.1
  156.6 3.0 %scatter_rows.1.m0 = bf16[640,128]{1,0:T(8,128)(2,1)S(1)} custom-call(s32[2]{0:T(128)S(1)} %pad_add_fusion.place_ref.rep_ref, s32[8]{0:T(128)S(1)} %copy-done.9, s32[1,32]{1,0:T(1,128)S(1)} %copy-done.13, s32[32,128]{1,0:T(8,128)S(1)} %bitcast.19, bf16[128,32,128]{2,1,0:T(8,128)(2,1)S(1)} %all-to-all-done.1.recv_ref, ...), custom_call_target="tpu_custom_call" | custom-call | flops 4000000000 | bytes 4000000 | tf_op jit(solution)/shard_map/scatter_rows/pallas_call | solution.py:496
  160.6 1.8 %collective-permute-start.34 = (bf16[640,128]{1,0:T(8,128)(2,1)S(1)}, bf16[640,128]{1,0:T(8,128)(2,1)S(1)}, u32[]{:S(2)}, u32[]{:S(2)}) collective-permute-start(bf16[640,128]{1,0:T(8,128)(2,1)S(1)} %scatter_rows.1.m0), channel_id=1, source_target_pairs={{0,96},{32,0},{64,32},{96,64},{1,97},{33,1},{65,33},{97,65},{2,98}... | collective-permute-start | bytes 491528 | tf_op jit(solution)/shard_map/ppermute | solution.py:555
  162.4 6.0 %collective-permute-done.32.m1 = bf16[640,128]{1,0:T(8,128)(2,1)S(1)} collective-permute-done((bf16[640,128]{1,0:T(8,128)(2,1)S(1)}, bf16[640,128]{1,0:T(8,128)(2,1)S(1)}, u32[]{:S(2)}, u32[]{:S(2)}) %collective-permute-start.32) | collective-permute-done | bytes 163872 | tf_op jit(solution)/shard_map/ppermute | solution.py:555
  169.2 2.0 %finish.1 = (f32[2048,128]{1,0:T(8,128)}, f32[128,256]{1,0:T(8,128)}) custom-call(s32[2]{0:T(128)S(1)} %pad_add_fusion.place_ref.rep_ref, bf16[640,128]{1,0:T(8,128)(2,1)S(1)} %scatter_rows.1.m0, bf16[640,128]{1,0:T(8,128)(2,1)S(1)} %collective-permute-done.32.m1, bf16[640,128]{1,0:T(8,128)(2,1)S(1)} %collective-permute-done.33.m2, ...), custom_call_target="tpu_custom_call" | custom-call | tf_op jit(solution)/shard_map/finish/pallas_call | solution.py:523
  (78 shorter events, 13.6 us)
Async XLA Ops:
  0.6 17.4 %copy-start.9 = (s32[8]{0:T(128)S(1)}, s32[8]{0:T(128)}, u32[]{:S(2)}) copy-start(s32[8]{0:T(128)} %hub_ref.3) | copy-start | bytes 100
  3.1 15.0 %copy-start.5 = (bf16[2048,128]{1,0:T(8,128)(2,1)S(1)}, bf16[2048,128]{1,0:T(8,128)(2,1)}, u32[]{:S(2)}) copy-start(bf16[2048,128]{1,0:T(8,128)(2,1)} %feat_ref.1) | copy-start | bytes 1572868
  3.1 37.6 %copy-start.14 = (s32[1,1,384]{2,1,0:T(1,128)S(1)}, s32[1,1,384]{2,1,0:T(1,128)}, u32[]{:S(2)}) copy-start(s32[1,1,384]{2,1,0:T(1,128)} %param.17) | copy-start | bytes 4612
  3.1 37.6 %copy-start.15 = (s32[1,1,384]{2,1,0:T(1,128)S(1)}, s32[1,1,384]{2,1,0:T(1,128)}, u32[]{:S(2)}) copy-start(s32[1,1,384]{2,1,0:T(1,128)} %param.18) | copy-start | bytes 4612
  8.5 47.2 %all-to-all-start = ((bf16[32,128,128]{2,1,0:T(8,128)(2,1)}), bf16[32,128,128]{2,1,0:T(8,128)(2,1)S(1)}, u32[]{:S(2)}, u32[]{:S(2)}) async-start(bf16[32,128,128]{2,1,0:T(8,128)(2,1)} %gather_rows.1), calls=%async_computation | async-start | bytes 2097152 | tf_op jit(solution)/shard_map/all_to_all | solution.py:585
  18.6 1.3 collective-permute-start
  20.0 14.1 %collective-permute-start.1 = (bf16[2,128,128]{2,1,0:T(8,128)(2,1)S(1)}, bf16[2,128,128]{2,1,0:T(8,128)(2,1)S(1)}, u32[]{:S(2)}, u32[]{:S(2)}) collective-permute-start(bf16[2,128,128]{2,1,0:T(8,128)(2,1)S(1)} %add.21), channel_id=1, source_target_pairs={{0,8},{1,9},{2,10},{3,11},{4,12},{5,13},{6,14},{7,15},{8,16},{9,17... | collective-permute-start | bytes 196616 | tf_op jit(solution)/shard_map/ppermute | solution.py:572
  21.5 14.3 %collective-permute-start.2 = (bf16[2,128,128]{2,1,0:T(8,128)(2,1)S(1)}, bf16[2,128,128]{2,1,0:T(8,128)(2,1)S(1)}, u32[]{:S(2)}, u32[]{:S(2)}) collective-permute-start(bf16[2,128,128]{2,1,0:T(8,128)(2,1)S(1)} %add.21), channel_id=1, source_target_pairs={{0,16},{1,17},{2,18},{3,19},{4,20},{5,21},{6,22},{7,23},{8,24},{9,... | collective-permute-start | bytes 196616 | tf_op jit(solution)/shard_map/ppermute | solution.py:572
  23.9 11.9 %collective-permute-start.3 = (bf16[2,128,128]{2,1,0:T(8,128)(2,1)S(1)}, bf16[2,128,128]{2,1,0:T(8,128)(2,1)S(1)}, u32[]{:S(2)}, u32[]{:S(2)}) collective-permute-start(bf16[2,128,128]{2,1,0:T(8,128)(2,1)S(1)} %add.21), channel_id=1, source_target_pairs={{0,24},{1,25},{2,26},{3,27},{4,28},{5,29},{6,30},{7,31},{8,0},{9,1... | collective-permute-start | bytes 196616 | tf_op jit(solution)/shard_map/ppermute | solution.py:572
  35.8 6.1 %collective-permute-start.4 = (bf16[2,128,128]{2,1,0:T(8,128)(2,1)S(1)}, bf16[2,128,128]{2,1,0:T(8,128)(2,1)S(1)}, u32[]{:S(2)}, u32[]{:S(2)}) collective-permute-start(bf16[2,128,128]{2,1,0:T(8,128)(2,1)S(1)} %add_add_fusion.1), channel_id=1, source_target_pairs={{0,2},{1,3},{2,4},{3,5},{4,6},{5,7},{6,0},{7,1},{8,10},{9,11},{10,... | collective-permute-start | bytes 196616 | tf_op jit(solution)/shard_map/ppermute | solution.py:573
  37.1 4.9 %collective-permute-start.5 = (bf16[2,128,128]{2,1,0:T(8,128)(2,1)S(1)}, bf16[2,128,128]{2,1,0:T(8,128)(2,1)S(1)}, u32[]{:S(2)}, u32[]{:S(2)}) collective-permute-start(bf16[2,128,128]{2,1,0:T(8,128)(2,1)S(1)} %add_add_fusion.1), channel_id=1, source_target_pairs={{0,4},{1,5},{2,6},{3,7},{4,0},{5,1},{6,2},{7,3},{8,12},{9,13},{10,... | collective-permute-start | bytes 196616 | tf_op jit(solution)/shard_map/ppermute | solution.py:573
  39.5 3.9 %collective-permute-start.6 = (bf16[2,128,128]{2,1,0:T(8,128)(2,1)S(1)}, bf16[2,128,128]{2,1,0:T(8,128)(2,1)S(1)}, u32[]{:S(2)}, u32[]{:S(2)}) collective-permute-start(bf16[2,128,128]{2,1,0:T(8,128)(2,1)S(1)} %add_add_fusion.1), channel_id=1, source_target_pairs={{0,6},{1,7},{2,0},{3,1},{4,2},{5,3},{6,4},{7,5},{8,14},{9,15},{10,... | collective-permute-start | bytes 196616 | tf_op jit(solution)/shard_map/ppermute | solution.py:573
  43.4 12.3 %collective-permute-start.7 = (bf16[2,128,128]{2,1,0:T(8,128)(2,1)S(1)}, bf16[2,128,128]{2,1,0:T(8,128)(2,1)S(1)}, u32[]{:S(2)}, u32[]{:S(2)}) collective-permute-start(bf16[2,128,128]{2,1,0:T(8,128)(2,1)S(1)} %add_add_fusion.h0), channel_id=1, source_target_pairs={{0,32},{32,64},{64,96},{96,0},{1,33},{33,65},{65,97},{97,1},{2,34}... | collective-permute-start | bytes 196616 | tf_op jit(solution)/shard_map/ppermute | solution.py:555
  44.8 10.9 %collective-permute-start.8 = (bf16[2,128,128]{2,1,0:T(8,128)(2,1)S(1)}, bf16[2,128,128]{2,1,0:T(8,128)(2,1)S(1)}, u32[]{:S(2)}, u32[]{:S(2)}) collective-permute-start(bf16[2,128,128]{2,1,0:T(8,128)(2,1)S(1)} %add_add_fusion.h0), channel_id=1, source_target_pairs={{0,64},{32,96},{64,0},{96,32},{1,65},{33,97},{65,1},{97,33},{2,66}... | collective-permute-start | bytes 196616 | tf_op jit(solution)/shard_map/ppermute | solution.py:555
  47.4 8.3 %collective-permute-start.9 = (bf16[2,128,128]{2,1,0:T(8,128)(2,1)S(1)}, bf16[2,128,128]{2,1,0:T(8,128)(2,1)S(1)}, u32[]{:S(2)}, u32[]{:S(2)}) collective-permute-start(bf16[2,128,128]{2,1,0:T(8,128)(2,1)S(1)} %add_add_fusion.h0), channel_id=1, source_target_pairs={{0,96},{32,0},{64,32},{96,64},{1,97},{33,1},{65,33},{97,65},{2,98}... | collective-permute-start | bytes 196616 | tf_op jit(solution)/shard_map/ppermute | solution.py:555
  48.5 4.6 %copy-start = (bf16[1,1,384,128,128]{4,3,2,1,0:T(8,128)(2,1)S(1)}, bf16[1,1,384,128,128]{4,3,2,1,0:T(8,128)(2,1)}, u32[]{:S(2)}) copy-start(bf16[1,1,384,128,128]{4,3,2,1,0:T(8,128)(2,1)} %param.19) | copy-start | bytes 37748740
  53.0 19.5 %copy-start.7 = (bf16[128,256]{1,0:T(8,128)(2,1)S(1)}, bf16[128,256]{1,0:T(8,128)(2,1)}, u32[]{:S(2)}) copy-start(bf16[128,256]{1,0:T(8,128)(2,1)} %w_ref.1) | copy-start | bytes 196612
  53.0 19.5 %copy-start.8 = (f32[256]{0:T(256)S(1)}, f32[256]{0:T(256)}, u32[]{:S(2)}) copy-start(f32[256]{0:T(256)} %param.12) | copy-start | bytes 3076
  55.7 4.6 %copy-start.1 = (bf16[1,1,384,128,128]{4,3,2,1,0:T(8,128)(2,1)S(1)}, bf16[1,1,384,128,128]{4,3,2,1,0:T(8,128)(2,1)}, u32[]{:S(2)}) copy-start(bf16[1,1,384,128,128]{4,3,2,1,0:T(8,128)(2,1)} %param.19) | copy-start | bytes 37748740
  60.3 22.3 %copy-start.2 = (bf16[1,1,384,128,128]{4,3,2,1,0:T(8,128)(2,1)S(1)}, bf16[1,1,384,128,128]{4,3,2,1,0:T(8,128)(2,1)}, u32[]{:S(2)}) copy-start(bf16[1,1,384,128,128]{4,3,2,1,0:T(8,128)(2,1)} %param.19) | copy-start | bytes 37748740
  65.4 6.4 %collective-permute-start.10 = (bf16[4,128,128]{2,1,0:T(8,128)(2,1)S(1)}, bf16[4,128,128]{2,1,0:T(8,128)(2,1)S(1)}, u32[]{:S(2)}, u32[]{:S(2)}) collective-permute-start(bf16[4,128,128]{2,1,0:T(8,128)(2,1)S(1)} %get-tuple-element.36), channel_id=1, source_target_pairs={{0,32},{32,64},{64,96},{96,0},{1,33},{33,65},{65,97},{97,1},{2,34}... | collective-permute-start | bytes 393224 | tf_op jit(solution)/shard_map/ppermute | solution.py:555
  65.8 6.2 %collective-permute-start.11 = (bf16[4,128,128]{2,1,0:T(8,128)(2,1)S(1)}, bf16[4,128,128]{2,1,0:T(8,128)(2,1)S(1)}, u32[]{:S(2)}, u32[]{:S(2)}) collective-permute-start(bf16[4,128,128]{2,1,0:T(8,128)(2,1)S(1)} %get-tuple-element.37), channel_id=1, source_target_pairs={{0,64},{32,96},{64,0},{96,32},{1,65},{33,97},{65,1},{97,33},{2,66}... | collective-permute-start | bytes 393224 | tf_op jit(solution)/shard_map/ppermute | solution.py:555
  67.1 5.4 %collective-permute-start.12 = (bf16[4,128,128]{2,1,0:T(8,128)(2,1)S(1)}, bf16[4,128,128]{2,1,0:T(8,128)(2,1)S(1)}, u32[]{:S(2)}, u32[]{:S(2)}) collective-permute-start(bf16[4,128,128]{2,1,0:T(8,128)(2,1)S(1)} %get-tuple-element.38), channel_id=1, source_target_pairs={{0,96},{32,0},{64,32},{96,64},{1,97},{33,1},{65,33},{97,65},{2,98}... | collective-permute-start | bytes 393224 | tf_op jit(solution)/shard_map/ppermute | solution.py:555
  75.3 5.1 %collective-permute-start.13 = (bf16[4,128,128]{2,1,0:T(8,128)(2,1)S(1)}, bf16[4,128,128]{2,1,0:T(8,128)(2,1)S(1)}, u32[]{:S(2)}, u32[]{:S(2)}) collective-permute-start(bf16[4,128,128]{2,1,0:T(8,128)(2,1)S(1)} %get-tuple-element.41.y0), channel_id=1, source_target_pairs={{0,32},{32,64},{64,96},{96,0},{1,33},{33,65},{65,97},{97,1},{2,34}... | collective-permute-start | bytes 393224 | tf_op jit(solution)/shard_map/ppermute | solution.py:555
  75.8 6.7 %collective-permute-start.14 = (bf16[4,128,128]{2,1,0:T(8,128)(2,1)S(1)}, bf16[4,128,128]{2,1,0:T(8,128)(2,1)S(1)}, u32[]{:S(2)}, u32[]{:S(2)}) collective-permute-start(bf16[4,128,128]{2,1,0:T(8,128)(2,1)S(1)} %get-tuple-element.41.y0), channel_id=1, source_target_pairs={{0,64},{32,96},{64,0},{96,32},{1,65},{33,97},{65,1},{97,33},{2,66}... | collective-permute-start | bytes 393224 | tf_op jit(solution)/shard_map/ppermute | solution.py:555
  78.8 3.8 %collective-permute-start.15 = (bf16[4,128,128]{2,1,0:T(8,128)(2,1)S(1)}, bf16[4,128,128]{2,1,0:T(8,128)(2,1)S(1)}, u32[]{:S(2)}, u32[]{:S(2)}) collective-permute-start(bf16[4,128,128]{2,1,0:T(8,128)(2,1)S(1)} %get-tuple-element.41.y0), channel_id=1, source_target_pairs={{0,96},{32,0},{64,32},{96,64},{1,97},{33,1},{65,33},{97,65},{2,98}... | collective-permute-start | bytes 393224 | tf_op jit(solution)/shard_map/ppermute | solution.py:555
  89.3 67.3 %copy-start.11 = (s32[1,32,128]{2,1,0:T(8,128)S(1)}, s32[1,32,128]{2,1,0:T(8,128)}, u32[]{:S(2)}) copy-start(s32[1,32,128]{2,1,0:T(8,128)} %param.14) | copy-start | bytes 49156
  89.3 67.3 %copy-start.13 = (s32[1,32]{1,0:T(1,128)S(1)}, s32[1,32]{1,0:T(1,128)}, u32[]{:S(2)}) copy-start(s32[1,32]{1,0:T(1,128)} %count_ref.3) | copy-start | bytes 388
  89.3 67.2 %all-to-all-start.1 = ((bf16[128,32,128]{2,1,0:T(8,128)(2,1)}), bf16[128,32,128]{2,1,0:T(8,128)(2,1)S(1)}, u32[]{:S(2)}, u32[]{:S(2)}) async-start(bf16[128,32,128]{2,1,0:T(8,128)(2,1)} %bitcast.6), calls=%async_computation.1 | async-start | bytes 2097152 | tf_op jit(solution)/shard_map/all_to_all | solution.py:585
  100.9 37.0 %collective-permute-start.16 = (bf16[512,256]{1,0:T(8,128)(2,1)S(1)}, bf16[512,256]{1,0:T(8,128)(2,1)S(1)}, u32[]{:S(2)}, u32[]{:S(2)}) collective-permute-start(bf16[512,256]{1,0:T(8,128)(2,1)S(1)} %get-tuple-element.50.o0), channel_id=1, source_target_pairs={{0,32},{32,64},{64,96},{96,0},{1,33},{33,65},{65,97},{97,1},{2,34}... | collective-permute-start | bytes 786440 | tf_op jit(solution)/shard_map/ppermute | solution.py:555
  102.3 20.4 %collective-permute-start.22 = (bf16[384,128]{1,0:T(8,128)(2,1)S(1)}, bf16[384,128]{1,0:T(8,128)(2,1)S(1)}, u32[]{:S(2)}, u32[]{:S(2)}) collective-permute-start(bf16[384,128]{1,0:T(8,128)(2,1)S(1)} %get-tuple-element.58), channel_id=1, source_target_pairs={{0,32},{32,64},{64,96},{96,0},{1,33},{33,65},{65,97},{97,1},{2,34}... | collective-permute-start | bytes 294920 | tf_op jit(solution)/shard_map/ppermute | solution.py:555
  103.5 21.4 %collective-permute-start.23 = (bf16[384,128]{1,0:T(8,128)(2,1)S(1)}, bf16[384,128]{1,0:T(8,128)(2,1)S(1)}, u32[]{:S(2)}, u32[]{:S(2)}) collective-permute-start(bf16[384,128]{1,0:T(8,128)(2,1)S(1)} %get-tuple-element.59), channel_id=1, source_target_pairs={{0,64},{32,96},{64,0},{96,32},{1,65},{33,97},{65,1},{97,33},{2,66}... | collective-permute-start | bytes 294920 | tf_op jit(solution)/shard_map/ppermute | solution.py:555
  105.1 19.9 %collective-permute-start.24 = (bf16[384,128]{1,0:T(8,128)(2,1)S(1)}, bf16[384,128]{1,0:T(8,128)(2,1)S(1)}, u32[]{:S(2)}, u32[]{:S(2)}) collective-permute-start(bf16[384,128]{1,0:T(8,128)(2,1)S(1)} %get-tuple-element.60), channel_id=1, source_target_pairs={{0,96},{32,0},{64,32},{96,64},{1,97},{33,1},{65,33},{97,65},{2,98}... | collective-permute-start | bytes 294920 | tf_op jit(solution)/shard_map/ppermute | solution.py:555
  125.0 5.5 %collective-permute-start.25 = (bf16[384,128]{1,0:T(8,128)(2,1)S(1)}, bf16[384,128]{1,0:T(8,128)(2,1)S(1)}, u32[]{:S(2)}, u32[]{:S(2)}) collective-permute-start(bf16[384,128]{1,0:T(8,128)(2,1)S(1)} %fold.3.refs_0_), channel_id=1, source_target_pairs={{0,2},{1,3},{2,4},{3,5},{4,6},{5,7},{6,0},{7,1},{8,10},{9,11},{10,... | collective-permute-start | bytes 294920 | tf_op jit(solution)/shard_map/ppermute | solution.py:573
  126.5 24.6 %collective-permute-start.17 = (bf16[512,256]{1,0:T(8,128)(2,1)S(1)}, bf16[512,256]{1,0:T(8,128)(2,1)S(1)}, u32[]{:S(2)}, u32[]{:S(2)}) collective-permute-start(bf16[512,256]{1,0:T(8,128)(2,1)S(1)} %get-tuple-element.50.o0), channel_id=1, source_target_pairs={{0,64},{32,96},{64,0},{96,32},{1,65},{33,97},{65,1},{97,33},{2,66}... | collective-permute-start | bytes 786440 | tf_op jit(solution)/shard_map/ppermute | solution.py:555
  126.6 6.9 %collective-permute-start.26 = (bf16[384,128]{1,0:T(8,128)(2,1)S(1)}, bf16[384,128]{1,0:T(8,128)(2,1)S(1)}, u32[]{:S(2)}, u32[]{:S(2)}) collective-permute-start(bf16[384,128]{1,0:T(8,128)(2,1)S(1)} %fold.3.refs_0_), channel_id=1, source_target_pairs={{0,4},{1,5},{2,6},{3,7},{4,0},{5,1},{6,2},{7,3},{8,12},{9,13},{10,... | collective-permute-start | bytes 294920 | tf_op jit(solution)/shard_map/ppermute | solution.py:573
  129.6 4.5 %collective-permute-start.27 = (bf16[384,128]{1,0:T(8,128)(2,1)S(1)}, bf16[384,128]{1,0:T(8,128)(2,1)S(1)}, u32[]{:S(2)}, u32[]{:S(2)}) collective-permute-start(bf16[384,128]{1,0:T(8,128)(2,1)S(1)} %fold.3.refs_0_), channel_id=1, source_target_pairs={{0,6},{1,7},{2,0},{3,1},{4,2},{5,3},{6,4},{7,5},{8,14},{9,15},{10,... | collective-permute-start | bytes 294920 | tf_op jit(solution)/shard_map/ppermute | solution.py:573
  130.5 24.4 %collective-permute-start.18 = (bf16[512,256]{1,0:T(8,128)(2,1)S(1)}, bf16[512,256]{1,0:T(8,128)(2,1)S(1)}, u32[]{:S(2)}, u32[]{:S(2)}) collective-permute-start(bf16[512,256]{1,0:T(8,128)(2,1)S(1)} %get-tuple-element.50.o0), channel_id=1, source_target_pairs={{0,96},{32,0},{64,32},{96,64},{1,97},{33,1},{65,33},{97,65},{2,98}... | collective-permute-start | bytes 786440 | tf_op jit(solution)/shard_map/ppermute | solution.py:555
  134.2 12.1 %collective-permute-start.28 = (bf16[384,128]{1,0:T(8,128)(2,1)S(1)}, bf16[384,128]{1,0:T(8,128)(2,1)S(1)}, u32[]{:S(2)}, u32[]{:S(2)}) collective-permute-start(bf16[384,128]{1,0:T(8,128)(2,1)S(1)} %fold.4.refs_0_), channel_id=1, source_target_pairs={{0,8},{1,9},{2,10},{3,11},{4,12},{5,13},{6,14},{7,15},{8,16},{9,17... | collective-permute-start | bytes 294920 | tf_op jit(solution)/shard_map/ppermute | solution.py:572
  135.4 11.0 %collective-permute-start.29 = (bf16[384,128]{1,0:T(8,128)(2,1)S(1)}, bf16[384,128]{1,0:T(8,128)(2,1)S(1)}, u32[]{:S(2)}, u32[]{:S(2)}) collective-permute-start(bf16[384,128]{1,0:T(8,128)(2,1)S(1)} %fold.4.refs_0_), channel_id=1, source_target_pairs={{0,16},{1,17},{2,18},{3,19},{4,20},{5,21},{6,22},{7,23},{8,24},{9,... | collective-permute-start | bytes 294920 | tf_op jit(solution)/shard_map/ppermute | solution.py:572
  137.8 11.2 %collective-permute-start.30 = (bf16[384,128]{1,0:T(8,128)(2,1)S(1)}, bf16[384,128]{1,0:T(8,128)(2,1)S(1)}, u32[]{:S(2)}, u32[]{:S(2)}) collective-permute-start(bf16[384,128]{1,0:T(8,128)(2,1)S(1)} %fold.4.refs_0_), channel_id=1, source_target_pairs={{0,24},{1,25},{2,26},{3,27},{4,28},{5,29},{6,30},{7,31},{8,0},{9,1... | collective-permute-start | bytes 294920 | tf_op jit(solution)/shard_map/ppermute | solution.py:572
  146.3 10.2 %collective-permute-start.19 = (bf16[16,32,128]{2,1,0:T(8,128)(2,1)S(1)}, bf16[16,32,128]{2,1,0:T(8,128)(2,1)S(1)}, u32[]{:S(2)}, u32[]{:S(2)}) collective-permute-start(bf16[16,32,128]{2,1,0:T(8,128)(2,1)S(1)} %get-tuple-element.54), channel_id=1, source_target_pairs={{0,32},{32,64},{64,96},{96,0},{1,33},{33,65},{65,97},{97,1},{2,34}... | collective-permute-start | bytes 393224 | tf_op jit(solution)/shard_map/ppermute | solution.py:555
  146.4 10.1 %collective-permute-start.20 = (bf16[16,32,128]{2,1,0:T(8,128)(2,1)S(1)}, bf16[16,32,128]{2,1,0:T(8,128)(2,1)S(1)}, u32[]{:S(2)}, u32[]{:S(2)}) collective-permute-start(bf16[16,32,128]{2,1,0:T(8,128)(2,1)S(1)} %get-tuple-element.55), channel_id=1, source_target_pairs={{0,64},{32,96},{64,0},{96,32},{1,65},{33,97},{65,1},{97,33},{2,66}... | collective-permute-start | bytes 393224 | tf_op jit(solution)/shard_map/ppermute | solution.py:555
  149.0 7.5 %collective-permute-start.21 = (bf16[16,32,128]{2,1,0:T(8,128)(2,1)S(1)}, bf16[16,32,128]{2,1,0:T(8,128)(2,1)S(1)}, u32[]{:S(2)}, u32[]{:S(2)}) collective-permute-start(bf16[16,32,128]{2,1,0:T(8,128)(2,1)S(1)} %get-tuple-element.56), channel_id=1, source_target_pairs={{0,96},{32,0},{64,32},{96,64},{1,97},{33,1},{65,33},{97,65},{2,98}... | collective-permute-start | bytes 393224 | tf_op jit(solution)/shard_map/ppermute | solution.py:555
  151.1 5.5 %collective-permute-start.31 = (bf16[384,128]{1,0:T(8,128)(2,1)S(1)}, bf16[384,128]{1,0:T(8,128)(2,1)S(1)}, u32[]{:S(2)}, u32[]{:S(2)}) collective-permute-start(bf16[384,128]{1,0:T(8,128)(2,1)S(1)} %fold.5.f0), channel_id=1, source_target_pairs={{0,1},{1,0},{2,3},{3,2},{4,5},{5,4},{6,7},{7,6},{8,9},{9,8},{10,11... | collective-permute-start | bytes 294920 | tf_op jit(solution)/shard_map/ppermute | solution.py:577
  159.6 8.7 %collective-permute-start.32 = (bf16[640,128]{1,0:T(8,128)(2,1)S(1)}, bf16[640,128]{1,0:T(8,128)(2,1)S(1)}, u32[]{:S(2)}, u32[]{:S(2)}) collective-permute-start(bf16[640,128]{1,0:T(8,128)(2,1)S(1)} %scatter_rows.1.m0), channel_id=1, source_target_pairs={{0,32},{32,64},{64,96},{96,0},{1,33},{33,65},{65,97},{97,1},{2,34}... | collective-permute-start | bytes 491528 | tf_op jit(solution)/shard_map/ppermute | solution.py:555
  159.7 8.6 %collective-permute-start.33 = (bf16[640,128]{1,0:T(8,128)(2,1)S(1)}, bf16[640,128]{1,0:T(8,128)(2,1)S(1)}, u32[]{:S(2)}, u32[]{:S(2)}) collective-permute-start(bf16[640,128]{1,0:T(8,128)(2,1)S(1)} %scatter_rows.1.m0), channel_id=1, source_target_pairs={{0,64},{32,96},{64,0},{96,32},{1,65},{33,97},{65,1},{97,33},{2,66}... | collective-permute-start | bytes 491528 | tf_op jit(solution)/shard_map/ppermute | solution.py:555
  160.6 8.6 %collective-permute-start.34 = (bf16[640,128]{1,0:T(8,128)(2,1)S(1)}, bf16[640,128]{1,0:T(8,128)(2,1)S(1)}, u32[]{:S(2)}, u32[]{:S(2)}) collective-permute-start(bf16[640,128]{1,0:T(8,128)(2,1)S(1)} %scatter_rows.1.m0), channel_id=1, source_target_pairs={{0,96},{32,0},{64,32},{96,64},{1,97},{33,1},{65,33},{97,65},{2,98}... | collective-permute-start | bytes 491528 | tf_op jit(solution)/shard_map/ppermute | solution.py:555
  (5 other events, 8.2 us)

commit v3 on v2

v3 whole, which is shorter than its diff:
```python
import functools
import math

import jax
import jax.numpy as jnp
from jax import lax
from jax.experimental import pallas as pl
from jax.experimental.pallas import tpu as pltpu
from jax.sharding import PartitionSpec as P

F32 = jnp.float32
BF16 = jnp.bfloat16
BLK = 128
N_REP = 4
N_DOM = 32
FIN = 128
HID = 256
ROWS = 2048
LOCAL = ROWS // BLK
HUBS = 8
BLOCKS = LOCAL + N_DOM + HUBS
TILES = 384
REMOTE = N_DOM
CHUNK = 32
FWD_SLOTS = 640
BWD_SLOTS = 512
QUARTER = ROWS // N_REP
QB = LOCAL // N_REP
FQ = FIN // N_REP
MSG = FQ + 16
HUB_ROWS = HUBS * BLK // N_DOM
LO = 256
VMEM_LIMIT = 24 * 1024 * 1024

VM = pl.BlockSpec(memory_space=pltpu.VMEM)
SM = pl.BlockSpec(memory_space=pltpu.SMEM)
FAR = pl.BlockSpec(memory_space=pltpu.HBM)
PARAMS = pltpu.CompilerParams(vmem_limit_bytes=VMEM_LIMIT)
TILE_PARAMS = PARAMS


def in_hbm(x):
    return pltpu.with_memory_space_constraint(x, pltpu.HBM)


def dot(a, b):
    return jnp.dot(a, b, preferred_element_type=F32)


def halves(x):
    high = x.astype(BF16)
    return high, (x - high.astype(F32)).astype(BF16)


def column(row):
    return jnp.broadcast_to(row, (BLK, BLK)).T


def low_onehot(col):
    low = jnp.where(col < 0, -1, col & (LO - 1))
    lane = lax.broadcasted_iota(jnp.int32, (BLK, BLK), 1)
    return jnp.concatenate(
        [jnp.where(low == lane + k * BLK, 1.0, 0.0) for k in range(LO // BLK)], axis=1
    ).astype(BF16)


def sort_tiles(bucket, operand, empty, edges, out_of, slots):
    sub = lax.broadcasted_iota(jnp.int32, (BLK, BLK), 0)
    lane = lax.broadcasted_iota(jnp.int32, (BLK, BLK), 1)
    line = lane[:1]
    parts = len(bucket)
    cols = [column(b) for b in bucket]
    hots = [jnp.where(c == lane, 1.0, 0.0) for c in cols]
    counts = sum(jnp.sum(h, axis=0, keepdims=True) for h in hots).astype(jnp.int32)
    padded = (counts + 1) & -2
    before = jnp.where(sub < lane, column(padded).astype(F32), 0.0)
    starts = jnp.sum(before, axis=0, keepdims=True).astype(jnp.int32)
    first = jnp.zeros((1, BLK), jnp.int32)
    low = 0
    for n, high in enumerate(edges):
        inside = (line >= low) & (line < high)
        size = jnp.sum(jnp.where(inside, padded, 0).astype(F32), axis=1, keepdims=True).astype(jnp.int32)
        gap = ((size + CHUNK - 1) & -CHUNK) - size
        starts = starts + jnp.where(line >= high, gap, 0)
        total = (size + CHUNK - 1) // CHUNK
        first = first + jnp.where(line > n, total, 0)
        low = high
    begin, end = column(starts), column(starts + padded)
    places = []
    for i in range(parts):
        rank = jnp.sum(jnp.where(hots[i] > 0.0, starts.astype(F32), 0.0), axis=1, keepdims=True)
        for j in range(i + 1):
            same = jnp.broadcast_to(bucket[j], (BLK, BLK)) == cols[i]
            if j == i:
                same = same & (lane < sub)
            rank = rank + jnp.sum(jnp.where(same, 1.0, 0.0), axis=1, keepdims=True)
        places.append(jnp.broadcast_to(rank.astype(jnp.int32), (BLK, BLK)))
    shifted = [column(o - empty).astype(F32) for o in operand]
    tiles, blocks, outs = [], [], []
    for s in range(slots // BLK):
        here = lane + s * BLK
        tile = jnp.zeros((1, BLK), F32)
        block = jnp.zeros((1, BLK), F32)
        for i in range(parts):
            hit = places[i] == here
            tile = tile + jnp.sum(jnp.where(hit, (sub + i * BLK).astype(F32), 0.0), axis=0, keepdims=True)
            block = block + jnp.sum(jnp.where(hit, shifted[i], 0.0), axis=0, keepdims=True)
        inside = (begin <= here) & (here < end)
        out = jnp.sum(jnp.where(inside, out_of(sub).astype(F32), 0.0), axis=0, keepdims=True)
        tiles.append(tile.astype(jnp.int32))
        blocks.append(block.astype(jnp.int32) + empty)
        outs.append(out.astype(jnp.int32))
    return tiles, blocks, outs, first


def order_kernel(dst_ref, src_ref, fwd_ref, bwd_ref):
    parts = TILES // BLK
    dst = [dst_ref[pl.ds(i, 1), :] for i in range(parts)]
    src = [src_ref[pl.ds(i, 1), :] for i in range(parts)]
    hub = LOCAL + REMOTE
    bucket = [d + jnp.where(s < LOCAL, 0, jnp.where(s < hub, LOCAL, 2 * LOCAL)) for d, s in zip(dst, src)]
    operand = [s - jnp.where(s < LOCAL, 0, jnp.where(s < hub, LOCAL, hub)) for s in src]
    edges = (LOCAL, 2 * LOCAL, 3 * LOCAL)
    found = sort_tiles(bucket, operand, REMOTE, edges, lambda b: b & (LOCAL - 1), FWD_SLOTS)
    for n, rows in enumerate(found[:3]):
        for s, row in enumerate(rows):
            fwd_ref[n, pl.ds(s, 1), :] = row
    fwd_ref[3, pl.ds(0, 1), :] = found[3]
    far = REMOTE + HUBS
    bucket = [jnp.where(s < LOCAL, s + far, s - LOCAL) for s in src]
    found = sort_tiles(
        bucket, dst, LOCAL, (far, far + LOCAL), lambda b: jnp.where(b < far, b, b - far), BWD_SLOTS
    )
    for n, rows in enumerate(found[:3]):
        for s, row in enumerate(rows):
            bwd_ref[n, pl.ds(s, 1), :] = row
    bwd_ref[3, pl.ds(0, 1), :] = found[3]


def order_tiles(dst, src):
    return pl.pallas_call(
        order_kernel,
        out_shape=[
            jax.ShapeDtypeStruct((4, FWD_SLOTS // BLK, BLK), jnp.int32),
            jax.ShapeDtypeStruct((4, BWD_SLOTS // BLK, BLK), jnp.int32),
        ],
        in_specs=[VM, VM],
        out_specs=[VM, VM],
        compiler_params=PARAMS,
        name="order_tiles",
    )(dst, src)


AHEAD = 3


def keep(tiles, buckets):
    chunks = -(-(tiles + buckets) // CHUNK)
    return [pltpu.VMEM((chunks * CHUNK, BLK, BLK), BF16), pltpu.SemaphoreType.DMA((chunks,))]


def extent(plan_ref, number):
    begin = plan_ref[3, 0, number]
    return begin, plan_ref[3, 0, number + 1] - begin


def where(i):
    return i // (BLK // CHUNK), lax.rem(i, BLK // CHUNK) * CHUNK


def fetch(plan_ref, number, c, w_ref, held, sems):
    row, col = where(extent(plan_ref, number)[0] + c)
    for k in range(CHUNK):
        tile = plan_ref[0, row, col + k]
        pltpu.make_async_copy(w_ref.at[tile], held.at[c * CHUNK + k], sems.at[c]).start()


def fetch_first(plan_ref, number, w_ref, held, sems):
    def first(c, carry):
        fetch(plan_ref, number, c, w_ref, held, sems)
        return carry

    lax.fori_loop(0, jnp.minimum(extent(plan_ref, number)[1], AHEAD), first, 0)


def run_class(plan_ref, number, w_ref, held, sems, product, acc):
    begin, count = extent(plan_ref, number)

    def chunk(c, carry):
        row, col = where(begin + c)
        if held is not None:
            slots = held.at[pl.ds(c * CHUNK, CHUNK)]
            pltpu.make_async_copy(w_ref.at[pl.ds(0, CHUNK)], slots, sems.at[c]).wait()

            @pl.when(c + AHEAD < count)
            def _():
                fetch(plan_ref, number, c + AHEAD, w_ref, held, sems)

        found = []
        for k in range(0, CHUNK, 2):
            pair = []
            for j in (k, k + 1):
                tile = w_ref[plan_ref[0, row, col + j]] if held is None else held[c * CHUNK + j]
                pair.append((tile, plan_ref[1, row, col + j]))
            one, two = pair
            found.append((plan_ref[2, row, col + k], product(one, two)))
        for d, value in found:
            acc[d] += value
        return carry

    lax.fori_loop(0, count, chunk, 0)


PEERS = 4


def gather_kernel(rows_hbm, count_ref, hub_ref, feat_hbm, out_ref, rows_ref, feat_ref, sems):
    loads = [
        pltpu.make_async_copy(feat_hbm, feat_ref, sems.at[0]),
        pltpu.make_async_copy(rows_hbm, rows_ref, sems.at[1]),
    ]
    for load in loads:
        load.start()
    for load in loads:
        load.wait()
    slot = lax.broadcasted_iota(jnp.int32, (1, BLK), 1)

    def step(i, carry):
        cols = []
        for j in range(PEERS):
            p = PEERS * i + j
            row = jnp.where(slot < count_ref[0, p], rows_ref[pl.ds(p, 1), :], -1)
            cols.append(column(row))
        hot = jnp.concatenate([low_onehot(c) for c in cols], axis=0)
        high = lax.shift_right_arithmetic(jnp.concatenate(cols, axis=0), 8)
        total = jnp.zeros((PEERS * BLK, FIN), F32)
        for pair in range(ROWS // LO // 2):
            left = feat_ref[pl.ds(2 * pair * LO, LO), :]
            right = feat_ref[pl.ds((2 * pair + 1) * LO, LO), :]
            got = dot(hot, jnp.concatenate([left, right], axis=1))
            total = jnp.where(high == 2 * pair, got[:, :FIN], total)
            total = jnp.where(high == 2 * pair + 1, got[:, FIN:], total)
        out_ref[pl.ds(PEERS * i, PEERS), pl.ds(0, BLK), :] = total.astype(BF16).reshape(PEERS, BLK, FIN)
        return carry

    lax.fori_loop(0, N_DOM // PEERS, step, 0)
    per_hub = BLK // HUB_ROWS
    for p in range(N_DOM):
        first = (hub_ref[p // per_hub] & (LOCAL - 1)) * BLK + (p % per_hub) * HUB_ROWS
        first = pl.multiple_of(first, HUB_ROWS)
        out_ref[p, pl.ds(BLK, HUB_ROWS), :] = feat_ref[pl.ds(first, HUB_ROWS), :]


def gather_rows(rows, counts, hubs, features):
    return pl.pallas_call(
        gather_kernel,
        out_shape=jax.ShapeDtypeStruct((N_DOM, BLK + HUB_ROWS, FIN), BF16),
        in_specs=[FAR, SM, SM, FAR],
        out_specs=VM,
        scratch_shapes=[
            pltpu.VMEM((N_DOM, BLK), jnp.int32),
            pltpu.VMEM((ROWS, FIN), BF16),
            pltpu.SemaphoreType.DMA((2,)),
        ],
        compiler_params=PARAMS,
        cost_estimate=pl.CostEstimate(flops=4 * 10**9, bytes_accessed=2 * 10**6, transcendentals=0),
        name="gather_rows",
    )(in_hbm(rows), counts, hubs, in_hbm(features))


def piece_kernel(place_ref, hub_ref, recv_ref, out_ref):
    owner = lax.shift_right_logical(hub_ref[place_ref[1] // (BLK // HUB_ROWS)], 4)
    piece = recv_ref[owner, pl.ds(BLK, HUB_ROWS), :]
    for p in range(N_DOM):
        out_ref[p] = piece


def hub_piece(place, hubs, received):
    return pl.pallas_call(
        piece_kernel,
        out_shape=jax.ShapeDtypeStruct((N_DOM, HUB_ROWS, FIN), BF16),
        in_specs=[SM, SM, VM],
        out_specs=VM,
        compiler_params=PARAMS,
        name="hub_piece",
    )(place, hubs, received)


def forward_product(xs):
    def product(one, two):
        left = jnp.concatenate([one[0], two[0]], axis=1)
        return dot(left, jnp.concatenate([xs[one[1]], xs[two[1]]], axis=0))

    return product


def forward_near_kernel(plan_ref, feat_ref, w_ref, acc_ref, xs, held, sems):
    fetch_first(plan_ref, 0, w_ref, held, sems)
    xs[pl.ds(0, LOCAL)] = feat_ref[...]
    xs[REMOTE] = jnp.zeros((BLK, FIN), BF16)
    acc_ref[...] = jnp.zeros_like(acc_ref)
    run_class(plan_ref, 0, w_ref, held, sems, forward_product(xs), acc_ref)


def forward_remote_kernel(plan_ref, near_ref, recv_ref, w_ref, acc_ref, xs, held, sems):
    fetch_first(plan_ref, 1, w_ref, held, sems)
    xs[pl.ds(0, REMOTE)] = recv_ref[:, pl.ds(0, BLK), :]
    xs[REMOTE] = jnp.zeros((BLK, FIN), BF16)
    acc_ref[...] = near_ref[...]
    run_class(plan_ref, 1, w_ref, held, sems, forward_product(xs), acc_ref)


def forward_hub_kernel(plan_ref, place_ref, far_ref, hub_ref, w_ref, own_ref, s1, s2, s3, xs, acc, held, sems):
    fetch_first(plan_ref, 2, w_ref, held, sems)
    xs[pl.ds(0, HUBS)] = hub_ref[...]
    xs[REMOTE] = jnp.zeros((BLK, FIN), BF16)
    acc[...] = far_ref[...]
    run_class(plan_ref, 2, w_ref, held, sems, forward_product(xs), acc)
    rep = place_ref[0]
    own_ref[...] = acc[pl.ds(rep * QB, QB)]
    for k, ref in ((1, s1), (2, s2), (3, s3)):
        ref[...] = acc[pl.ds(lax.rem(rep + k, N_REP) * QB, QB)].astype(BF16)


FORWARD_XS = pltpu.VMEM((REMOTE + 1, BLK, FIN), BF16)


def forward_near(plan, features, weights):
    return pl.pallas_call(
        forward_near_kernel,
        out_shape=jax.ShapeDtypeStruct((LOCAL, BLK, FIN), F32),
        in_specs=[SM, VM, FAR],
        out_specs=VM,
        scratch_shapes=[FORWARD_XS] + keep(LOCAL * LOCAL, LOCAL),
        compiler_params=TILE_PARAMS,
        cost_estimate=pl.CostEstimate(flops=10**9, bytes_accessed=4 * 10**6, transcendentals=0),
        name="forward_near",
    )(plan, features, weights)


def forward_remote(plan, near, received, weights):
    return pl.pallas_call(
        forward_remote_kernel,
        out_shape=jax.ShapeDtypeStruct((LOCAL, BLK, FIN), F32),
        in_specs=[SM, VM, VM, FAR],
        out_specs=VM,
        scratch_shapes=[FORWARD_XS] + keep(TILES, LOCAL),
        compiler_params=TILE_PARAMS,
        cost_estimate=pl.CostEstimate(flops=4 * 10**9, bytes_accessed=9 * 10**6, transcendentals=0),
        name="forward_remote",
    )(plan, near, received, weights)


def forward_hub(plan, place, far, hubs, weights):
    quarter = (QB, BLK, FIN)
    return pl.pallas_call(
        forward_hub_kernel,
        out_shape=[jax.ShapeDtypeStruct(quarter, F32)] + [jax.ShapeDtypeStruct(quarter, BF16)] * 3,
        in_specs=[SM, SM, VM, VM, FAR],
        out_specs=[VM] * 4,
        scratch_shapes=[FORWARD_XS, pltpu.VMEM((LOCAL, BLK, FIN), F32)] + keep(LOCAL * HUBS, LOCAL),
        compiler_params=TILE_PARAMS,
        cost_estimate=pl.CostEstimate(flops=10**9, bytes_accessed=3 * 10**6, transcendentals=0),
        name="forward_hub",
    )(plan, place, far, hubs, weights)


def middle_kernel(own_ref, a_ref, b_ref, c_ref, w_ref, bias_ref, cot_ref, out_ref, y_ref, gw_ref):
    zx = (own_ref[...] + a_ref[...].astype(F32)) + (b_ref[...].astype(F32) + c_ref[...].astype(F32))
    zx = zx.reshape(QUARTER, FIN)
    weight = w_ref[...]
    zh, zl = halves(zx)
    pre = dot(zh, weight) + dot(zl, weight) + bias_ref[...]
    root = math.sqrt(2.0 / math.pi)
    square = pre * pre
    bent = jnp.tanh(root * (pre + 0.044715 * (square * pre)))
    cdf = 0.5 * (1.0 + bent)
    out_ref[...] = (pre * cdf).astype(BF16)
    slope = cdf + (0.5 * pre) * ((1.0 - bent * bent) * (root * (1.0 + (3 * 0.044715) * square)))
    pre_grad = (cot_ref[...].astype(F32) * slope).astype(BF16)
    yt = lax.dot_general(weight, pre_grad, (((1,), (1,)), ((), ())), preferred_element_type=F32)
    yt = yt.astype(BF16)
    for k in range(QB):
        y_ref[k] = yt[:, k * BLK : (k + 1) * BLK]
    th, tl = halves(zx.T)
    gw = dot(th, pre_grad) + dot(tl, pre_grad)
    for part, piece in enumerate(halves(gw)):
        for c in range(16):
            g, side = c // 2, c % 2
            gw_ref[part * 16 + c] = piece[g * 16 : (g + 1) * 16, side * BLK : (side + 1) * BLK]


def middle(rep, own, a, b, c, weight, bias, cotangent):
    whole = lambda shape: pl.BlockSpec(shape, lambda i, rep_ref: (0,) * len(shape))
    quarter = (QB, BLK, FIN)
    return pl.pallas_call(
        lambda rep_ref, *refs: middle_kernel(*refs),
        grid_spec=pltpu.PrefetchScalarGridSpec(
            num_scalar_prefetch=1,
            grid=(1,),
            in_specs=[whole(quarter)] * 4
            + [
                whole((FIN, HID)),
                whole((1, HID)),
                pl.BlockSpec((QUARTER, HID), lambda i, rep_ref: (rep_ref[0], 0)),
            ],
            out_specs=[whole((QUARTER, HID)), whole((QB, FIN, BLK)), whole((32, 16, BLK))],
        ),
        out_shape=[
            jax.ShapeDtypeStruct((QUARTER, HID), BF16),
            jax.ShapeDtypeStruct((QB, FIN, BLK), BF16),
            jax.ShapeDtypeStruct((32, 16, BLK), BF16),
        ],
        compiler_params=PARAMS,
        cost_estimate=pl.CostEstimate(flops=2 * 10**10, bytes_accessed=2 * 10**6, transcendentals=0),
        name="middle",
    )(rep, own, a, b, c, weight, bias, cotangent)


def hold_kernel(w_ref, after_ref, held_ref, sem):
    del after_ref
    copy = pltpu.make_async_copy(w_ref, held_ref, sem)
    copy.start()
    copy.wait()


def hold_tiles(weights, after):
    return pl.pallas_call(
        hold_kernel,
        out_shape=pltpu.VMEM((TILES, BLK, BLK), BF16),
        in_specs=[FAR, pl.BlockSpec(memory_space=pl.ANY)],
        out_specs=VM,
        scratch_shapes=[pltpu.SemaphoreType.DMA],
        compiler_params=PARAMS,
        cost_estimate=pl.CostEstimate(flops=0, bytes_accessed=13 * 10**6, transcendentals=0),
        name="hold_tiles",
    )(weights, after)


def backward_product(ys):
    def product(one, two):
        left = jnp.concatenate([ys[one[1]], ys[two[1]]], axis=1)
        return dot(left, jnp.concatenate([one[0], two[0]], axis=0))

    return product


def load_ys(rep, refs, ys):
    for k, ref in enumerate(refs):
        ys[pl.ds(lax.rem(rep + N_REP - k, N_REP) * QB, QB)] = ref[...]
    ys[LOCAL] = jnp.zeros((FIN, BLK), BF16)


def backward_far_kernel(
    plan_ref, rep_ref, y0, y1, y2, y3, gw_ref, w_ref, msg_ref, ys, acc
):
    load_ys(rep_ref[0], (y0, y1, y2, y3), ys)
    acc[...] = jnp.zeros_like(acc)
    run_class(plan_ref, 0, w_ref, None, None, backward_product(ys), acc)
    for q in range(N_REP):
        msg_ref[q, :, pl.ds(0, FQ), :] = acc[pl.ds(0, REMOTE), pl.ds(q * FQ, FQ), :].astype(BF16)
        for m in range(16):
            piece = acc[REMOTE + m // 2, pl.ds(q * FQ + (m % 2) * 16, 16), :]
            msg_ref[q, 2 * m, pl.ds(FQ, 16), :] = piece.astype(BF16)
            if m < 8:
                msg_ref[q, 2 * m + 1, pl.ds(FQ, 16), :] = gw_ref[q * 8 + m]
            else:
                msg_ref[q, 2 * m + 1, pl.ds(FQ, 16), :] = jnp.zeros((16, BLK), BF16)


def backward_far(plan, rep, ys, gw, weights):
    return pl.pallas_call(
        backward_far_kernel,
        out_shape=jax.ShapeDtypeStruct((N_REP, N_DOM, MSG, BLK), BF16),
        in_specs=[SM, SM] + [VM] * 6,
        out_specs=VM,
        scratch_shapes=[
            pltpu.VMEM((LOCAL + 1, FIN, BLK), BF16),
            pltpu.VMEM((REMOTE + HUBS, FIN, BLK), F32),
        ],
        compiler_params=TILE_PARAMS,
        cost_estimate=pl.CostEstimate(flops=4 * 10**9, bytes_accessed=14 * 10**6, transcendentals=0),
        name="backward_far",
    )(plan, rep, *ys, gw, weights)


def backward_near_kernel(
    plan_ref, rep_ref, y0, y1, y2, y3, w_ref, own_ref, s1, s2, s3, ys, acc, held, sems
):
    fetch_first(plan_ref, 1, w_ref, held, sems)
    rep = rep_ref[0]
    load_ys(rep, (y0, y1, y2, y3), ys)
    acc[...] = jnp.zeros_like(acc)
    run_class(plan_ref, 1, w_ref, held, sems, backward_product(ys), acc)

    def rows_of(k):
        start = pl.multiple_of(lax.rem(rep + k, N_REP) * FQ, FQ)
        return acc[:, pl.ds(start, FQ), :]

    own_ref[...] = rows_of(0)
    for k, ref in ((1, s1), (2, s2), (3, s3)):
        ref[...] = rows_of(k).astype(BF16)


def backward_near(plan, rep, ys, weights):
    part = (LOCAL, FQ, BLK)
    return pl.pallas_call(
        backward_near_kernel,
        out_shape=[jax.ShapeDtypeStruct(part, F32)] + [jax.ShapeDtypeStruct(part, BF16)] * 3,
        in_specs=[SM, SM] + [VM] * 4 + [FAR],
        out_specs=[VM] * 4,
        scratch_shapes=[
            pltpu.VMEM((LOCAL + 1, FIN, BLK), BF16),
            pltpu.VMEM((LOCAL, FIN, BLK), F32),
        ]
        + keep(LOCAL * LOCAL, LOCAL),
        compiler_params=TILE_PARAMS,
        cost_estimate=pl.CostEstimate(flops=10**9, bytes_accessed=14 * 10**6, transcendentals=0),
        name="backward_near",
    )(plan, rep, *ys, weights)


SCATTER_PEERS = 8


def scatter_kernel(count_ref, rows_ref, recv_ref, own_ref, a_ref, b_ref, c_ref, out_ref, acc):
    chunks = ROWS // LO
    slot = lax.broadcasted_iota(jnp.int32, (1, BLK), 1)
    acc[...] = jnp.zeros_like(acc)

    def step(i, carry):
        hots, sides = [], []
        for j in range(SCATTER_PEERS):
            p = SCATTER_PEERS * i + j
            row = jnp.where(slot < count_ref[0, p], rows_ref[pl.ds(p, 1), :], -1)
            hots.append(low_onehot(column(row)))
            total = recv_ref[p, pl.ds(0, FQ), :].astype(F32)
            for r in range(1, N_REP):
                total = total + recv_ref[r * N_DOM + p, pl.ds(0, FQ), :].astype(F32)
            high = lax.shift_right_arithmetic(row, 8)
            pieces = [halves(jnp.where(high == c, total, 0.0)) for c in range(chunks)]
            sides.append(jnp.concatenate([h for h, _ in pieces] + [l for _, l in pieces], axis=0))
        acc[...] += dot(jnp.concatenate(sides, axis=1), jnp.concatenate(hots, axis=0))
        return carry

    lax.fori_loop(0, N_DOM // SCATTER_PEERS, step, 0)
    for b in range(LOCAL):
        c, side = b // 2, b % 2
        lanes = pl.ds(side * BLK, BLK)
        here = acc[pl.ds(c * FQ, FQ), lanes] + acc[pl.ds((chunks + c) * FQ, FQ), lanes]
        near = own_ref[b] + a_ref[b].astype(F32) + b_ref[b].astype(F32) + c_ref[b].astype(F32)
        out_ref[b] = (here + near).astype(BF16)


def scatter_rows(counts, rows, received, own, a, b, c):
    return pl.pallas_call(
        scatter_kernel,
        out_shape=jax.ShapeDtypeStruct((LOCAL, FQ, BLK), BF16),
        in_specs=[SM] + [VM] * 6,
        out_specs=VM,
        scratch_shapes=[pltpu.VMEM((2 * FIN * 2, LO), F32)],
        compiler_params=PARAMS,
        cost_estimate=pl.CostEstimate(flops=4 * 10**9, bytes_accessed=4 * 10**6, transcendentals=0),
        name="scatter_rows",
    )(counts, rows, received, own, a, b, c)


def final_kernel(place_ref, hub_ref, m0, m1, m2, m3, shared_ref, gx_ref, gw_ref, blocks, *, scale):
    rep = place_ref[0]
    for k, ref in enumerate((m0, m1, m2, m3)):
        start = pl.multiple_of(lax.rem(rep + N_REP - k, N_REP) * FQ, FQ)
        blocks[:, pl.ds(start, FQ), :] = ref[...].astype(F32)
    for h in range(HUBS):
        block = hub_ref[h]

        @pl.when(lax.shift_right_logical(block, 4) == place_ref[1])
        def _():
            for q in range(N_REP):
                for k in range(2):
                    piece = shared_ref[q * N_DOM + 4 * h + 2 * k].astype(F32)
                    blocks[block & (LOCAL - 1), pl.ds(q * FQ + k * 16, 16), :] += piece

    for b in range(LOCAL):
        gx_ref[pl.ds(b * BLK, BLK), :] = blocks[b].T
    for c in range(16):
        g, side = c // 2, c % 2
        high, low = [shared_ref[(n // 8) * N_DOM + 2 * (n % 8) + 1].astype(F32) for n in (c, 16 + c)]
        gw_ref[pl.ds(g * 16, 16), pl.ds(side * BLK, BLK)] = (high + low) * scale


def finish(place, hubs, parts, shared, scale):
    return pl.pallas_call(
        functools.partial(final_kernel, scale=scale),
        out_shape=[
            jax.ShapeDtypeStruct((ROWS, FIN), F32),
            jax.ShapeDtypeStruct((FIN, HID), F32),
        ],
        in_specs=[SM, SM] + [VM] * 5,
        out_specs=[VM] * 2,
        scratch_shapes=[pltpu.VMEM((LOCAL, FIN, BLK), F32)],
        compiler_params=PARAMS,
        name="finish",
    )(place, hubs, *parts, shared)


def place_kernel(act_ref, out_ref):
    out_ref[...] = act_ref[...]


def place_output(output):
    return pl.pallas_call(
        place_kernel,
        out_shape=jax.ShapeDtypeStruct(output.shape, output.dtype),
        in_specs=[VM],
        out_specs=VM,
        compiler_params=PARAMS,
        name="place_output",
    )(output)


def turn(value, k):
    return lax.ppermute(value, "rep", [(i, (i + k) % N_REP) for i in range(N_REP)])


def around(value):
    return [value] + [turn(value, k) for k in (1, 2, 3)]


def swap(value, axes):
    return lax.all_to_all(value, axes, split_axis=0, concat_axis=0, tiled=True)


def shards(
    features,
    proj_weight,
    bias,
    cotangent,
    send_rows,
    send_count,
    hub_blocks,
    tile_dst,
    tile_src,
    tile_weight,
):
    rep = lax.axis_index("rep").astype(jnp.int32)
    dom = lax.axis_index("dom").astype(jnp.int32)
    place = jnp.stack([rep, dom])
    hub_blocks, send_count = in_hbm(hub_blocks), in_hbm(send_count)
    blocks = features.reshape(LOCAL, BLK, FIN)
    rows = send_rows[0]

    weights = tile_weight[0, 0]
    received = swap(gather_rows(rows, send_count, hub_blocks, features), "dom")
    fwd, bwd = order_tiles(
        tile_dst[0, 0].reshape(TILES // BLK, BLK), tile_src[0, 0].reshape(TILES // BLK, BLK)
    )
    stored = in_hbm(weights)
    near = forward_near(fwd, blocks, stored)
    hubs = swap(hub_piece(place, hub_blocks, received), "dom").reshape(HUBS, BLK, FIN)
    far = forward_remote(fwd, near, received, stored)
    own, s1, s2, s3 = forward_hub(fwd, place, far, hubs, stored)
    a, b, c = turn(s1, 1), turn(s2, 2), turn(s3, 3)
    out_part, y_part, gw = middle(
        place, own, a, b, c, proj_weight, bias.reshape(1, HID), cotangent
    )
    ys = around(y_part)
    message = backward_far(bwd, place, ys, gw, hold_tiles(stored, y_part))
    out_part, message = lax.optimization_barrier((out_part, message))
    output = lax.all_gather(out_part, "rep", axis=0, tiled=True)
    returned = swap(message.reshape(N_REP * N_DOM, MSG, BLK), ("rep", "dom"))
    own, s1, s2, s3 = backward_near(bwd, place, ys, stored)
    a, b, c = turn(s1, 1), turn(s2, 2), turn(s3, 3)

    piece = jnp.sum(returned[:, FQ:, :].astype(F32), axis=0).astype(BF16)
    shared = swap(jnp.broadcast_to(piece[None], (N_REP * N_DOM, 16, BLK)), ("rep", "dom"))
    part = scatter_rows(send_count, rows, returned, own, a, b, c)
    output, _ = lax.optimization_barrier((output, part))
    grad_x, grad_w = finish(place, hub_blocks, around(part), shared, 1.0 / math.sqrt(ROWS * N_DOM))
    return (place_output(output), grad_x, grad_w)


def solution(mesh):
    in_specs = (
        P("dom", None),
        P(),
        P(),
        P("dom", None),
        P("dom", None, None),
        P("dom", None),
        P(),
        P("rep", "dom", None),
        P("rep", "dom", None),
        P("rep", "dom", None, None, None),
    )
    out_specs = (P("dom", None), P("dom", None), P())
    return jax.shard_map(shards, mesh=mesh, in_specs=in_specs, out_specs=out_specs, check_vma=False)
```

time: 173 us -> 155 us (0.90)
  starting transfers between devices: 70.3 us -> 45.1 us
  Pallas kernels: 32.6 us -> 51.1 us
  local copies, waits for them, and re-layouts: 17.4 us -> 2.12 us
  between operations: 0.91 us -> 14.3 us
  waiting for transfers between devices: 49.8 us -> 41.5 us
    all_to_all x2 -> x4, waiting for transfers between devices: 0.01 us -> 30.6 us  [swap(): return lax.all_to_all(value, axes, split_axis=0, concat_axis=0, tiled=True)]
    ppermute x14 -> x0, starting transfers between devices: 24.2 us -> none  [the longest x6 10.2 us: over_chips(): lax.ppermute(value, 'dom', chips(0, k, 0))]
    ppermute x21 -> x12, waiting for transfers between devices: 33 us -> 10.2 us  [turn(): lax.ppermute(value, 'rep', [(i, (i + k) % N_REP) for i in range(N_REP)])]
    ppermute x14 -> x0, waiting for transfers between devices: 16.8 us -> none  [the longest x6 10.7 us: over_chips(): lax.ppermute(value, 'dom', chips(k, 0, 0))]
    unnamed x32 -> x16, local copies, waits for them, and re-layouts: 17.4 us -> 1.26 us
    pallas_call x10 -> x9, Pallas kernels: 24.1 us -> 36.5 us  [the longest x1 6.84 us: gather_rows(): pl.pallas_call(gather_kernel, out_shape=jax.ShapeDtypeStruct((N_DOM, BLK...]
    ppermute x21 -> x12, starting transfers between devices: 25.1 us -> 17.7 us  [turn(): lax.ppermute(value, 'rep', [(i, (i + k) % N_REP) for i in range(N_REP)])]
    all_to_all x2 -> x4, starting transfers between devices: 21 us -> 27.4 us  [swap(): return lax.all_to_all(value, axes, split_axis=0, concat_axis=0, tiled=True)]
  transfers between devices with their start and end apart: 37 -> 17, of which waited for: 16 -> 8; matrix products, arithmetic and copies ran while one was open for 0% -> 1% of each run, Pallas kernels for 5% -> 18%
where the time goes in v3:
time: 155 us; the launch traced here: 154 us
  Pallas kernels  51.1 us (33%)
  starting transfers between devices  45.1 us (29%)
  waiting for transfers between devices  41.5 us (27%)
  between operations  14.3 us (9%)
  local copies, waits for them, and re-layouts  2.12 us (1%)
    all_to_all x4, waiting for transfers between devices, swap(): return lax.all_to_all(value, axes, split_axis=0, concat_axis=0, tiled=True)  30.6 us
    all_to_all x4, starting transfers between devices, swap(): return lax.all_to_all(value, axes, split_axis=0, concat_axis=0, tiled=True)  27.4 us
    ppermute x12, starting transfers between devices, turn(): lax.ppermute(value, 'rep', [(i, (i + k) % N_REP) for i in range(N_REP)])  17.7 us
    ppermute x12, waiting for transfers between devices, turn(): lax.ppermute(value, 'rep', [(i, (i + k) % N_REP) for i in range(N_REP)])  10.2 us
    pallas_call x1, Pallas kernels, gather_rows(): pl.pallas_call(gather_kernel, out_shape=jax.ShapeDtypeStruct((N_DOM, BLK...  6.84 us
    pallas_call x1, Pallas kernels, backward_far(): pl.pallas_call(backward_far_kernel, out_shape=jax.ShapeDtypeStruct((N_REP...  6.39 us
    pallas_call x1, Pallas kernels, forward_remote(): pl.pallas_call(forward_remote_kernel, out_shape=jax.ShapeDtypeStruct((LOC...  6.16 us
    pallas_call x1, Pallas kernels, backward_near(): pl.pallas_call(backward_near_kernel, out_shape=[jax.ShapeDtypeStruct(part...  5.63 us
  transfers between devices with their start and end apart: 17, of which 8 were waited for; matrix products, arithmetic and copies ran while one was open for 1% of the time, Pallas kernels for 18%

profile of v3, /device:TPU:1, one launch (start us, length us, event | category | flops | bytes accessed | tf_op | source)
XLA Modules:
  0.0 154.4 jit_solution(16197195105705835333)
XLA Ops:
  7.2 6.8 %gather_rows.1 = bf16[32,160,128]{2,1,0:T(8,128)(2,1)} custom-call(s32[32,128]{1,0:T(8,128)} %bitcast.13, s32[1,32]{1,0:T(1,128)} %count_ref.3, s32[8]{0:T(128)} %hub_ref.5, bf16[2048,128]{1,0:T(8,128)(2,1)} %feat_hbm.1), custom_call_target="tpu_custom_call" | custom-call | flops 4000000000 | bytes 2000000 | tf_op jit(solution)/shard_map/gather_rows/pallas_call | solution.py:255
  14.0 0.0 copy-start.6
  14.0 0.0 copy-start.7
  14.0 0.0 copy-start.1
  14.0 9.6 %all-to-all-start = ((bf16[32,160,128]{2,1,0:T(8,128)(2,1)}), bf16[32,160,128]{2,1,0:T(8,128)(2,1)S(1)}, u32[]{:S(2)}, u32[]{:S(2)}) async-start(bf16[32,160,128]{2,1,0:T(8,128)(2,1)} %gather_rows.1), calls=%async_computation | async-start | bytes 2621440 | tf_op jit(solution)/shard_map/all_to_all | solution.py:630
  23.7 1.2 order_tiles.1
  24.9 5.6 %forward_near.1.near_ref = f32[16,128,128]{2,1,0:T(8,128)S(1)} custom-call(s32[4,5,128]{2,1,0:T(8,128)S(1)} %get-tuple-element.21.plan_ref, bf16[16,128,128]{2,1,0:T(8,128)(2,1)S(1)} %bitcast.10, bf16[384,128,128]{2,1,0:T(8,128)(2,1)} %bitcast.16), custom_call_target="tpu_custom_call" | custom-call | flops 1000000000 | bytes 4000000 | tf_op jit(solution)/shard_map/forward_near/pallas_call | solution.py:329
  30.5 0.1 pad_add_fusion.place_ref.rep_ref
  30.6 12.8 %all-to-all-done.recv_ref = bf16[32,160,128]{2,1,0:T(8,128)(2,1)S(1)} async-done(((bf16[32,160,128]{2,1,0:T(8,128)(2,1)}), bf16[32,160,128]{2,1,0:T(8,128)(2,1)S(1)}, u32[]{:S(2)}, u32[]{:S(2)}) %all-to-all-start) | async-done | bytes 1310752 | tf_op jit(solution)/shard_map/all_to_all | solution.py:630
  43.4 1.4 hub_piece.1
  44.8 4.6 %all-to-all-start.1 = ((bf16[32,32,128]{2,1,0:T(8,128)(2,1)}), bf16[32,32,128]{2,1,0:T(8,128)(2,1)}, u32[]{:S(2)}, u32[]{:S(2)}) async-start(bf16[32,32,128]{2,1,0:T(8,128)(2,1)} %hub_piece.1), calls=%async_computation.1 | async-start | bytes 524288 | tf_op jit(solution)/shard_map/all_to_all | solution.py:630
  49.4 6.2 %forward_remote.1.far_ref = f32[16,128,128]{2,1,0:T(8,128)S(1)} custom-call(s32[4,5,128]{2,1,0:T(8,128)S(1)} %get-tuple-element.21.plan_ref, f32[16,128,128]{2,1,0:T(8,128)S(1)} %forward_near.1.near_ref, bf16[32,160,128]{2,1,0:T(8,128)(2,1)S(1)} %all-to-all-done.recv_ref, bf16[384,128,128]{2,1,0:T(8,128)(2,1)} %bitcast.17), custom_call_target="tpu_custom_call" | custom-call | flops 4000000000 | bytes 9000000 | tf_op jit(solution)/shard_map/forward_remote/pallas_call | solution.py:342
  55.6 3.0 %all-to-all-done.1 = bf16[32,32,128]{2,1,0:T(8,128)(2,1)} async-done(((bf16[32,32,128]{2,1,0:T(8,128)(2,1)}), bf16[32,32,128]{2,1,0:T(8,128)(2,1)}, u32[]{:S(2)}, u32[]{:S(2)}) %all-to-all-start.1) | async-done | bytes 262176 | tf_op jit(solution)/shard_map/all_to_all | solution.py:630
  58.5 5.1 %forward_hub.1 = (f32[4,128,128]{2,1,0:T(8,128)S(1)}, bf16[4,128,128]{2,1,0:T(8,128)(2,1)S(1)}, bf16[4,128,128]{2,1,0:T(8,128)(2,1)S(1)}, bf16[4,128,128]{2,1,0:T(8,128)(2,1)S(1)}) custom-call(s32[4,5,128]{2,1,0:T(8,128)S(1)} %get-tuple-element.21.plan_ref, s32[2]{0:T(128)S(1)} %pad_add_fusion.place_ref.rep_ref, f32[16,128,128]{2,1,0:T(8,128)S(1)} %forward_remote.1.far_ref, ...), custom_call_target="tpu_custom_call" | custom-call | flops 1000000000 | bytes 3000000 | tf_op jit(solution)/shard_map/forward_hub/pallas_call | solution.py:356
  63.7 0.1 collective-permute-start
  63.8 3.0 %collective-permute-start.1 = (bf16[4,128,128]{2,1,0:T(8,128)(2,1)S(1)}, bf16[4,128,128]{2,1,0:T(8,128)(2,1)S(1)}, u32[]{:S(2)}, u32[]{:S(2)}) collective-permute-start(bf16[4,128,128]{2,1,0:T(8,128)(2,1)S(1)} %get-tuple-element.24), channel_id=1, source_target_pairs={{0,64},{32,96},{64,0},{96,32},{1,65},{33,97},{65,1},{97,33},{2,66}... | collective-permute-start | bytes 393224 | tf_op jit(solution)/shard_map/ppermute | solution.py:622
  66.8 2.0 %collective-permute-start.2 = (bf16[4,128,128]{2,1,0:T(8,128)(2,1)S(1)}, bf16[4,128,128]{2,1,0:T(8,128)(2,1)S(1)}, u32[]{:S(2)}, u32[]{:S(2)}) collective-permute-start(bf16[4,128,128]{2,1,0:T(8,128)(2,1)S(1)} %get-tuple-element.25), channel_id=1, source_target_pairs={{0,96},{32,0},{64,32},{96,64},{1,97},{33,1},{65,33},{97,65},{2,98}... | collective-permute-start | bytes 393224 | tf_op jit(solution)/shard_map/ppermute | solution.py:622
  68.8 0.7 collective-permute-done.refs_1_
  69.4 3.7 %collective-permute-done.1.refs_2_ = bf16[4,128,128]{2,1,0:T(8,128)(2,1)S(1)} collective-permute-done((bf16[4,128,128]{2,1,0:T(8,128)(2,1)S(1)}, bf16[4,128,128]{2,1,0:T(8,128)(2,1)S(1)}, u32[]{:S(2)}, u32[]{:S(2)}) %collective-permute-start.1) | collective-permute-done | bytes 131104 | tf_op jit(solution)/shard_map/ppermute | solution.py:622
  73.1 0.6 collective-permute-done.2.refs_3_
  73.7 1.9 %middle.1 = (bf16[512,256]{1,0:T(8,128)(2,1)}, bf16[4,128,128]{2,1,0:T(8,128)(2,1)S(1)}, bf16[32,16,128]{2,1,0:T(8,128)(2,1)S(1)}) custom-call(s32[2]{0:T(128)S(1)} %pad_add_fusion.place_ref.rep_ref, f32[4,128,128]{2,1,0:T(8,128)S(1)} %get-tuple-element.22.refs_0_, bf16[4,128,128]{2,1,0:T(8,128)(2,1)S(1)} %collective-permute-done.refs_1_, ...), custom_call_target="tpu_custom_call" | custom-call | flops 20000000000 | bytes 2000000 | tf_op jit(solution)/shard_map/middle/pallas_call | solution.py:396
  75.6 1.3 collective-permute-start.3
  76.9 1.8 %collective-permute-start.4 = (bf16[4,128,128]{2,1,0:T(8,128)(2,1)S(1)}, bf16[4,128,128]{2,1,0:T(8,128)(2,1)S(1)}, u32[]{:S(2)}, u32[]{:S(2)}) collective-permute-start(bf16[4,128,128]{2,1,0:T(8,128)(2,1)S(1)} %get-tuple-element.28.after_ref.y0), channel_id=1, source_target_pairs={{0,64},{32,96},{64,0},{96,32},{1,65},{33,97},{65,1},{97,33},{2,66}... | collective-permute-start | bytes 393224 | tf_op jit(solution)/shard_map/ppermute | solution.py:622
  78.7 1.0 collective-permute-start.5
  79.8 4.6 %hold_tiles.1.w_ref = bf16[384,128,128]{2,1,0:T(8,128)(2,1)S(1)} custom-call(bf16[384,128,128]{2,1,0:T(8,128)(2,1)} %bitcast.19, bf16[4,128,128]{2,1,0:T(8,128)(2,1)S(1)} %get-tuple-element.28.after_ref.y0), custom_call_target="tpu_custom_call" | custom-call | bytes 13000000 | tf_op jit(solution)/shard_map/hold_tiles/pallas_call | solution.py:428
  84.4 0.0 collective-permute-done.5.y3
  84.5 6.4 %backward_far.1 = bf16[4,32,48,128]{3,2,1,0:T(8,128)(2,1)} custom-call(s32[4,4,128]{2,1,0:T(4,128)S(1)} %get-tuple-element.27.plan_ref, s32[2]{0:T(128)S(1)} %pad_add_fusion.place_ref.rep_ref, bf16[4,128,128]{2,1,0:T(8,128)(2,1)S(1)} %get-tuple-element.28.after_ref.y0, bf16[4,128,128]{2,1,0:T(8,128)(2,1)S(1)} %collective-permute-done.3.y1, ...), custom_call_target="tpu_custom_call" | custom-call | flops 4000000000 | bytes 14000000 | tf_op jit(solution)/shard_map/backward_far/pallas_call | solution.py:472
  90.8 8.4 %all-to-all-start.2 = ((bf16[128,48,128]{2,1,0:T(8,128)(2,1)}), bf16[128,48,128]{2,1,0:T(8,128)(2,1)S(1)}, u32[]{:S(2)}, u32[]{:S(2)}) async-start(bf16[128,48,128]{2,1,0:T(8,128)(2,1)} %bitcast.7), calls=%async_computation.2 | async-start | bytes 3145728 | tf_op jit(solution)/shard_map/all_to_all | solution.py:630
  99.3 0.0 all-gather.2.cloned.1.call-start
  99.3 0.7 all-gather.2.cloned.1.call-update
  100.0 5.6 %backward_near.1 = (f32[16,32,128]{2,1,0:T(8,128)S(1)}, bf16[16,32,128]{2,1,0:T(8,128)(2,1)S(1)}, bf16[16,32,128]{2,1,0:T(8,128)(2,1)S(1)}, bf16[16,32,128]{2,1,0:T(8,128)(2,1)S(1)}) custom-call(s32[4,4,128]{2,1,0:T(4,128)S(1)} %get-tuple-element.27.plan_ref, s32[2]{0:T(128)S(1)} %pad_add_fusion.place_ref.rep_ref, ...), custom_call_target="tpu_custom_call" | custom-call | flops 1000000000 | bytes 14000000 | tf_op jit(solution)/shard_map/backward_near/pallas_call | solution.py:507
  105.7 0.0 copy-start.4
  105.7 0.1 collective-permute-start.6
  105.8 2.2 %collective-permute-start.7 = (bf16[16,32,128]{2,1,0:T(8,128)(2,1)S(1)}, bf16[16,32,128]{2,1,0:T(8,128)(2,1)S(1)}, u32[]{:S(2)}, u32[]{:S(2)}) collective-permute-start(bf16[16,32,128]{2,1,0:T(8,128)(2,1)S(1)} %get-tuple-element.34), channel_id=1, source_target_pairs={{0,64},{32,96},{64,0},{96,32},{1,65},{33,97},{65,1},{97,33},{2,66}... | collective-permute-start | bytes 393224 | tf_op jit(solution)/shard_map/ppermute | solution.py:622
  108.0 1.2 collective-permute-start.8
  109.2 14.8 %all-to-all-done.2.recv_ref = bf16[128,48,128]{2,1,0:T(8,128)(2,1)S(1)} async-done(((bf16[128,48,128]{2,1,0:T(8,128)(2,1)}), bf16[128,48,128]{2,1,0:T(8,128)(2,1)S(1)}, u32[]{:S(2)}, u32[]{:S(2)}) %all-to-all-start.2) | async-done | bytes 1572896 | tf_op jit(solution)/shard_map/all_to_all | solution.py:630
  124.0 0.1 slice_reduce_fusion
  124.1 0.9 broadcast_in_dim.2
  125.0 4.8 %all-to-all-start.3 = ((bf16[128,16,128]{2,1,0:T(8,128)(2,1)}), bf16[128,16,128]{2,1,0:T(8,128)(2,1)S(1)}, u32[]{:S(2)}, u32[]{:S(2)}) async-start(bf16[128,16,128]{2,1,0:T(8,128)(2,1)} %broadcast_in_dim.2), calls=%async_computation.3 | async-start | bytes 1048576 | tf_op jit(solution)/shard_map/all_to_all | solution.py:630
  129.9 3.1 %scatter_rows.1.m0 = bf16[16,32,128]{2,1,0:T(8,128)(2,1)S(1)} custom-call(s32[1,32]{1,0:T(1,128)} %count_ref.3, s32[32,128]{1,0:T(8,128)S(1)} %bitcast.14, bf16[128,48,128]{2,1,0:T(8,128)(2,1)S(1)} %all-to-all-done.2.recv_ref, f32[16,32,128]{2,1,0:T(8,128)S(1)} %get-tuple-element.32.own_ref, bf16[16,32,128]{2,1,0:T(8,128)(2,1)S(1)} %collective-permute-done.6.a_ref, ...), custom_call_target="tpu_custom_call" | custom-call | flops 4000000000 | bytes 4000000 | tf_op jit(solution)/shard_map/scatter_rows/pallas_call | solution.py:556
  132.9 1.5 collective-permute-start.9
  134.4 2.5 %collective-permute-start.10 = (bf16[16,32,128]{2,1,0:T(8,128)(2,1)S(1)}, bf16[16,32,128]{2,1,0:T(8,128)(2,1)S(1)}, u32[]{:S(2)}, u32[]{:S(2)}) collective-permute-start(bf16[16,32,128]{2,1,0:T(8,128)(2,1)S(1)} %scatter_rows.1.m0), channel_id=1, source_target_pairs={{0,64},{32,96},{64,0},{96,32},{1,65},{33,97},{65,1},{97,33},{2,66}... | collective-permute-start | bytes 393224 | tf_op jit(solution)/shard_map/ppermute | solution.py:622
  136.9 1.1 collective-permute-start.11
  138.0 1.2 copy-done
  139.2 1.0 place_output.1
  140.2 1.7 %collective-permute-done.9.m1 = bf16[16,32,128]{2,1,0:T(8,128)(2,1)S(1)} collective-permute-done((bf16[16,32,128]{2,1,0:T(8,128)(2,1)S(1)}, bf16[16,32,128]{2,1,0:T(8,128)(2,1)S(1)}, u32[]{:S(2)}, u32[]{:S(2)}) %collective-permute-start.9) | collective-permute-done | bytes 131104 | tf_op jit(solution)/shard_map/ppermute | solution.py:622
  142.0 3.4 %collective-permute-done.10.m2 = bf16[16,32,128]{2,1,0:T(8,128)(2,1)S(1)} collective-permute-done((bf16[16,32,128]{2,1,0:T(8,128)(2,1)S(1)}, bf16[16,32,128]{2,1,0:T(8,128)(2,1)S(1)}, u32[]{:S(2)}, u32[]{:S(2)}) %collective-permute-start.10) | collective-permute-done | bytes 131104 | tf_op jit(solution)/shard_map/ppermute | solution.py:622
  145.4 2.1 %finish.1 = (f32[2048,128]{1,0:T(8,128)}, f32[128,256]{1,0:T(8,128)}) custom-call(s32[2]{0:T(128)S(1)} %pad_add_fusion.place_ref.rep_ref, s32[8]{0:T(128)} %hub_ref.5, bf16[16,32,128]{2,1,0:T(8,128)(2,1)S(1)} %scatter_rows.1.m0, bf16[16,32,128]{2,1,0:T(8,128)(2,1)S(1)} %collective-permute-done.9.m1, bf16[16,32,128]{2,1,0:T(8,128)(2,1)S(1)} %collective-permute-done.10.m2, ...), custom_call_target="tpu_custom_call" | custom-call | tf_op jit(solution)/shard_map/finish/pallas_call | solution.py:592
  (21 shorter events, 0.1 us)
Async XLA Ops:
  14.0 9.6 %copy-start.6 = (s32[1,1,384]{2,1,0:T(1,128)S(1)}, s32[1,1,384]{2,1,0:T(1,128)}, u32[]{:S(2)}) copy-start(s32[1,1,384]{2,1,0:T(1,128)} %param.17) | copy-start | bytes 4612
  14.0 9.6 %copy-start.7 = (s32[1,1,384]{2,1,0:T(1,128)S(1)}, s32[1,1,384]{2,1,0:T(1,128)}, u32[]{:S(2)}) copy-start(s32[1,1,384]{2,1,0:T(1,128)} %param.18) | copy-start | bytes 4612
  14.0 10.9 %copy-start.1 = (bf16[2048,128]{1,0:T(8,128)(2,1)S(1)}, bf16[2048,128]{1,0:T(8,128)(2,1)}, u32[]{:S(2)}) copy-start(bf16[2048,128]{1,0:T(8,128)(2,1)} %feat_hbm.1) | copy-start | bytes 1572868
  14.0 29.4 %all-to-all-start = ((bf16[32,160,128]{2,1,0:T(8,128)(2,1)}), bf16[32,160,128]{2,1,0:T(8,128)(2,1)S(1)}, u32[]{:S(2)}, u32[]{:S(2)}) async-start(bf16[32,160,128]{2,1,0:T(8,128)(2,1)} %gather_rows.1), calls=%async_computation | async-start | bytes 2621440 | tf_op jit(solution)/shard_map/all_to_all | solution.py:630
  44.8 13.7 %all-to-all-start.1 = ((bf16[32,32,128]{2,1,0:T(8,128)(2,1)}), bf16[32,32,128]{2,1,0:T(8,128)(2,1)}, u32[]{:S(2)}, u32[]{:S(2)}) async-start(bf16[32,32,128]{2,1,0:T(8,128)(2,1)} %hub_piece.1), calls=%async_computation.1 | async-start | bytes 524288 | tf_op jit(solution)/shard_map/all_to_all | solution.py:630
  58.5 15.2 %copy-start.2 = (bf16[2048,256]{1,0:T(8,128)(2,1)S(1)}, bf16[2048,256]{1,0:T(8,128)(2,1)}, u32[]{:S(2)}) copy-start(bf16[2048,256]{1,0:T(8,128)(2,1)} %refs_6_.1) | copy-start | bytes 3145732
  58.5 15.2 %copy-start.3 = (bf16[128,256]{1,0:T(8,128)(2,1)S(1)}, bf16[128,256]{1,0:T(8,128)(2,1)}, u32[]{:S(2)}) copy-start(bf16[128,256]{1,0:T(8,128)(2,1)} %refs_4_.1) | copy-start | bytes 196612
  58.5 15.2 %copy-start.5 = (f32[256]{0:T(256)S(1)}, f32[256]{0:T(256)}, u32[]{:S(2)}) copy-start(f32[256]{0:T(256)} %param.12) | copy-start | bytes 3076
  63.7 5.8 %collective-permute-start = (bf16[4,128,128]{2,1,0:T(8,128)(2,1)S(1)}, bf16[4,128,128]{2,1,0:T(8,128)(2,1)S(1)}, u32[]{:S(2)}, u32[]{:S(2)}) collective-permute-start(bf16[4,128,128]{2,1,0:T(8,128)(2,1)S(1)} %get-tuple-element.23), channel_id=1, source_target_pairs={{0,32},{32,64},{64,96},{96,0},{1,33},{33,65},{65,97},{97,1},{2,34}... | collective-permute-start | bytes 393224 | tf_op jit(solution)/shard_map/ppermute | solution.py:622
  63.8 9.3 %collective-permute-start.1 = (bf16[4,128,128]{2,1,0:T(8,128)(2,1)S(1)}, bf16[4,128,128]{2,1,0:T(8,128)(2,1)S(1)}, u32[]{:S(2)}, u32[]{:S(2)}) collective-permute-start(bf16[4,128,128]{2,1,0:T(8,128)(2,1)S(1)} %get-tuple-element.24), channel_id=1, source_target_pairs={{0,64},{32,96},{64,0},{96,32},{1,65},{33,97},{65,1},{97,33},{2,66}... | collective-permute-start | bytes 393224 | tf_op jit(solution)/shard_map/ppermute | solution.py:622
  66.8 7.0 %collective-permute-start.2 = (bf16[4,128,128]{2,1,0:T(8,128)(2,1)S(1)}, bf16[4,128,128]{2,1,0:T(8,128)(2,1)S(1)}, u32[]{:S(2)}, u32[]{:S(2)}) collective-permute-start(bf16[4,128,128]{2,1,0:T(8,128)(2,1)S(1)} %get-tuple-element.25), channel_id=1, source_target_pairs={{0,96},{32,0},{64,32},{96,64},{1,97},{33,1},{65,33},{97,65},{2,98}... | collective-permute-start | bytes 393224 | tf_op jit(solution)/shard_map/ppermute | solution.py:622
  75.6 8.7 %collective-permute-start.3 = (bf16[4,128,128]{2,1,0:T(8,128)(2,1)S(1)}, bf16[4,128,128]{2,1,0:T(8,128)(2,1)S(1)}, u32[]{:S(2)}, u32[]{:S(2)}) collective-permute-start(bf16[4,128,128]{2,1,0:T(8,128)(2,1)S(1)} %get-tuple-element.28.after_ref.y0), channel_id=1, source_target_pairs={{0,32},{32,64},{64,96},{96,0},{1,33},{33,65},{65,97},{97,1},{2,34}... | collective-permute-start | bytes 393224 | tf_op jit(solution)/shard_map/ppermute | solution.py:622
  76.9 7.5 %collective-permute-start.4 = (bf16[4,128,128]{2,1,0:T(8,128)(2,1)S(1)}, bf16[4,128,128]{2,1,0:T(8,128)(2,1)S(1)}, u32[]{:S(2)}, u32[]{:S(2)}) collective-permute-start(bf16[4,128,128]{2,1,0:T(8,128)(2,1)S(1)} %get-tuple-element.28.after_ref.y0), channel_id=1, source_target_pairs={{0,64},{32,96},{64,0},{96,32},{1,65},{33,97},{65,1},{97,33},{2,66}... | collective-permute-start | bytes 393224 | tf_op jit(solution)/shard_map/ppermute | solution.py:622
  78.7 5.7 %collective-permute-start.5 = (bf16[4,128,128]{2,1,0:T(8,128)(2,1)S(1)}, bf16[4,128,128]{2,1,0:T(8,128)(2,1)S(1)}, u32[]{:S(2)}, u32[]{:S(2)}) collective-permute-start(bf16[4,128,128]{2,1,0:T(8,128)(2,1)S(1)} %get-tuple-element.28.after_ref.y0), channel_id=1, source_target_pairs={{0,96},{32,0},{64,32},{96,64},{1,97},{33,1},{65,33},{97,65},{2,98}... | collective-permute-start | bytes 393224 | tf_op jit(solution)/shard_map/ppermute | solution.py:622
  90.8 33.1 %all-to-all-start.2 = ((bf16[128,48,128]{2,1,0:T(8,128)(2,1)}), bf16[128,48,128]{2,1,0:T(8,128)(2,1)S(1)}, u32[]{:S(2)}, u32[]{:S(2)}) async-start(bf16[128,48,128]{2,1,0:T(8,128)(2,1)} %bitcast.7), calls=%async_computation.2 | async-start | bytes 3145728 | tf_op jit(solution)/shard_map/all_to_all | solution.py:630
  99.3 38.7 %all-gather.2.cloned.1.call-start = ((), (), s32[]{:S(2)}) async-start(), calls=%async_computation.4 | async-start | bytes 1310720 | tf_op jit(solution)/shard_map/all_gather | solution.py:669
  105.7 24.2 %copy-start.4 = (s32[1,32,128]{2,1,0:T(8,128)S(1)}, s32[1,32,128]{2,1,0:T(8,128)}, u32[]{:S(2)}) copy-start(s32[1,32,128]{2,1,0:T(8,128)} %param.14) | copy-start | bytes 49156
  105.7 24.2 %collective-permute-start.6 = (bf16[16,32,128]{2,1,0:T(8,128)(2,1)S(1)}, bf16[16,32,128]{2,1,0:T(8,128)(2,1)S(1)}, u32[]{:S(2)}, u32[]{:S(2)}) collective-permute-start(bf16[16,32,128]{2,1,0:T(8,128)(2,1)S(1)} %get-tuple-element.33), channel_id=1, source_target_pairs={{0,32},{32,64},{64,96},{96,0},{1,33},{33,65},{65,97},{97,1},{2,34}... | collective-permute-start | bytes 393224 | tf_op jit(solution)/shard_map/ppermute | solution.py:622
  105.8 24.0 %collective-permute-start.7 = (bf16[16,32,128]{2,1,0:T(8,128)(2,1)S(1)}, bf16[16,32,128]{2,1,0:T(8,128)(2,1)S(1)}, u32[]{:S(2)}, u32[]{:S(2)}) collective-permute-start(bf16[16,32,128]{2,1,0:T(8,128)(2,1)S(1)} %get-tuple-element.34), channel_id=1, source_target_pairs={{0,64},{32,96},{64,0},{96,32},{1,65},{33,97},{65,1},{97,33},{2,66}... | collective-permute-start | bytes 393224 | tf_op jit(solution)/shard_map/ppermute | solution.py:622
  108.0 21.9 %collective-permute-start.8 = (bf16[16,32,128]{2,1,0:T(8,128)(2,1)S(1)}, bf16[16,32,128]{2,1,0:T(8,128)(2,1)S(1)}, u32[]{:S(2)}, u32[]{:S(2)}) collective-permute-start(bf16[16,32,128]{2,1,0:T(8,128)(2,1)S(1)} %get-tuple-element.35), channel_id=1, source_target_pairs={{0,96},{32,0},{64,32},{96,64},{1,97},{33,1},{65,33},{97,65},{2,98}... | collective-permute-start | bytes 393224 | tf_op jit(solution)/shard_map/ppermute | solution.py:622
  125.0 20.4 %all-to-all-start.3 = ((bf16[128,16,128]{2,1,0:T(8,128)(2,1)}), bf16[128,16,128]{2,1,0:T(8,128)(2,1)S(1)}, u32[]{:S(2)}, u32[]{:S(2)}) async-start(bf16[128,16,128]{2,1,0:T(8,128)(2,1)} %broadcast_in_dim.2), calls=%async_computation.3 | async-start | bytes 1048576 | tf_op jit(solution)/shard_map/all_to_all | solution.py:630
  132.9 9.0 %collective-permute-start.9 = (bf16[16,32,128]{2,1,0:T(8,128)(2,1)S(1)}, bf16[16,32,128]{2,1,0:T(8,128)(2,1)S(1)}, u32[]{:S(2)}, u32[]{:S(2)}) collective-permute-start(bf16[16,32,128]{2,1,0:T(8,128)(2,1)S(1)} %scatter_rows.1.m0), channel_id=1, source_target_pairs={{0,32},{32,64},{64,96},{96,0},{1,33},{33,65},{65,97},{97,1},{2,34}... | collective-permute-start | bytes 393224 | tf_op jit(solution)/shard_map/ppermute | solution.py:622
  134.4 11.0 %collective-permute-start.10 = (bf16[16,32,128]{2,1,0:T(8,128)(2,1)S(1)}, bf16[16,32,128]{2,1,0:T(8,128)(2,1)S(1)}, u32[]{:S(2)}, u32[]{:S(2)}) collective-permute-start(bf16[16,32,128]{2,1,0:T(8,128)(2,1)S(1)} %scatter_rows.1.m0), channel_id=1, source_target_pairs={{0,64},{32,96},{64,0},{96,32},{1,65},{33,97},{65,1},{97,33},{2,66}... | collective-permute-start | bytes 393224 | tf_op jit(solution)/shard_map/ppermute | solution.py:622
  136.9 8.6 %collective-permute-start.11 = (bf16[16,32,128]{2,1,0:T(8,128)(2,1)S(1)}, bf16[16,32,128]{2,1,0:T(8,128)(2,1)S(1)}, u32[]{:S(2)}, u32[]{:S(2)}) collective-permute-start(bf16[16,32,128]{2,1,0:T(8,128)(2,1)S(1)} %scatter_rows.1.m0), channel_id=1, source_target_pairs={{0,96},{32,0},{64,32},{96,64},{1,97},{33,1},{65,33},{97,65},{2,98}... | collective-permute-start | bytes 393224 | tf_op jit(solution)/shard_map/ppermute | solution.py:622
  138.0 1.2 copy-start
Sparse Core Ops, SparseCore 0:
  102.4 34.8 all-gather.1

commit v4 on v3

--- a/solution.py
+++ b/solution.py
@@ -22,7 +22,7 @@
 TILES = 384
 REMOTE = N_DOM
 CHUNK = 32
-FWD_SLOTS = 640
+FWD_SLOTS = 512
 BWD_SLOTS = 512
 QUARTER = ROWS // N_REP
 QB = LOCAL // N_REP
@@ -117,11 +117,10 @@
     parts = TILES // BLK
     dst = [dst_ref[pl.ds(i, 1), :] for i in range(parts)]
     src = [src_ref[pl.ds(i, 1), :] for i in range(parts)]
-    hub = LOCAL + REMOTE
-    bucket = [d + jnp.where(s < LOCAL, 0, jnp.where(s < hub, LOCAL, 2 * LOCAL)) for d, s in zip(dst, src)]
-    operand = [s - jnp.where(s < LOCAL, 0, jnp.where(s < hub, LOCAL, hub)) for s in src]
-    edges = (LOCAL, 2 * LOCAL, 3 * LOCAL)
-    found = sort_tiles(bucket, operand, REMOTE, edges, lambda b: b & (LOCAL - 1), FWD_SLOTS)
+    bucket = [jnp.where(s < LOCAL, d, d + LOCAL) for d, s in zip(dst, src)]
+    operand = [jnp.where(s < LOCAL, s, s - LOCAL) for s in src]
+    empty = REMOTE + HUBS
+    found = sort_tiles(bucket, operand, empty, (LOCAL, 2 * LOCAL), lambda b: b & (LOCAL - 1), FWD_SLOTS)
     for n, rows in enumerate(found[:3]):
         for s, row in enumerate(rows):
             fwd_ref[n, pl.ds(s, 1), :] = row
@@ -211,10 +210,10 @@
     lax.fori_loop(0, count, chunk, 0)
 
 
-PEERS = 4
-
-
-def gather_kernel(rows_hbm, count_ref, hub_ref, feat_hbm, out_ref, rows_ref, feat_ref, sems):
+PEERS = 8
+
+
+def gather_kernel(rows_hbm, count_ref, feat_hbm, out_ref, rows_ref, feat_ref, sems):
     loads = [
         pltpu.make_async_copy(feat_hbm, feat_ref, sems.at[0]),
         pltpu.make_async_copy(rows_hbm, rows_ref, sems.at[1]),
@@ -244,18 +243,13 @@
         return carry
 
     lax.fori_loop(0, N_DOM // PEERS, step, 0)
-    per_hub = BLK // HUB_ROWS
-    for p in range(N_DOM):
-        first = (hub_ref[p // per_hub] & (LOCAL - 1)) * BLK + (p % per_hub) * HUB_ROWS
-        first = pl.multiple_of(first, HUB_ROWS)
-        out_ref[p, pl.ds(BLK, HUB_ROWS), :] = feat_ref[pl.ds(first, HUB_ROWS), :]
-
-
-def gather_rows(rows, counts, hubs, features):
+
+
+def gather_rows(rows, counts, features):
     return pl.pallas_call(
         gather_kernel,
         out_shape=jax.ShapeDtypeStruct((N_DOM, BLK + HUB_ROWS, FIN), BF16),
-        in_specs=[FAR, SM, SM, FAR],
+        in_specs=[FAR, SM, FAR],
         out_specs=VM,
         scratch_shapes=[
             pltpu.VMEM((N_DOM, BLK), jnp.int32),
@@ -265,25 +259,54 @@
         compiler_params=PARAMS,
         cost_estimate=pl.CostEstimate(flops=4 * 10**9, bytes_accessed=2 * 10**6, transcendentals=0),
         name="gather_rows",
-    )(in_hbm(rows), counts, hubs, in_hbm(features))
-
-
-def piece_kernel(place_ref, hub_ref, recv_ref, out_ref):
+    )(in_hbm(rows), counts, in_hbm(features))
+
+
+def hub_pick_kernel(hub_ref, feat_hbm, out_ref, sem):
+    copies = []
+    for h in range(HUBS):
+        block = hub_ref[h] & (LOCAL - 1)
+        copies.append(pltpu.make_async_copy(feat_hbm.at[block], out_ref.at[h], sem.at[h]))
+    for copy in copies:
+        copy.start()
+    for copy in copies:
+        copy.wait()
+
+
+def pick_hubs(hubs, features):
+    return pl.pallas_call(
+        hub_pick_kernel,
+        out_shape=jax.ShapeDtypeStruct((HUBS, BLK, FIN), BF16),
+        in_specs=[SM, FAR],
+        out_specs=VM,
+        scratch_shapes=[pltpu.SemaphoreType.DMA((HUBS,))],
+        compiler_params=PARAMS,
+        name="pick_hubs",
+    )(hubs, in_hbm(features))
+
+
+def insert_kernel(place_ref, hub_ref, spread_ref, listed_ref, out_ref, wide, sem):
+    del listed_ref
     owner = lax.shift_right_logical(hub_ref[place_ref[1] // (BLK // HUB_ROWS)], 4)
-    piece = recv_ref[owner, pl.ds(BLK, HUB_ROWS), :]
+    piece = spread_ref[owner]
     for p in range(N_DOM):
-        out_ref[p] = piece
-
-
-def hub_piece(place, hubs, received):
-    return pl.pallas_call(
-        piece_kernel,
-        out_shape=jax.ShapeDtypeStruct((N_DOM, HUB_ROWS, FIN), BF16),
-        in_specs=[SM, SM, VM],
-        out_specs=VM,
-        compiler_params=PARAMS,
-        name="hub_piece",
-    )(place, hubs, received)
+        wide[p] = piece
+    copy = pltpu.make_async_copy(wide, out_ref.at[:, pl.ds(BLK, HUB_ROWS), :], sem)
+    copy.start()
+    copy.wait()
+
+
+def insert_hubs(place, hubs, spread, listed):
+    return pl.pallas_call(
+        insert_kernel,
+        out_shape=jax.ShapeDtypeStruct(listed.shape, BF16),
+        in_specs=[SM, SM, VM, pl.BlockSpec(memory_space=pl.ANY)],
+        out_specs=pl.BlockSpec(memory_space=pl.ANY),
+        scratch_shapes=[pltpu.VMEM((N_DOM, HUB_ROWS, FIN), BF16), pltpu.SemaphoreType.DMA],
+        input_output_aliases={3: 0},
+        compiler_params=PARAMS,
+        name="insert_hubs",
+    )(place, hubs, spread, listed)
 
 
 def forward_product(xs):
@@ -294,35 +317,31 @@
     return product
 
 
+FORWARD_XS = pltpu.VMEM((REMOTE + HUBS + 1, BLK, FIN), BF16)
+
+
 def forward_near_kernel(plan_ref, feat_ref, w_ref, acc_ref, xs, held, sems):
     fetch_first(plan_ref, 0, w_ref, held, sems)
     xs[pl.ds(0, LOCAL)] = feat_ref[...]
-    xs[REMOTE] = jnp.zeros((BLK, FIN), BF16)
+    xs[REMOTE + HUBS] = jnp.zeros((BLK, FIN), BF16)
     acc_ref[...] = jnp.zeros_like(acc_ref)
     run_class(plan_ref, 0, w_ref, held, sems, forward_product(xs), acc_ref)
 
 
-def forward_remote_kernel(plan_ref, near_ref, recv_ref, w_ref, acc_ref, xs, held, sems):
+def forward_far_kernel(plan_ref, place_ref, near_ref, recv_ref, w_ref, own_ref, s1, s2, s3, xs, acc, held, sems):
     fetch_first(plan_ref, 1, w_ref, held, sems)
     xs[pl.ds(0, REMOTE)] = recv_ref[:, pl.ds(0, BLK), :]
-    xs[REMOTE] = jnp.zeros((BLK, FIN), BF16)
-    acc_ref[...] = near_ref[...]
-    run_class(plan_ref, 1, w_ref, held, sems, forward_product(xs), acc_ref)
-
-
-def forward_hub_kernel(plan_ref, place_ref, far_ref, hub_ref, w_ref, own_ref, s1, s2, s3, xs, acc, held, sems):
-    fetch_first(plan_ref, 2, w_ref, held, sems)
-    xs[pl.ds(0, HUBS)] = hub_ref[...]
-    xs[REMOTE] = jnp.zeros((BLK, FIN), BF16)
-    acc[...] = far_ref[...]
-    run_class(plan_ref, 2, w_ref, held, sems, forward_product(xs), acc)
+    per_hub = BLK // HUB_ROWS
+    for p in range(N_DOM):
+        rows = pl.ds((p % per_hub) * HUB_ROWS, HUB_ROWS)
+        xs[REMOTE + p // per_hub, rows, :] = recv_ref[p, pl.ds(BLK, HUB_ROWS), :]
+    xs[REMOTE + HUBS] = jnp.zeros((BLK, FIN), BF16)
+    acc[...] = near_ref[...]
+    run_class(plan_ref, 1, w_ref, held, sems, forward_product(xs), acc)
     rep = place_ref[0]
     own_ref[...] = acc[pl.ds(rep * QB, QB)]
     for k, ref in ((1, s1), (2, s2), (3, s3)):
         ref[...] = acc[pl.ds(lax.rem(rep + k, N_REP) * QB, QB)].astype(BF16)
-
-
-FORWARD_XS = pltpu.VMEM((REMOTE + 1, BLK, FIN), BF16)
 
 
 def forward_near(plan, features, weights):
@@ -338,83 +357,77 @@
     )(plan, features, weights)
 
 
-def forward_remote(plan, near, received, weights):
-    return pl.pallas_call(
-        forward_remote_kernel,
-        out_shape=jax.ShapeDtypeStruct((LOCAL, BLK, FIN), F32),
-        in_specs=[SM, VM, VM, FAR],
-        out_specs=VM,
-        scratch_shapes=[FORWARD_XS] + keep(TILES, LOCAL),
-        compiler_params=TILE_PARAMS,
-        cost_estimate=pl.CostEstimate(flops=4 * 10**9, bytes_accessed=9 * 10**6, transcendentals=0),
-        name="forward_remote",
-    )(plan, near, received, weights)
-
-
-def forward_hub(plan, place, far, hubs, weights):
+def forward_far(plan, place, near, received, weights):
     quarter = (QB, BLK, FIN)
     return pl.pallas_call(
-        forward_hub_kernel,
+        forward_far_kernel,
         out_shape=[jax.ShapeDtypeStruct(quarter, F32)] + [jax.ShapeDtypeStruct(quarter, BF16)] * 3,
         in_specs=[SM, SM, VM, VM, FAR],
         out_specs=[VM] * 4,
-        scratch_shapes=[FORWARD_XS, pltpu.VMEM((LOCAL, BLK, FIN), F32)] + keep(LOCAL * HUBS, LOCAL),
+        scratch_shapes=[FORWARD_XS, pltpu.VMEM((LOCAL, BLK, FIN), F32)] + keep(TILES, LOCAL),
         compiler_params=TILE_PARAMS,
-        cost_estimate=pl.CostEstimate(flops=10**9, bytes_accessed=3 * 10**6, transcendentals=0),
-        name="forward_hub",
-    )(plan, place, far, hubs, weights)
-
-
-def middle_kernel(own_ref, a_ref, b_ref, c_ref, w_ref, bias_ref, cot_ref, out_ref, y_ref, gw_ref):
-    zx = (own_ref[...] + a_ref[...].astype(F32)) + (b_ref[...].astype(F32) + c_ref[...].astype(F32))
-    zx = zx.reshape(QUARTER, FIN)
+        cost_estimate=pl.CostEstimate(flops=4 * 10**9, bytes_accessed=12 * 10**6, transcendentals=0),
+        name="forward_far",
+    )(plan, place, near, received, weights)
+
+
+def sum_kernel(own_ref, a_ref, b_ref, c_ref, out_ref):
+    far = a_ref[...].astype(F32) + b_ref[...].astype(F32) + c_ref[...].astype(F32)
+    out_ref[...] = (own_ref[...] + far).astype(BF16)
+
+
+def sum_quarter(own, a, b, c):
+    return pl.pallas_call(
+        sum_kernel,
+        out_shape=jax.ShapeDtypeStruct((QB, BLK, FIN), BF16),
+        in_specs=[VM] * 4,
+        out_specs=VM,
+        compiler_params=PARAMS,
+        name="sum_quarter",
+    )(own, a, b, c)
+
+
+def middle_kernel(place_ref, z0, z1, z2, z3, w_ref, bias_ref, cot_ref, out_ref, y_ref, gw_ref):
     weight = w_ref[...]
-    zh, zl = halves(zx)
-    pre = dot(zh, weight) + dot(zl, weight) + bias_ref[...]
     root = math.sqrt(2.0 / math.pi)
-    square = pre * pre
-    bent = jnp.tanh(root * (pre + 0.044715 * (square * pre)))
-    cdf = 0.5 * (1.0 + bent)
-    out_ref[...] = (pre * cdf).astype(BF16)
-    slope = cdf + (0.5 * pre) * ((1.0 - bent * bent) * (root * (1.0 + (3 * 0.044715) * square)))
-    pre_grad = (cot_ref[...].astype(F32) * slope).astype(BF16)
-    yt = lax.dot_general(weight, pre_grad, (((1,), (1,)), ((), ())), preferred_element_type=F32)
-    yt = yt.astype(BF16)
-    for k in range(QB):
-        y_ref[k] = yt[:, k * BLK : (k + 1) * BLK]
-    th, tl = halves(zx.T)
-    gw = dot(th, pre_grad) + dot(tl, pre_grad)
-    for part, piece in enumerate(halves(gw)):
-        for c in range(16):
-            g, side = c // 2, c % 2
-            gw_ref[part * 16 + c] = piece[g * 16 : (g + 1) * 16, side * BLK : (side + 1) * BLK]
-
-
-def middle(rep, own, a, b, c, weight, bias, cotangent):
-    whole = lambda shape: pl.BlockSpec(shape, lambda i, rep_ref: (0,) * len(shape))
-    quarter = (QB, BLK, FIN)
-    return pl.pallas_call(
-        lambda rep_ref, *refs: middle_kernel(*refs),
-        grid_spec=pltpu.PrefetchScalarGridSpec(
-            num_scalar_prefetch=1,
-            grid=(1,),
-            in_specs=[whole(quarter)] * 4
-            + [
-                whole((FIN, HID)),
-                whole((1, HID)),
-                pl.BlockSpec((QUARTER, HID), lambda i, rep_ref: (rep_ref[0], 0)),
-            ],
-            out_specs=[whole((QUARTER, HID)), whole((QB, FIN, BLK)), whole((32, 16, BLK))],
-        ),
+    for turned, ref in enumerate((z0, z1, z2, z3)):
+        quarter = lax.rem(place_ref[0] + N_REP - turned, N_REP)
+        zx = ref[...].reshape(QUARTER, FIN)
+        pre = dot(zx, weight) + bias_ref[...]
+        square = pre * pre
+        bent = jnp.tanh(root * (pre + 0.044715 * (square * pre)))
+        cdf = 0.5 * (1.0 + bent)
+        rows = pl.ds(pl.multiple_of(quarter * QUARTER, QUARTER), QUARTER)
+        out_ref[rows, :] = (pre * cdf).astype(BF16)
+        slope = cdf + (0.5 * pre) * ((1.0 - bent * bent) * (root * (1.0 + (3 * 0.044715) * square)))
+        pre_grad = (cot_ref[rows, :].astype(F32) * slope).astype(BF16)
+        yt = lax.dot_general(weight, pre_grad, (((1,), (1,)), ((), ())), preferred_element_type=F32)
+        yt = yt.astype(BF16)
+        for k in range(QB):
+            y_ref[quarter * QB + k] = yt[:, k * BLK : (k + 1) * BLK]
+        if turned == 0:
+            gw = dot(zx.T, pre_grad)
+            for part, piece in enumerate(halves(gw)):
+                for c in range(16):
+                    g, side = c // 2, c % 2
+                    gw_ref[part * 16 + c] = piece[g * 16 : (g + 1) * 16, side * BLK : (side + 1) * BLK]
+    y_ref[LOCAL] = jnp.zeros((FIN, BLK), BF16)
+
+
+def middle(place, zs, weight, bias, cotangent):
+    return pl.pallas_call(
+        middle_kernel,
         out_shape=[
-            jax.ShapeDtypeStruct((QUARTER, HID), BF16),
-            jax.ShapeDtypeStruct((QB, FIN, BLK), BF16),
+            jax.ShapeDtypeStruct((ROWS, HID), BF16),
+            jax.ShapeDtypeStruct((LOCAL + 1, FIN, BLK), BF16),
             jax.ShapeDtypeStruct((32, 16, BLK), BF16),
         ],
-        compiler_params=PARAMS,
-        cost_estimate=pl.CostEstimate(flops=2 * 10**10, bytes_accessed=2 * 10**6, transcendentals=0),
+        in_specs=[SM] + [VM] * 7,
+        out_specs=[VM] * 3,
+        compiler_params=PARAMS,
+        cost_estimate=pl.CostEstimate(flops=5 * 10**9, bytes_accessed=3 * 10**6, transcendentals=0),
         name="middle",
-    )(rep, own, a, b, c, weight, bias, cotangent)
+    )(place, *zs, weight, bias, cotangent)
 
 
 def hold_kernel(w_ref, after_ref, held_ref, sem):
@@ -445,16 +458,7 @@
     return product
 
 
-def load_ys(rep, refs, ys):
-    for k, ref in enumerate(refs):
-        ys[pl.ds(lax.rem(rep + N_REP - k, N_REP) * QB, QB)] = ref[...]
-    ys[LOCAL] = jnp.zeros((FIN, BLK), BF16)
-
-
-def backward_far_kernel(
-    plan_ref, rep_ref, y0, y1, y2, y3, gw_ref, w_ref, msg_ref, ys, acc
-):
-    load_ys(rep_ref[0], (y0, y1, y2, y3), ys)
+def backward_far_kernel(plan_ref, ys, gw_ref, w_ref, msg_ref, acc):
     acc[...] = jnp.zeros_like(acc)
     run_class(plan_ref, 0, w_ref, None, None, backward_product(ys), acc)
     for q in range(N_REP):
@@ -468,28 +472,22 @@
                 msg_ref[q, 2 * m + 1, pl.ds(FQ, 16), :] = jnp.zeros((16, BLK), BF16)
 
 
-def backward_far(plan, rep, ys, gw, weights):
+def backward_far(plan, ys, gw, weights):
     return pl.pallas_call(
         backward_far_kernel,
         out_shape=jax.ShapeDtypeStruct((N_REP, N_DOM, MSG, BLK), BF16),
-        in_specs=[SM, SM] + [VM] * 6,
+        in_specs=[SM] + [VM] * 3,
         out_specs=VM,
-        scratch_shapes=[
-            pltpu.VMEM((LOCAL + 1, FIN, BLK), BF16),
-            pltpu.VMEM((REMOTE + HUBS, FIN, BLK), F32),
-        ],
+        scratch_shapes=[pltpu.VMEM((REMOTE + HUBS, FIN, BLK), F32)],
         compiler_params=TILE_PARAMS,
         cost_estimate=pl.CostEstimate(flops=4 * 10**9, bytes_accessed=14 * 10**6, transcendentals=0),
         name="backward_far",
-    )(plan, rep, *ys, gw, weights)
-
-
-def backward_near_kernel(
-    plan_ref, rep_ref, y0, y1, y2, y3, w_ref, own_ref, s1, s2, s3, ys, acc, held, sems
-):
+    )(plan, ys, gw, weights)
+
+
+def backward_near_kernel(plan_ref, rep_ref, ys, w_ref, own_ref, s1, s2, s3, acc, held, sems):
     fetch_first(plan_ref, 1, w_ref, held, sems)
     rep = rep_ref[0]
-    load_ys(rep, (y0, y1, y2, y3), ys)
     acc[...] = jnp.zeros_like(acc)
     run_class(plan_ref, 1, w_ref, held, sems, backward_product(ys), acc)
 
@@ -507,17 +505,13 @@
     return pl.pallas_call(
         backward_near_kernel,
         out_shape=[jax.ShapeDtypeStruct(part, F32)] + [jax.ShapeDtypeStruct(part, BF16)] * 3,
-        in_specs=[SM, SM] + [VM] * 4 + [FAR],
+        in_specs=[SM, SM, VM, FAR],
         out_specs=[VM] * 4,
-        scratch_shapes=[
-            pltpu.VMEM((LOCAL + 1, FIN, BLK), BF16),
-            pltpu.VMEM((LOCAL, FIN, BLK), F32),
-        ]
-        + keep(LOCAL * LOCAL, LOCAL),
+        scratch_shapes=[pltpu.VMEM((LOCAL, FIN, BLK), F32)] + keep(LOCAL * LOCAL, LOCAL),
         compiler_params=TILE_PARAMS,
         cost_estimate=pl.CostEstimate(flops=10**9, bytes_accessed=14 * 10**6, transcendentals=0),
         name="backward_near",
-    )(plan, rep, *ys, weights)
+    )(plan, rep, ys, weights)
 
 
 SCATTER_PEERS = 8
@@ -601,21 +595,6 @@
         compiler_params=PARAMS,
         name="finish",
     )(place, hubs, *parts, shared)
-
-
-def place_kernel(act_ref, out_ref):
-    out_ref[...] = act_ref[...]
-
-
-def place_output(output):
-    return pl.pallas_call(
-        place_kernel,
-        out_shape=jax.ShapeDtypeStruct(output.shape, output.dtype),
-        in_specs=[VM],
-        out_specs=VM,
-        compiler_params=PARAMS,
-        name="place_output",
-    )(output)
 
 
 def turn(value, k):
@@ -650,23 +629,20 @@
     rows = send_rows[0]
 
     weights = tile_weight[0, 0]
-    received = swap(gather_rows(rows, send_count, hub_blocks, features), "dom")
+    spread = swap(pick_hubs(hub_blocks, blocks).reshape(N_DOM, HUB_ROWS, FIN), "dom")
+    listed = gather_rows(rows, send_count, features)
+    received = swap(insert_hubs(place, hub_blocks, spread, listed), "dom")
     fwd, bwd = order_tiles(
         tile_dst[0, 0].reshape(TILES // BLK, BLK), tile_src[0, 0].reshape(TILES // BLK, BLK)
     )
     stored = in_hbm(weights)
     near = forward_near(fwd, blocks, stored)
-    hubs = swap(hub_piece(place, hub_blocks, received), "dom").reshape(HUBS, BLK, FIN)
-    far = forward_remote(fwd, near, received, stored)
-    own, s1, s2, s3 = forward_hub(fwd, place, far, hubs, stored)
+    own, s1, s2, s3 = forward_far(fwd, place, near, received, stored)
     a, b, c = turn(s1, 1), turn(s2, 2), turn(s3, 3)
-    out_part, y_part, gw = middle(
-        place, own, a, b, c, proj_weight, bias.reshape(1, HID), cotangent
-    )
-    ys = around(y_part)
-    message = backward_far(bwd, place, ys, gw, hold_tiles(stored, y_part))
-    out_part, message = lax.optimization_barrier((out_part, message))
-    output = lax.all_gather(out_part, "rep", axis=0, tiled=True)
+    zq = sum_quarter(own, a, b, c)
+    held = hold_tiles(stored, zq)
+    output, ys, gw = middle(place, around(zq), proj_weight, bias.reshape(1, HID), cotangent)
+    message = backward_far(bwd, ys, gw, held)
     returned = swap(message.reshape(N_REP * N_DOM, MSG, BLK), ("rep", "dom"))
     own, s1, s2, s3 = backward_near(bwd, place, ys, stored)
     a, b, c = turn(s1, 1), turn(s2, 2), turn(s3, 3)
@@ -674,9 +650,8 @@
     piece = jnp.sum(returned[:, FQ:, :].astype(F32), axis=0).astype(BF16)
     shared = swap(jnp.broadcast_to(piece[None], (N_REP * N_DOM, 16, BLK)), ("rep", "dom"))
     part = scatter_rows(send_count, rows, returned, own, a, b, c)
-    output, _ = lax.optimization_barrier((output, part))
     grad_x, grad_w = finish(place, hub_blocks, around(part), shared, 1.0 / math.sqrt(ROWS * N_DOM))
-    return (place_output(output), grad_x, grad_w)
+    return (output, grad_x, grad_w)
 
 
 def solution(mesh):

time: 155 us -> 141 us (0.910)
  between operations: 14.3 us -> 0.91 us
  Pallas kernels: 51.1 us -> 45.3 us
  waiting for transfers between devices: 41.5 us -> 44.7 us
  starting transfers between devices: 45.1 us -> 47.6 us
    all_to_all x4, waiting for transfers between devices: 30.6 us -> 33.3 us  [swap(): return lax.all_to_all(value, axes, split_axis=0, concat_axis=0, tiled=True)]
    ppermute x12, starting transfers between devices: 17.7 us -> 20.3 us  [turn(): lax.ppermute(value, 'rep', [(i, (i + k) % N_REP) for i in range(N_REP)])]
    pallas_call x1, Pallas kernels: 5.6 us -> 3.84 us  [forward_near(): pl.pallas_call(forward_near_kernel, out_shape=jax.ShapeDtypeStruct((LOCAL...]
    pallas_call x1, Pallas kernels: 5.63 us -> 4.02 us  [backward_near(): pl.pallas_call(backward_near_kernel, out_shape=[jax.ShapeDtypeStruct(part...]
  transfers between devices with their start and end apart: 17 -> 16, of which waited for: 8 -> 8; matrix products, arithmetic and copies ran while one was open for 1% -> 1% of each run, Pallas kernels for 18% -> 16%
where the time goes in v4:
time: 141 us; the launch traced here: 140 us
  starting transfers between devices  47.6 us (34%)
  Pallas kernels  45.3 us (32%)
  waiting for transfers between devices  44.7 us (32%)
    all_to_all x4, waiting for transfers between devices, swap(): return lax.all_to_all(value, axes, split_axis=0, concat_axis=0, tiled=True)  33.3 us
    all_to_all x4, starting transfers between devices, swap(): return lax.all_to_all(value, axes, split_axis=0, concat_axis=0, tiled=True)  27.3 us
    ppermute x12, starting transfers between devices, turn(): lax.ppermute(value, 'rep', [(i, (i + k) % N_REP) for i in range(N_REP)])  20.3 us
    ppermute x12, waiting for transfers between devices, turn(): lax.ppermute(value, 'rep', [(i, (i + k) % N_REP) for i in range(N_REP)])  11.4 us
    pallas_call x1, Pallas kernels, forward_far(): pl.pallas_call(forward_far_kernel, out_shape=[jax.ShapeDtypeStruct(quarte...  6.93 us
    pallas_call x1, Pallas kernels, backward_far(): pl.pallas_call(backward_far_kernel, out_shape=jax.ShapeDtypeStruct((N_REP...  6.33 us
    pallas_call x1, Pallas kernels, gather_rows(): pl.pallas_call(gather_kernel, out_shape=jax.ShapeDtypeStruct((N_DOM, BLK...  5.93 us
    pallas_call x1, Pallas kernels, hold_tiles(): pl.pallas_call(hold_kernel, out_shape=pltpu.VMEM((TILES, BLK, BLK), BF16)...  4.58 us
  transfers between devices with their start and end apart: 16, of which 8 were waited for; matrix products, arithmetic and copies ran while one was open for 1% of the time, Pallas kernels for 16%

profile of v4, /device:TPU:1, one launch (start us, length us, event | category | flops | bytes accessed | tf_op | source)
XLA Modules:
  0.0 139.6 jit_solution(7765666280241074647)
XLA Ops:
  0.6 2.3 %pick_hubs.1 = bf16[8,128,128]{2,1,0:T(8,128)(2,1)} custom-call(s32[8]{0:T(128)} %hub_ref.5, bf16[16,128,128]{2,1,0:T(8,128)(2,1)} %bitcast.10), custom_call_target="tpu_custom_call" | custom-call | tf_op jit(solution)/shard_map/pick_hubs/pallas_call | solution.py:277
  2.9 9.4 %all-to-all-start = ((bf16[32,32,128]{2,1,0:T(8,128)(2,1)}), bf16[32,32,128]{2,1,0:T(8,128)(2,1)S(1)}, u32[]{:S(2)}, u32[]{:S(2)}) async-start(bf16[32,32,128]{2,1,0:T(8,128)(2,1)} %bitcast.4), calls=%async_computation | async-start | bytes 524288 | tf_op jit(solution)/shard_map/all_to_all | solution.py:609
  12.4 0.1 pad_add_fusion.place_ref.rep_ref
  12.5 5.9 %gather_rows.1.listed_ref = bf16[32,160,128]{2,1,0:T(8,128)(2,1)} custom-call(s32[32,128]{1,0:T(8,128)} %bitcast.14, s32[1,32]{1,0:T(1,128)} %count_ref.3, bf16[2048,128]{1,0:T(8,128)(2,1)} %feat_hbm.1), custom_call_target="tpu_custom_call" | custom-call | flops 4000000000 | bytes 2000000 | tf_op jit(solution)/shard_map/gather_rows/pallas_call | solution.py:249
  18.4 3.0 %all-to-all-done.spread_ref = bf16[32,32,128]{2,1,0:T(8,128)(2,1)S(1)} async-done(((bf16[32,32,128]{2,1,0:T(8,128)(2,1)}), bf16[32,32,128]{2,1,0:T(8,128)(2,1)S(1)}, u32[]{:S(2)}, u32[]{:S(2)}) %all-to-all-start) | async-done | bytes 262176 | tf_op jit(solution)/shard_map/all_to_all | solution.py:609
  21.4 1.4 %insert_hubs.1 = bf16[32,160,128]{2,1,0:T(8,128)(2,1)} custom-call(s32[2]{0:T(128)S(1)} %pad_add_fusion.place_ref.rep_ref, s32[8]{0:T(128)} %hub_ref.5, bf16[32,32,128]{2,1,0:T(8,128)(2,1)S(1)} %all-to-all-done.spread_ref, bf16[32,160,128]{2,1,0:T(8,128)(2,1)} %gather_rows.1.listed_ref), custom_call_target="tpu_custom_call", output_to_operand_aliasing={{}: (3, {})} | custom-call | tf_op jit(solution)/shard_map/insert_hubs/pallas_call | solution.py:300
  22.8 0.0 copy-start.5
  22.8 0.0 copy-start.6
  22.9 0.0 copy-start
  22.9 4.6 %all-to-all-start.1 = ((bf16[32,160,128]{2,1,0:T(8,128)(2,1)}), bf16[32,160,128]{2,1,0:T(8,128)(2,1)S(1)}, u32[]{:S(2)}, u32[]{:S(2)}) async-start(bf16[32,160,128]{2,1,0:T(8,128)(2,1)} %insert_hubs.1), calls=%async_computation.1 | async-start | bytes 2621440 | tf_op jit(solution)/shard_map/all_to_all | solution.py:609
  27.5 1.2 order_tiles.1
  28.7 3.8 %forward_near.1.near_ref = f32[16,128,128]{2,1,0:T(8,128)S(1)} custom-call(s32[4,4,128]{2,1,0:T(4,128)S(1)} %get-tuple-element.18.plan_ref, bf16[16,128,128]{2,1,0:T(8,128)(2,1)S(1)} %bitcast.11, bf16[384,128,128]{2,1,0:T(8,128)(2,1)} %bitcast.17), custom_call_target="tpu_custom_call" | custom-call | flops 1000000000 | bytes 4000000 | tf_op jit(solution)/shard_map/forward_near/pallas_call | solution.py:348
  32.6 14.7 %all-to-all-done.1.recv_ref = bf16[32,160,128]{2,1,0:T(8,128)(2,1)S(1)} async-done(((bf16[32,160,128]{2,1,0:T(8,128)(2,1)}), bf16[32,160,128]{2,1,0:T(8,128)(2,1)S(1)}, u32[]{:S(2)}, u32[]{:S(2)}) %all-to-all-start.1) | async-done | bytes 1310752 | tf_op jit(solution)/shard_map/all_to_all | solution.py:609
  47.2 6.9 %forward_far.1 = (f32[4,128,128]{2,1,0:T(8,128)S(1)}, bf16[4,128,128]{2,1,0:T(8,128)(2,1)S(1)}, bf16[4,128,128]{2,1,0:T(8,128)(2,1)S(1)}, bf16[4,128,128]{2,1,0:T(8,128)(2,1)S(1)}) custom-call(s32[4,4,128]{2,1,0:T(4,128)S(1)} %get-tuple-element.18.plan_ref, s32[2]{0:T(128)S(1)} %pad_add_fusion.place_ref.rep_ref, f32[16,128,128]{2,1,0:T(8,128)S(1)} %forward_near.1.near_ref, ...), custom_call_target="tpu_custom_call" | custom-call | flops 4000000000 | bytes 12000000 | tf_op jit(solution)/shard_map/forward_far/pallas_call | solution.py:362
  54.2 1.5 %collective-permute-start = (bf16[4,128,128]{2,1,0:T(8,128)(2,1)S(1)}, bf16[4,128,128]{2,1,0:T(8,128)(2,1)S(1)}, u32[]{:S(2)}, u32[]{:S(2)}) collective-permute-start(bf16[4,128,128]{2,1,0:T(8,128)(2,1)S(1)} %get-tuple-element.20), channel_id=1, source_target_pairs={{0,32},{32,64},{64,96},{96,0},{1,33},{33,65},{65,97},{97,1},{2,34}... | collective-permute-start | bytes 393224 | tf_op jit(solution)/shard_map/ppermute | solution.py:601
  55.7 2.4 %collective-permute-start.1 = (bf16[4,128,128]{2,1,0:T(8,128)(2,1)S(1)}, bf16[4,128,128]{2,1,0:T(8,128)(2,1)S(1)}, u32[]{:S(2)}, u32[]{:S(2)}) collective-permute-start(bf16[4,128,128]{2,1,0:T(8,128)(2,1)S(1)} %get-tuple-element.21), channel_id=1, source_target_pairs={{0,64},{32,96},{64,0},{96,32},{1,65},{33,97},{65,1},{97,33},{2,66}... | collective-permute-start | bytes 393224 | tf_op jit(solution)/shard_map/ppermute | solution.py:601
  58.1 1.1 collective-permute-start.2
  59.1 0.2 collective-permute-done.a_ref
  59.3 2.8 %collective-permute-done.1.b_ref = bf16[4,128,128]{2,1,0:T(8,128)(2,1)S(1)} collective-permute-done((bf16[4,128,128]{2,1,0:T(8,128)(2,1)S(1)}, bf16[4,128,128]{2,1,0:T(8,128)(2,1)S(1)}, u32[]{:S(2)}, u32[]{:S(2)}) %collective-permute-start.1) | collective-permute-done | bytes 131104 | tf_op jit(solution)/shard_map/ppermute | solution.py:601
  62.1 1.0 collective-permute-done.2.c_ref
  63.1 0.1 sum_quarter.1.z0.after_ref
  63.2 0.0 copy-start.1
  63.2 0.0 copy-start.2
  63.2 0.0 copy-start.4
  63.2 1.8 %collective-permute-start.3 = (bf16[4,128,128]{2,1,0:T(8,128)(2,1)S(1)}, bf16[4,128,128]{2,1,0:T(8,128)(2,1)S(1)}, u32[]{:S(2)}, u32[]{:S(2)}) collective-permute-start(bf16[4,128,128]{2,1,0:T(8,128)(2,1)S(1)} %sum_quarter.1.z0.after_ref), channel_id=1, source_target_pairs={{0,32},{32,64},{64,96},{96,0},{1,33},{33,65},{65,97},{97,1},{2,34}... | collective-permute-start | bytes 393224 | tf_op jit(solution)/shard_map/ppermute | solution.py:601
  65.0 2.4 %collective-permute-start.4 = (bf16[4,128,128]{2,1,0:T(8,128)(2,1)S(1)}, bf16[4,128,128]{2,1,0:T(8,128)(2,1)S(1)}, u32[]{:S(2)}, u32[]{:S(2)}) collective-permute-start(bf16[4,128,128]{2,1,0:T(8,128)(2,1)S(1)} %sum_quarter.1.z0.after_ref), channel_id=1, source_target_pairs={{0,64},{32,96},{64,0},{96,32},{1,65},{33,97},{65,1},{97,33},{2,66}... | collective-permute-start | bytes 393224 | tf_op jit(solution)/shard_map/ppermute | solution.py:601
  67.4 1.0 collective-permute-start.5
  68.3 4.6 %hold_tiles.1.w_ref = bf16[384,128,128]{2,1,0:T(8,128)(2,1)S(1)} custom-call(bf16[384,128,128]{2,1,0:T(8,128)(2,1)} %bitcast.19, bf16[4,128,128]{2,1,0:T(8,128)(2,1)S(1)} %sum_quarter.1.z0.after_ref), custom_call_target="tpu_custom_call" | custom-call | bytes 13000000 | tf_op jit(solution)/shard_map/hold_tiles/pallas_call | solution.py:441
  72.9 0.0 collective-permute-done.3.z1
  73.0 3.4 %middle.1 = (bf16[2048,256]{1,0:T(8,128)(2,1)}, bf16[17,128,128]{2,1,0:T(8,128)(2,1)S(1)}, bf16[32,16,128]{2,1,0:T(8,128)(2,1)S(1)}) custom-call(s32[2]{0:T(128)S(1)} %pad_add_fusion.place_ref.rep_ref, bf16[4,128,128]{2,1,0:T(8,128)(2,1)S(1)} %sum_quarter.1.z0.after_ref, bf16[4,128,128]{2,1,0:T(8,128)(2,1)S(1)} %collective-permute-done.3.z1, ...), custom_call_target="tpu_custom_call" | custom-call | flops 5000000000 | bytes 3000000 | tf_op jit(solution)/shard_map/middle/pallas_call | solution.py:418
  76.4 6.3 %backward_far.1 = bf16[4,32,48,128]{3,2,1,0:T(8,128)(2,1)} custom-call(s32[4,4,128]{2,1,0:T(4,128)S(1)} %get-tuple-element.24.plan_ref, bf16[17,128,128]{2,1,0:T(8,128)(2,1)S(1)} %get-tuple-element.25.ys, bf16[32,16,128]{2,1,0:T(8,128)(2,1)S(1)} %get-tuple-element.26.gw_ref, bf16[384,128,128]{2,1,0:T(8,128)(2,1)S(1)} %hold_tiles.1.w_ref), custom_call_target="tpu_custom_call" | custom-call | flops 4000000000 | bytes 14000000 | tf_op jit(solution)/shard_map/backward_far/pallas_call | solution.py:476
  82.8 8.6 %all-to-all-start.2 = ((bf16[128,48,128]{2,1,0:T(8,128)(2,1)}), bf16[128,48,128]{2,1,0:T(8,128)(2,1)S(1)}, u32[]{:S(2)}, u32[]{:S(2)}) async-start(bf16[128,48,128]{2,1,0:T(8,128)(2,1)} %bitcast.7), calls=%async_computation.2 | async-start | bytes 3145728 | tf_op jit(solution)/shard_map/all_to_all | solution.py:609
  91.4 4.0 %backward_near.1 = (f32[16,32,128]{2,1,0:T(8,128)S(1)}, bf16[16,32,128]{2,1,0:T(8,128)(2,1)S(1)}, bf16[16,32,128]{2,1,0:T(8,128)(2,1)S(1)}, bf16[16,32,128]{2,1,0:T(8,128)(2,1)S(1)}) custom-call(s32[4,4,128]{2,1,0:T(4,128)S(1)} %get-tuple-element.24.plan_ref, s32[2]{0:T(128)S(1)} %pad_add_fusion.place_ref.rep_ref, ...), custom_call_target="tpu_custom_call" | custom-call | flops 1000000000 | bytes 14000000 | tf_op jit(solution)/shard_map/backward_near/pallas_call | solution.py:505
  95.4 0.0 copy-start.3
  95.4 1.5 %collective-permute-start.6 = (bf16[16,32,128]{2,1,0:T(8,128)(2,1)S(1)}, bf16[16,32,128]{2,1,0:T(8,128)(2,1)S(1)}, u32[]{:S(2)}, u32[]{:S(2)}) collective-permute-start(bf16[16,32,128]{2,1,0:T(8,128)(2,1)S(1)} %get-tuple-element.28), channel_id=1, source_target_pairs={{0,32},{32,64},{64,96},{96,0},{1,33},{33,65},{65,97},{97,1},{2,34}... | collective-permute-start | bytes 393224 | tf_op jit(solution)/shard_map/ppermute | solution.py:601
  96.9 2.4 %collective-permute-start.7 = (bf16[16,32,128]{2,1,0:T(8,128)(2,1)S(1)}, bf16[16,32,128]{2,1,0:T(8,128)(2,1)S(1)}, u32[]{:S(2)}, u32[]{:S(2)}) collective-permute-start(bf16[16,32,128]{2,1,0:T(8,128)(2,1)S(1)} %get-tuple-element.29), channel_id=1, source_target_pairs={{0,64},{32,96},{64,0},{96,32},{1,65},{33,97},{65,1},{97,33},{2,66}... | collective-permute-start | bytes 393224 | tf_op jit(solution)/shard_map/ppermute | solution.py:601
  99.3 1.2 collective-permute-start.8
  100.5 15.6 %all-to-all-done.2.recv_ref = bf16[128,48,128]{2,1,0:T(8,128)(2,1)S(1)} async-done(((bf16[128,48,128]{2,1,0:T(8,128)(2,1)}), bf16[128,48,128]{2,1,0:T(8,128)(2,1)S(1)}, u32[]{:S(2)}, u32[]{:S(2)}) %all-to-all-start.2) | async-done | bytes 1572896 | tf_op jit(solution)/shard_map/all_to_all | solution.py:609
  116.1 0.1 slice_reduce_fusion
  116.2 0.9 broadcast_in_dim.2
  117.1 4.7 %all-to-all-start.3 = ((bf16[128,16,128]{2,1,0:T(8,128)(2,1)}), bf16[128,16,128]{2,1,0:T(8,128)(2,1)S(1)}, u32[]{:S(2)}, u32[]{:S(2)}) async-start(bf16[128,16,128]{2,1,0:T(8,128)(2,1)} %broadcast_in_dim.2), calls=%async_computation.3 | async-start | bytes 1048576 | tf_op jit(solution)/shard_map/all_to_all | solution.py:609
  121.8 3.1 %scatter_rows.1.m0 = bf16[16,32,128]{2,1,0:T(8,128)(2,1)S(1)} custom-call(s32[1,32]{1,0:T(1,128)} %count_ref.3, s32[32,128]{1,0:T(8,128)S(1)} %bitcast.15, bf16[128,48,128]{2,1,0:T(8,128)(2,1)S(1)} %all-to-all-done.2.recv_ref, f32[16,32,128]{2,1,0:T(8,128)S(1)} %get-tuple-element.27.own_ref, bf16[16,32,128]{2,1,0:T(8,128)(2,1)S(1)} %collective-permute-done.6.a_ref, ...), custom_call_target="tpu_custom_call" | custom-call | flops 4000000000 | bytes 4000000 | tf_op jit(solution)/shard_map/scatter_rows/pallas_call | solution.py:550
  124.9 1.5 %collective-permute-start.9 = (bf16[16,32,128]{2,1,0:T(8,128)(2,1)S(1)}, bf16[16,32,128]{2,1,0:T(8,128)(2,1)S(1)}, u32[]{:S(2)}, u32[]{:S(2)}) collective-permute-start(bf16[16,32,128]{2,1,0:T(8,128)(2,1)S(1)} %scatter_rows.1.m0), channel_id=1, source_target_pairs={{0,32},{32,64},{64,96},{96,0},{1,33},{33,65},{65,97},{97,1},{2,34}... | collective-permute-start | bytes 393224 | tf_op jit(solution)/shard_map/ppermute | solution.py:601
  126.4 2.5 %collective-permute-start.10 = (bf16[16,32,128]{2,1,0:T(8,128)(2,1)S(1)}, bf16[16,32,128]{2,1,0:T(8,128)(2,1)S(1)}, u32[]{:S(2)}, u32[]{:S(2)}) collective-permute-start(bf16[16,32,128]{2,1,0:T(8,128)(2,1)S(1)} %scatter_rows.1.m0), channel_id=1, source_target_pairs={{0,64},{32,96},{64,0},{96,32},{1,65},{33,97},{65,1},{97,33},{2,66}... | collective-permute-start | bytes 393224 | tf_op jit(solution)/shard_map/ppermute | solution.py:601
  128.9 1.1 collective-permute-start.11
  130.1 4.0 %collective-permute-done.9.m1 = bf16[16,32,128]{2,1,0:T(8,128)(2,1)S(1)} collective-permute-done((bf16[16,32,128]{2,1,0:T(8,128)(2,1)S(1)}, bf16[16,32,128]{2,1,0:T(8,128)(2,1)S(1)}, u32[]{:S(2)}, u32[]{:S(2)}) %collective-permute-start.9) | collective-permute-done | bytes 131104 | tf_op jit(solution)/shard_map/ppermute | solution.py:601
  134.0 3.4 %collective-permute-done.10.m2 = bf16[16,32,128]{2,1,0:T(8,128)(2,1)S(1)} collective-permute-done((bf16[16,32,128]{2,1,0:T(8,128)(2,1)S(1)}, bf16[16,32,128]{2,1,0:T(8,128)(2,1)S(1)}, u32[]{:S(2)}, u32[]{:S(2)}) %collective-permute-start.10) | collective-permute-done | bytes 131104 | tf_op jit(solution)/shard_map/ppermute | solution.py:601
  137.5 2.1 %finish.1 = (f32[2048,128]{1,0:T(8,128)}, f32[128,256]{1,0:T(8,128)}) custom-call(s32[2]{0:T(128)S(1)} %pad_add_fusion.place_ref.rep_ref, s32[8]{0:T(128)} %hub_ref.5, bf16[16,32,128]{2,1,0:T(8,128)(2,1)S(1)} %scatter_rows.1.m0, bf16[16,32,128]{2,1,0:T(8,128)(2,1)S(1)} %collective-permute-done.9.m1, bf16[16,32,128]{2,1,0:T(8,128)(2,1)S(1)} %collective-permute-done.10.m2, ...), custom_call_target="tpu_custom_call" | custom-call | tf_op jit(solution)/shard_map/finish/pallas_call | solution.py:586
  (16 shorter events, 0.1 us)
Async XLA Ops:
  2.9 18.4 %all-to-all-start = ((bf16[32,32,128]{2,1,0:T(8,128)(2,1)}), bf16[32,32,128]{2,1,0:T(8,128)(2,1)S(1)}, u32[]{:S(2)}, u32[]{:S(2)}) async-start(bf16[32,32,128]{2,1,0:T(8,128)(2,1)} %bitcast.4), calls=%async_computation | async-start | bytes 524288 | tf_op jit(solution)/shard_map/all_to_all | solution.py:609
  22.8 4.6 %copy-start.5 = (s32[1,1,384]{2,1,0:T(1,128)S(1)}, s32[1,1,384]{2,1,0:T(1,128)}, u32[]{:S(2)}) copy-start(s32[1,1,384]{2,1,0:T(1,128)} %param.17) | copy-start | bytes 4612
  22.8 4.6 %copy-start.6 = (s32[1,1,384]{2,1,0:T(1,128)S(1)}, s32[1,1,384]{2,1,0:T(1,128)}, u32[]{:S(2)}) copy-start(s32[1,1,384]{2,1,0:T(1,128)} %param.18) | copy-start | bytes 4612
  22.9 5.8 %copy-start = (bf16[2048,128]{1,0:T(8,128)(2,1)S(1)}, bf16[2048,128]{1,0:T(8,128)(2,1)}, u32[]{:S(2)}) copy-start(bf16[2048,128]{1,0:T(8,128)(2,1)} %feat_hbm.1) | copy-start | bytes 1572868
  22.9 24.4 %all-to-all-start.1 = ((bf16[32,160,128]{2,1,0:T(8,128)(2,1)}), bf16[32,160,128]{2,1,0:T(8,128)(2,1)S(1)}, u32[]{:S(2)}, u32[]{:S(2)}) async-start(bf16[32,160,128]{2,1,0:T(8,128)(2,1)} %insert_hubs.1), calls=%async_computation.1 | async-start | bytes 2621440 | tf_op jit(solution)/shard_map/all_to_all | solution.py:609
  54.2 5.1 %collective-permute-start = (bf16[4,128,128]{2,1,0:T(8,128)(2,1)S(1)}, bf16[4,128,128]{2,1,0:T(8,128)(2,1)S(1)}, u32[]{:S(2)}, u32[]{:S(2)}) collective-permute-start(bf16[4,128,128]{2,1,0:T(8,128)(2,1)S(1)} %get-tuple-element.20), channel_id=1, source_target_pairs={{0,32},{32,64},{64,96},{96,0},{1,33},{33,65},{65,97},{97,1},{2,34}... | collective-permute-start | bytes 393224 | tf_op jit(solution)/shard_map/ppermute | solution.py:601
  55.7 6.5 %collective-permute-start.1 = (bf16[4,128,128]{2,1,0:T(8,128)(2,1)S(1)}, bf16[4,128,128]{2,1,0:T(8,128)(2,1)S(1)}, u32[]{:S(2)}, u32[]{:S(2)}) collective-permute-start(bf16[4,128,128]{2,1,0:T(8,128)(2,1)S(1)} %get-tuple-element.21), channel_id=1, source_target_pairs={{0,64},{32,96},{64,0},{96,32},{1,65},{33,97},{65,1},{97,33},{2,66}... | collective-permute-start | bytes 393224 | tf_op jit(solution)/shard_map/ppermute | solution.py:601
  58.1 5.0 %collective-permute-start.2 = (bf16[4,128,128]{2,1,0:T(8,128)(2,1)S(1)}, bf16[4,128,128]{2,1,0:T(8,128)(2,1)S(1)}, u32[]{:S(2)}, u32[]{:S(2)}) collective-permute-start(bf16[4,128,128]{2,1,0:T(8,128)(2,1)S(1)} %get-tuple-element.22), channel_id=1, source_target_pairs={{0,96},{32,0},{64,32},{96,64},{1,97},{33,1},{65,33},{97,65},{2,98}... | collective-permute-start | bytes 393224 | tf_op jit(solution)/shard_map/ppermute | solution.py:601
  63.2 9.8 %copy-start.1 = (bf16[2048,256]{1,0:T(8,128)(2,1)S(1)}, bf16[2048,256]{1,0:T(8,128)(2,1)}, u32[]{:S(2)}) copy-start(bf16[2048,256]{1,0:T(8,128)(2,1)} %cot_ref.1) | copy-start | bytes 3145732
  63.2 9.8 %copy-start.2 = (bf16[128,256]{1,0:T(8,128)(2,1)S(1)}, bf16[128,256]{1,0:T(8,128)(2,1)}, u32[]{:S(2)}) copy-start(bf16[128,256]{1,0:T(8,128)(2,1)} %w_ref.1) | copy-start | bytes 196612
  63.2 9.8 %copy-start.4 = (f32[256]{0:T(256)S(1)}, f32[256]{0:T(256)}, u32[]{:S(2)}) copy-start(f32[256]{0:T(256)} %param.12) | copy-start | bytes 3076
  63.2 9.8 %collective-permute-start.3 = (bf16[4,128,128]{2,1,0:T(8,128)(2,1)S(1)}, bf16[4,128,128]{2,1,0:T(8,128)(2,1)S(1)}, u32[]{:S(2)}, u32[]{:S(2)}) collective-permute-start(bf16[4,128,128]{2,1,0:T(8,128)(2,1)S(1)} %sum_quarter.1.z0.after_ref), channel_id=1, source_target_pairs={{0,32},{32,64},{64,96},{96,0},{1,33},{33,65},{65,97},{97,1},{2,34}... | collective-permute-start | bytes 393224 | tf_op jit(solution)/shard_map/ppermute | solution.py:601
  65.0 7.9 %collective-permute-start.4 = (bf16[4,128,128]{2,1,0:T(8,128)(2,1)S(1)}, bf16[4,128,128]{2,1,0:T(8,128)(2,1)S(1)}, u32[]{:S(2)}, u32[]{:S(2)}) collective-permute-start(bf16[4,128,128]{2,1,0:T(8,128)(2,1)S(1)} %sum_quarter.1.z0.after_ref), channel_id=1, source_target_pairs={{0,64},{32,96},{64,0},{96,32},{1,65},{33,97},{65,1},{97,33},{2,66}... | collective-permute-start | bytes 393224 | tf_op jit(solution)/shard_map/ppermute | solution.py:601
  67.4 5.6 %collective-permute-start.5 = (bf16[4,128,128]{2,1,0:T(8,128)(2,1)S(1)}, bf16[4,128,128]{2,1,0:T(8,128)(2,1)S(1)}, u32[]{:S(2)}, u32[]{:S(2)}) collective-permute-start(bf16[4,128,128]{2,1,0:T(8,128)(2,1)S(1)} %sum_quarter.1.z0.after_ref), channel_id=1, source_target_pairs={{0,96},{32,0},{64,32},{96,64},{1,97},{33,1},{65,33},{97,65},{2,98}... | collective-permute-start | bytes 393224 | tf_op jit(solution)/shard_map/ppermute | solution.py:601
  82.8 33.3 %all-to-all-start.2 = ((bf16[128,48,128]{2,1,0:T(8,128)(2,1)}), bf16[128,48,128]{2,1,0:T(8,128)(2,1)S(1)}, u32[]{:S(2)}, u32[]{:S(2)}) async-start(bf16[128,48,128]{2,1,0:T(8,128)(2,1)} %bitcast.7), calls=%async_computation.2 | async-start | bytes 3145728 | tf_op jit(solution)/shard_map/all_to_all | solution.py:609
  95.4 26.4 %copy-start.3 = (s32[1,32,128]{2,1,0:T(8,128)S(1)}, s32[1,32,128]{2,1,0:T(8,128)}, u32[]{:S(2)}) copy-start(s32[1,32,128]{2,1,0:T(8,128)} %param.14) | copy-start | bytes 49156
  95.4 26.3 %collective-permute-start.6 = (bf16[16,32,128]{2,1,0:T(8,128)(2,1)S(1)}, bf16[16,32,128]{2,1,0:T(8,128)(2,1)S(1)}, u32[]{:S(2)}, u32[]{:S(2)}) collective-permute-start(bf16[16,32,128]{2,1,0:T(8,128)(2,1)S(1)} %get-tuple-element.28), channel_id=1, source_target_pairs={{0,32},{32,64},{64,96},{96,0},{1,33},{33,65},{65,97},{97,1},{2,34}... | collective-permute-start | bytes 393224 | tf_op jit(solution)/shard_map/ppermute | solution.py:601
  96.9 24.9 %collective-permute-start.7 = (bf16[16,32,128]{2,1,0:T(8,128)(2,1)S(1)}, bf16[16,32,128]{2,1,0:T(8,128)(2,1)S(1)}, u32[]{:S(2)}, u32[]{:S(2)}) collective-permute-start(bf16[16,32,128]{2,1,0:T(8,128)(2,1)S(1)} %get-tuple-element.29), channel_id=1, source_target_pairs={{0,64},{32,96},{64,0},{96,32},{1,65},{33,97},{65,1},{97,33},{2,66}... | collective-permute-start | bytes 393224 | tf_op jit(solution)/shard_map/ppermute | solution.py:601
  99.3 22.5 %collective-permute-start.8 = (bf16[16,32,128]{2,1,0:T(8,128)(2,1)S(1)}, bf16[16,32,128]{2,1,0:T(8,128)(2,1)S(1)}, u32[]{:S(2)}, u32[]{:S(2)}) collective-permute-start(bf16[16,32,128]{2,1,0:T(8,128)(2,1)S(1)} %get-tuple-element.30), channel_id=1, source_target_pairs={{0,96},{32,0},{64,32},{96,64},{1,97},{33,1},{65,33},{97,65},{2,98}... | collective-permute-start | bytes 393224 | tf_op jit(solution)/shard_map/ppermute | solution.py:601
  117.1 20.4 %all-to-all-start.3 = ((bf16[128,16,128]{2,1,0:T(8,128)(2,1)}), bf16[128,16,128]{2,1,0:T(8,128)(2,1)S(1)}, u32[]{:S(2)}, u32[]{:S(2)}) async-start(bf16[128,16,128]{2,1,0:T(8,128)(2,1)} %broadcast_in_dim.2), calls=%async_computation.3 | async-start | bytes 1048576 | tf_op jit(solution)/shard_map/all_to_all | solution.py:609
  124.9 9.1 %collective-permute-start.9 = (bf16[16,32,128]{2,1,0:T(8,128)(2,1)S(1)}, bf16[16,32,128]{2,1,0:T(8,128)(2,1)S(1)}, u32[]{:S(2)}, u32[]{:S(2)}) collective-permute-start(bf16[16,32,128]{2,1,0:T(8,128)(2,1)S(1)} %scatter_rows.1.m0), channel_id=1, source_target_pairs={{0,32},{32,64},{64,96},{96,0},{1,33},{33,65},{65,97},{97,1},{2,34}... | collective-permute-start | bytes 393224 | tf_op jit(solution)/shard_map/ppermute | solution.py:601
  126.4 11.1 %collective-permute-start.10 = (bf16[16,32,128]{2,1,0:T(8,128)(2,1)S(1)}, bf16[16,32,128]{2,1,0:T(8,128)(2,1)S(1)}, u32[]{:S(2)}, u32[]{:S(2)}) collective-permute-start(bf16[16,32,128]{2,1,0:T(8,128)(2,1)S(1)} %scatter_rows.1.m0), channel_id=1, source_target_pairs={{0,64},{32,96},{64,0},{96,32},{1,65},{33,97},{65,1},{97,33},{2,66}... | collective-permute-start | bytes 393224 | tf_op jit(solution)/shard_map/ppermute | solution.py:601
  128.9 8.5 %collective-permute-start.11 = (bf16[16,32,128]{2,1,0:T(8,128)(2,1)S(1)}, bf16[16,32,128]{2,1,0:T(8,128)(2,1)S(1)}, u32[]{:S(2)}, u32[]{:S(2)}) collective-permute-start(bf16[16,32,128]{2,1,0:T(8,128)(2,1)S(1)} %scatter_rows.1.m0), channel_id=1, source_target_pairs={{0,96},{32,0},{64,32},{96,64},{1,97},{33,1},{65,33},{97,65},{2,98}... | collective-permute-start | bytes 393224 | tf_op jit(solution)/shard_map/ppermute | solution.py:601

commit v5 on v4

--- a/solution.py
+++ b/solution.py
@@ -101,12 +101,15 @@
         here = lane + s * BLK
         tile = jnp.zeros((1, BLK), F32)
         block = jnp.zeros((1, BLK), F32)
+        taken = jnp.zeros((1, BLK), F32)
         for i in range(parts):
             hit = places[i] == here
+            taken = taken + jnp.sum(jnp.where(hit, 1.0, 0.0), axis=0, keepdims=True)
             tile = tile + jnp.sum(jnp.where(hit, (sub + i * BLK).astype(F32), 0.0), axis=0, keepdims=True)
             block = block + jnp.sum(jnp.where(hit, shifted[i], 0.0), axis=0, keepdims=True)
         inside = (begin <= here) & (here < end)
         out = jnp.sum(jnp.where(inside, out_of(sub).astype(F32), 0.0), axis=0, keepdims=True)
+        tile = tile + (1.0 - taken) * (here[:1] & 255).astype(F32)
         tiles.append(tile.astype(jnp.int32))
         blocks.append(block.astype(jnp.int32) + empty)
         outs.append(out.astype(jnp.int32))
@@ -262,33 +265,37 @@
     )(in_hbm(rows), counts, in_hbm(features))
 
 
-def hub_pick_kernel(hub_ref, feat_hbm, out_ref, sem):
-    copies = []
+def hub_pick_kernel(place_ref, hub_ref, feat_ref, out_ref):
     for h in range(HUBS):
-        block = hub_ref[h] & (LOCAL - 1)
-        copies.append(pltpu.make_async_copy(feat_hbm.at[block], out_ref.at[h], sem.at[h]))
-    for copy in copies:
-        copy.start()
-    for copy in copies:
-        copy.wait()
-
-
-def pick_hubs(hubs, features):
+        block = hub_ref[h]
+        mine = lax.shift_right_logical(block, 4) == place_ref[1]
+
+        @pl.when(mine)
+        def _():
+            out_ref[h] = feat_ref[block & (LOCAL - 1)]
+
+        @pl.when(jnp.logical_not(mine))
+        def _():
+            out_ref[h] = jnp.zeros((BLK, FIN), BF16)
+
+
+def pick_hubs(place, hubs, features):
     return pl.pallas_call(
         hub_pick_kernel,
         out_shape=jax.ShapeDtypeStruct((HUBS, BLK, FIN), BF16),
-        in_specs=[SM, FAR],
+        in_specs=[SM, SM, VM],
         out_specs=VM,
-        scratch_shapes=[pltpu.SemaphoreType.DMA((HUBS,))],
         compiler_params=PARAMS,
         name="pick_hubs",
-    )(hubs, in_hbm(features))
-
-
-def insert_kernel(place_ref, hub_ref, spread_ref, listed_ref, out_ref, wide, sem):
+    )(place, hubs, in_hbm(features))
+
+
+def insert_kernel(spread_ref, listed_ref, out_ref, wide, sem):
     del listed_ref
-    owner = lax.shift_right_logical(hub_ref[place_ref[1] // (BLK // HUB_ROWS)], 4)
-    piece = spread_ref[owner]
+    piece = spread_ref[0].astype(F32)
+    for p in range(1, N_DOM):
+        piece = piece + spread_ref[p].astype(F32)
+    piece = piece.astype(BF16)
     for p in range(N_DOM):
         wide[p] = piece
     copy = pltpu.make_async_copy(wide, out_ref.at[:, pl.ds(BLK, HUB_ROWS), :], sem)
@@ -296,17 +303,17 @@
     copy.wait()
 
 
-def insert_hubs(place, hubs, spread, listed):
+def insert_hubs(spread, listed):
     return pl.pallas_call(
         insert_kernel,
         out_shape=jax.ShapeDtypeStruct(listed.shape, BF16),
-        in_specs=[SM, SM, VM, pl.BlockSpec(memory_space=pl.ANY)],
+        in_specs=[VM, pl.BlockSpec(memory_space=pl.ANY)],
         out_specs=pl.BlockSpec(memory_space=pl.ANY),
         scratch_shapes=[pltpu.VMEM((N_DOM, HUB_ROWS, FIN), BF16), pltpu.SemaphoreType.DMA],
-        input_output_aliases={3: 0},
+        input_output_aliases={1: 0},
         compiler_params=PARAMS,
         name="insert_hubs",
-    )(place, hubs, spread, listed)
+    )(spread, listed)
 
 
 def forward_product(xs):
@@ -394,12 +401,13 @@
         quarter = lax.rem(place_ref[0] + N_REP - turned, N_REP)
         zx = ref[...].reshape(QUARTER, FIN)
         pre = dot(zx, weight) + bias_ref[...]
-        square = pre * pre
-        bent = jnp.tanh(root * (pre + 0.044715 * (square * pre)))
-        cdf = 0.5 * (1.0 + bent)
+        cubic = (root * 0.044715) * (pre * pre)
+        bent = jnp.tanh(pre * (root + cubic))
+        half = 0.5 * pre
+        cdf = 0.5 * bent + 0.5
         rows = pl.ds(pl.multiple_of(quarter * QUARTER, QUARTER), QUARTER)
-        out_ref[rows, :] = (pre * cdf).astype(BF16)
-        slope = cdf + (0.5 * pre) * ((1.0 - bent * bent) * (root * (1.0 + (3 * 0.044715) * square)))
+        out_ref[rows, :] = (half * bent + half).astype(BF16)
+        slope = cdf + half * ((1.0 - bent * bent) * (root + 3.0 * cubic))
         pre_grad = (cot_ref[rows, :].astype(F32) * slope).astype(BF16)
         yt = lax.dot_general(weight, pre_grad, (((1,), (1,)), ((), ())), preferred_element_type=F32)
         yt = yt.astype(BF16)
@@ -629,18 +637,19 @@
     rows = send_rows[0]
 
     weights = tile_weight[0, 0]
-    spread = swap(pick_hubs(hub_blocks, blocks).reshape(N_DOM, HUB_ROWS, FIN), "dom")
+    spread = swap(pick_hubs(place, hub_blocks, blocks).reshape(N_DOM, HUB_ROWS, FIN), "dom")
     listed = gather_rows(rows, send_count, features)
-    received = swap(insert_hubs(place, hub_blocks, spread, listed), "dom")
+    received = swap(insert_hubs(spread, listed), "dom")
     fwd, bwd = order_tiles(
         tile_dst[0, 0].reshape(TILES // BLK, BLK), tile_src[0, 0].reshape(TILES // BLK, BLK)
     )
     stored = in_hbm(weights)
     near = forward_near(fwd, blocks, stored)
     own, s1, s2, s3 = forward_far(fwd, place, near, received, stored)
+    held = hold_tiles(stored, s1)
     a, b, c = turn(s1, 1), turn(s2, 2), turn(s3, 3)
+    a, held = lax.optimization_barrier((a, held))
     zq = sum_quarter(own, a, b, c)
-    held = hold_tiles(stored, zq)
     output, ys, gw = middle(place, around(zq), proj_weight, bias.reshape(1, HID), cotangent)
     message = backward_far(bwd, ys, gw, held)
     returned = swap(message.reshape(N_REP * N_DOM, MSG, BLK), ("rep", "dom"))

time: 141 us -> 138 us (0.979)
  starting transfers between devices: 47.6 us -> 45 us
    all_to_all x4, starting transfers between devices: 27.3 us -> 24.8 us  [swap(): return lax.all_to_all(value, axes, split_axis=0, concat_axis=0, tiled=True)]
where the time goes in v5:
time: 138 us
  waiting for transfers between devices  45.5 us (33%)
  Pallas kernels  45.2 us (33%)
  starting transfers between devices  45 us (33%)
    all_to_all x4, waiting for transfers between devices, swap(): return lax.all_to_all(value, axes, split_axis=0, concat_axis=0, tiled=True)  33.3 us
    all_to_all x4, starting transfers between devices, swap(): return lax.all_to_all(value, axes, split_axis=0, concat_axis=0, tiled=True)  24.8 us
    ppermute x12, starting transfers between devices, turn(): lax.ppermute(value, 'rep', [(i, (i + k) % N_REP) for i in range(N_REP)])  20.2 us
    ppermute x12, waiting for transfers between devices, turn(): lax.ppermute(value, 'rep', [(i, (i + k) % N_REP) for i in range(N_REP)])  12.1 us
    pallas_call x1, Pallas kernels, forward_far(): pl.pallas_call(forward_far_kernel, out_shape=[jax.ShapeDtypeStruct(quarte...  7.45 us
    pallas_call x1, Pallas kernels, backward_far(): pl.pallas_call(backward_far_kernel, out_shape=jax.ShapeDtypeStruct((N_REP...  6.81 us
    pallas_call x1, Pallas kernels, gather_rows(): pl.pallas_call(gather_kernel, out_shape=jax.ShapeDtypeStruct((N_DOM, BLK...  5.93 us
    pallas_call x1, Pallas kernels, hold_tiles(): pl.pallas_call(hold_kernel, out_shape=pltpu.VMEM((TILES, BLK, BLK), BF16)...  4.58 us
  transfers between devices with their start and end apart: 16, of which 8 were waited for; matrix products, arithmetic and copies ran while one was open for 1% of the time, Pallas kernels for 16%

profile of v5, /device:TPU:1, one launch (start us, length us, event | category | flops | bytes accessed | tf_op | source)
XLA Modules:
  0.0 137.7 jit_solution(8559960536099132601)
XLA Ops:
  0.6 0.1 pad_add_fusion.place_ref.rep_ref
  0.7 1.9 %pick_hubs.1 = bf16[8,128,128]{2,1,0:T(8,128)(2,1)} custom-call(s32[2]{0:T(128)S(1)} %pad_add_fusion.place_ref.rep_ref, s32[8]{0:T(128)} %hub_ref.3, bf16[16,128,128]{2,1,0:T(8,128)(2,1)} %bitcast.10), custom_call_target="tpu_custom_call" | custom-call | tf_op jit(solution)/shard_map/pick_hubs/pallas_call | solution.py:283
  2.6 9.4 %all-to-all-start = ((bf16[32,32,128]{2,1,0:T(8,128)(2,1)}), bf16[32,32,128]{2,1,0:T(8,128)(2,1)S(1)}, u32[]{:S(2)}, u32[]{:S(2)}) async-start(bf16[32,32,128]{2,1,0:T(8,128)(2,1)} %bitcast.4), calls=%async_computation | async-start | bytes 524288 | tf_op jit(solution)/shard_map/all_to_all | solution.py:617
  12.0 5.9 %gather_rows.1.listed_ref = bf16[32,160,128]{2,1,0:T(8,128)(2,1)} custom-call(s32[32,128]{1,0:T(8,128)} %bitcast.14, s32[1,32]{1,0:T(1,128)} %count_ref.3, bf16[2048,128]{1,0:T(8,128)(2,1)} %feat_hbm.1), custom_call_target="tpu_custom_call" | custom-call | flops 4000000000 | bytes 2000000 | tf_op jit(solution)/shard_map/gather_rows/pallas_call | solution.py:252
  18.0 3.1 %all-to-all-done.spread_ref = bf16[32,32,128]{2,1,0:T(8,128)(2,1)S(1)} async-done(((bf16[32,32,128]{2,1,0:T(8,128)(2,1)}), bf16[32,32,128]{2,1,0:T(8,128)(2,1)S(1)}, u32[]{:S(2)}, u32[]{:S(2)}) %all-to-all-start) | async-done | bytes 262176 | tf_op jit(solution)/shard_map/all_to_all | solution.py:617
  21.0 0.8 insert_hubs.1
  21.8 0.0 copy-start.5
  21.8 0.0 copy-start.6
  21.8 0.0 copy-start
  21.8 4.5 %all-to-all-start.1 = ((bf16[32,160,128]{2,1,0:T(8,128)(2,1)}), bf16[32,160,128]{2,1,0:T(8,128)(2,1)S(1)}, u32[]{:S(2)}, u32[]{:S(2)}) async-start(bf16[32,160,128]{2,1,0:T(8,128)(2,1)} %insert_hubs.1), calls=%async_computation.1 | async-start | bytes 2621440 | tf_op jit(solution)/shard_map/all_to_all | solution.py:617
  26.4 1.3 order_tiles.1
  27.7 3.8 %forward_near.1.near_ref = f32[16,128,128]{2,1,0:T(8,128)S(1)} custom-call(s32[4,4,128]{2,1,0:T(4,128)S(1)} %get-tuple-element.20.plan_ref, bf16[16,128,128]{2,1,0:T(8,128)(2,1)S(1)} %bitcast.11, bf16[384,128,128]{2,1,0:T(8,128)(2,1)} %bitcast.17), custom_call_target="tpu_custom_call" | custom-call | flops 1000000000 | bytes 4000000 | tf_op jit(solution)/shard_map/forward_near/pallas_call | solution.py:355
  31.5 14.6 %all-to-all-done.1.recv_ref = bf16[32,160,128]{2,1,0:T(8,128)(2,1)S(1)} async-done(((bf16[32,160,128]{2,1,0:T(8,128)(2,1)}), bf16[32,160,128]{2,1,0:T(8,128)(2,1)S(1)}, u32[]{:S(2)}, u32[]{:S(2)}) %all-to-all-start.1) | async-done | bytes 1310752 | tf_op jit(solution)/shard_map/all_to_all | solution.py:617
  46.1 7.5 %forward_far.1 = (f32[4,128,128]{2,1,0:T(8,128)S(1)}, bf16[4,128,128]{2,1,0:T(8,128)(2,1)S(1)}, bf16[4,128,128]{2,1,0:T(8,128)(2,1)S(1)}, bf16[4,128,128]{2,1,0:T(8,128)(2,1)S(1)}) custom-call(s32[4,4,128]{2,1,0:T(4,128)S(1)} %get-tuple-element.20.plan_ref, s32[2]{0:T(128)S(1)} %pad_add_fusion.place_ref.rep_ref, f32[16,128,128]{2,1,0:T(8,128)S(1)} %forward_near.1.near_ref, ...), custom_call_target="tpu_custom_call" | custom-call | flops 4000000000 | bytes 12000000 | tf_op jit(solution)/shard_map/forward_far/pallas_call | solution.py:369
  53.6 0.8 collective-permute-start
  54.3 2.7 %collective-permute-start.1 = (bf16[4,128,128]{2,1,0:T(8,128)(2,1)S(1)}, bf16[4,128,128]{2,1,0:T(8,128)(2,1)S(1)}, u32[]{:S(2)}, u32[]{:S(2)}) collective-permute-start(bf16[4,128,128]{2,1,0:T(8,128)(2,1)S(1)} %get-tuple-element.24), channel_id=1, source_target_pairs={{0,64},{32,96},{64,0},{96,32},{1,65},{33,97},{65,1},{97,33},{2,66}... | collective-permute-start | bytes 393224 | tf_op jit(solution)/shard_map/ppermute | solution.py:609
  57.0 1.6 %collective-permute-start.2 = (bf16[4,128,128]{2,1,0:T(8,128)(2,1)S(1)}, bf16[4,128,128]{2,1,0:T(8,128)(2,1)S(1)}, u32[]{:S(2)}, u32[]{:S(2)}) collective-permute-start(bf16[4,128,128]{2,1,0:T(8,128)(2,1)S(1)} %get-tuple-element.25), channel_id=1, source_target_pairs={{0,96},{32,0},{64,32},{96,64},{1,97},{33,1},{65,33},{97,65},{2,98}... | collective-permute-start | bytes 393224 | tf_op jit(solution)/shard_map/ppermute | solution.py:609
  58.6 4.6 %hold_tiles.1.w_ref = bf16[384,128,128]{2,1,0:T(8,128)(2,1)S(1)} custom-call(bf16[384,128,128]{2,1,0:T(8,128)(2,1)} %bitcast.19, bf16[4,128,128]{2,1,0:T(8,128)(2,1)S(1)} %get-tuple-element.22.after_ref), custom_call_target="tpu_custom_call" | custom-call | bytes 13000000 | tf_op jit(solution)/shard_map/hold_tiles/pallas_call | solution.py:449
  63.2 0.0 collective-permute-done.a_ref
  63.2 0.1 collective-permute-done.2.c_ref
  63.3 0.1 sum_quarter.1.z0
  63.4 1.2 collective-permute-start.3
  64.6 2.6 %collective-permute-start.4 = (bf16[4,128,128]{2,1,0:T(8,128)(2,1)S(1)}, bf16[4,128,128]{2,1,0:T(8,128)(2,1)S(1)}, u32[]{:S(2)}, u32[]{:S(2)}) collective-permute-start(bf16[4,128,128]{2,1,0:T(8,128)(2,1)S(1)} %sum_quarter.1.z0), channel_id=1, source_target_pairs={{0,64},{32,96},{64,0},{96,32},{1,65},{33,97},{65,1},{97,33},{2,66}... | collective-permute-start | bytes 393224 | tf_op jit(solution)/shard_map/ppermute | solution.py:609
  67.2 1.2 collective-permute-start.5
  68.4 0.1 collective-permute-done.3.z1
  68.5 4.5 %collective-permute-done.4.z2 = bf16[4,128,128]{2,1,0:T(8,128)(2,1)S(1)} collective-permute-done((bf16[4,128,128]{2,1,0:T(8,128)(2,1)S(1)}, bf16[4,128,128]{2,1,0:T(8,128)(2,1)S(1)}, u32[]{:S(2)}, u32[]{:S(2)}) %collective-permute-start.4) | collective-permute-done | bytes 131104 | tf_op jit(solution)/shard_map/ppermute | solution.py:609
  73.0 0.0 collective-permute-done.5.z3
  73.0 3.5 %middle.1 = (bf16[2048,256]{1,0:T(8,128)(2,1)}, bf16[17,128,128]{2,1,0:T(8,128)(2,1)S(1)}, bf16[32,16,128]{2,1,0:T(8,128)(2,1)S(1)}) custom-call(s32[2]{0:T(128)S(1)} %pad_add_fusion.place_ref.rep_ref, bf16[4,128,128]{2,1,0:T(8,128)(2,1)S(1)} %sum_quarter.1.z0, bf16[4,128,128]{2,1,0:T(8,128)(2,1)S(1)} %collective-permute-done.3.z1, ...), custom_call_target="tpu_custom_call" | custom-call | flops 5000000000 | bytes 3000000 | tf_op jit(solution)/shard_map/middle/pallas_call | solution.py:426
  76.5 6.8 %backward_far.1 = bf16[4,32,48,128]{3,2,1,0:T(8,128)(2,1)} custom-call(s32[4,4,128]{2,1,0:T(4,128)S(1)} %get-tuple-element.27.plan_ref, bf16[17,128,128]{2,1,0:T(8,128)(2,1)S(1)} %get-tuple-element.28.ys, bf16[32,16,128]{2,1,0:T(8,128)(2,1)S(1)} %get-tuple-element.29.gw_ref, bf16[384,128,128]{2,1,0:T(8,128)(2,1)S(1)} %hold_tiles.1.w_ref), custom_call_target="tpu_custom_call" | custom-call | flops 4000000000 | bytes 14000000 | tf_op jit(solution)/shard_map/backward_far/pallas_call | solution.py:484
  83.3 6.2 %all-to-all-start.2 = ((bf16[128,48,128]{2,1,0:T(8,128)(2,1)}), bf16[128,48,128]{2,1,0:T(8,128)(2,1)S(1)}, u32[]{:S(2)}, u32[]{:S(2)}) async-start(bf16[128,48,128]{2,1,0:T(8,128)(2,1)} %bitcast.7), calls=%async_computation.2 | async-start | bytes 3145728 | tf_op jit(solution)/shard_map/all_to_all | solution.py:617
  89.5 4.0 %backward_near.1 = (f32[16,32,128]{2,1,0:T(8,128)S(1)}, bf16[16,32,128]{2,1,0:T(8,128)(2,1)S(1)}, bf16[16,32,128]{2,1,0:T(8,128)(2,1)S(1)}, bf16[16,32,128]{2,1,0:T(8,128)(2,1)S(1)}) custom-call(s32[4,4,128]{2,1,0:T(4,128)S(1)} %get-tuple-element.27.plan_ref, s32[2]{0:T(128)S(1)} %pad_add_fusion.place_ref.rep_ref, ...), custom_call_target="tpu_custom_call" | custom-call | flops 1000000000 | bytes 14000000 | tf_op jit(solution)/shard_map/backward_near/pallas_call | solution.py:513
  93.5 0.0 copy-start.3
  93.5 1.4 %collective-permute-start.6 = (bf16[16,32,128]{2,1,0:T(8,128)(2,1)S(1)}, bf16[16,32,128]{2,1,0:T(8,128)(2,1)S(1)}, u32[]{:S(2)}, u32[]{:S(2)}) collective-permute-start(bf16[16,32,128]{2,1,0:T(8,128)(2,1)S(1)} %get-tuple-element.32), channel_id=1, source_target_pairs={{0,32},{32,64},{64,96},{96,0},{1,33},{33,65},{65,97},{97,1},{2,34}... | collective-permute-start | bytes 393224 | tf_op jit(solution)/shard_map/ppermute | solution.py:609
  94.9 2.5 %collective-permute-start.7 = (bf16[16,32,128]{2,1,0:T(8,128)(2,1)S(1)}, bf16[16,32,128]{2,1,0:T(8,128)(2,1)S(1)}, u32[]{:S(2)}, u32[]{:S(2)}) collective-permute-start(bf16[16,32,128]{2,1,0:T(8,128)(2,1)S(1)} %get-tuple-element.33), channel_id=1, source_target_pairs={{0,64},{32,96},{64,0},{96,32},{1,65},{33,97},{65,1},{97,33},{2,66}... | collective-permute-start | bytes 393224 | tf_op jit(solution)/shard_map/ppermute | solution.py:609
  97.4 1.1 collective-permute-start.8
  98.5 15.7 %all-to-all-done.2.recv_ref = bf16[128,48,128]{2,1,0:T(8,128)(2,1)S(1)} async-done(((bf16[128,48,128]{2,1,0:T(8,128)(2,1)}), bf16[128,48,128]{2,1,0:T(8,128)(2,1)S(1)}, u32[]{:S(2)}, u32[]{:S(2)}) %all-to-all-start.2) | async-done | bytes 1572896 | tf_op jit(solution)/shard_map/all_to_all | solution.py:617
  114.2 0.1 slice_reduce_fusion
  114.4 0.9 broadcast_in_dim.2
  115.2 4.7 %all-to-all-start.3 = ((bf16[128,16,128]{2,1,0:T(8,128)(2,1)}), bf16[128,16,128]{2,1,0:T(8,128)(2,1)S(1)}, u32[]{:S(2)}, u32[]{:S(2)}) async-start(bf16[128,16,128]{2,1,0:T(8,128)(2,1)} %broadcast_in_dim.2), calls=%async_computation.3 | async-start | bytes 1048576 | tf_op jit(solution)/shard_map/all_to_all | solution.py:617
  119.9 0.0 collective-permute-done.7.b_ref
  119.9 0.0 collective-permute-done.8.c_ref
  119.9 3.1 %scatter_rows.1.m0 = bf16[16,32,128]{2,1,0:T(8,128)(2,1)S(1)} custom-call(s32[1,32]{1,0:T(1,128)} %count_ref.3, s32[32,128]{1,0:T(8,128)S(1)} %bitcast.15, bf16[128,48,128]{2,1,0:T(8,128)(2,1)S(1)} %all-to-all-done.2.recv_ref, f32[16,32,128]{2,1,0:T(8,128)S(1)} %get-tuple-element.31.own_ref, bf16[16,32,128]{2,1,0:T(8,128)(2,1)S(1)} %collective-permute-done.6.a_ref, ...), custom_call_target="tpu_custom_call" | custom-call | flops 4000000000 | bytes 4000000 | tf_op jit(solution)/shard_map/scatter_rows/pallas_call | solution.py:558
  123.0 1.5 %collective-permute-start.9 = (bf16[16,32,128]{2,1,0:T(8,128)(2,1)S(1)}, bf16[16,32,128]{2,1,0:T(8,128)(2,1)S(1)}, u32[]{:S(2)}, u32[]{:S(2)}) collective-permute-start(bf16[16,32,128]{2,1,0:T(8,128)(2,1)S(1)} %scatter_rows.1.m0), channel_id=1, source_target_pairs={{0,32},{32,64},{64,96},{96,0},{1,33},{33,65},{65,97},{97,1},{2,34}... | collective-permute-start | bytes 393224 | tf_op jit(solution)/shard_map/ppermute | solution.py:609
  124.5 2.5 %collective-permute-start.10 = (bf16[16,32,128]{2,1,0:T(8,128)(2,1)S(1)}, bf16[16,32,128]{2,1,0:T(8,128)(2,1)S(1)}, u32[]{:S(2)}, u32[]{:S(2)}) collective-permute-start(bf16[16,32,128]{2,1,0:T(8,128)(2,1)S(1)} %scatter_rows.1.m0), channel_id=1, source_target_pairs={{0,64},{32,96},{64,0},{96,32},{1,65},{33,97},{65,1},{97,33},{2,66}... | collective-permute-start | bytes 393224 | tf_op jit(solution)/shard_map/ppermute | solution.py:609
  127.1 1.1 collective-permute-start.11
  128.2 4.0 %collective-permute-done.9.m1 = bf16[16,32,128]{2,1,0:T(8,128)(2,1)S(1)} collective-permute-done((bf16[16,32,128]{2,1,0:T(8,128)(2,1)S(1)}, bf16[16,32,128]{2,1,0:T(8,128)(2,1)S(1)}, u32[]{:S(2)}, u32[]{:S(2)}) %collective-permute-start.9) | collective-permute-done | bytes 131104 | tf_op jit(solution)/shard_map/ppermute | solution.py:609
  132.2 3.4 %collective-permute-done.10.m2 = bf16[16,32,128]{2,1,0:T(8,128)(2,1)S(1)} collective-permute-done((bf16[16,32,128]{2,1,0:T(8,128)(2,1)S(1)}, bf16[16,32,128]{2,1,0:T(8,128)(2,1)S(1)}, u32[]{:S(2)}, u32[]{:S(2)}) %collective-permute-start.10) | collective-permute-done | bytes 131104 | tf_op jit(solution)/shard_map/ppermute | solution.py:609
  135.6 2.1 %finish.1 = (f32[2048,128]{1,0:T(8,128)}, f32[128,256]{1,0:T(8,128)}) custom-call(s32[2]{0:T(128)S(1)} %pad_add_fusion.place_ref.rep_ref, s32[8]{0:T(128)} %hub_ref.3, bf16[16,32,128]{2,1,0:T(8,128)(2,1)S(1)} %scatter_rows.1.m0, bf16[16,32,128]{2,1,0:T(8,128)(2,1)S(1)} %collective-permute-done.9.m1, bf16[16,32,128]{2,1,0:T(8,128)(2,1)S(1)} %collective-permute-done.10.m2, ...), custom_call_target="tpu_custom_call" | custom-call | tf_op jit(solution)/shard_map/finish/pallas_call | solution.py:594
  (16 shorter events, 0.1 us)
Async XLA Ops:
  2.6 18.4 %all-to-all-start = ((bf16[32,32,128]{2,1,0:T(8,128)(2,1)}), bf16[32,32,128]{2,1,0:T(8,128)(2,1)S(1)}, u32[]{:S(2)}, u32[]{:S(2)}) async-start(bf16[32,32,128]{2,1,0:T(8,128)(2,1)} %bitcast.4), calls=%async_computation | async-start | bytes 524288 | tf_op jit(solution)/shard_map/all_to_all | solution.py:617
  21.8 4.5 %copy-start.5 = (s32[1,1,384]{2,1,0:T(1,128)S(1)}, s32[1,1,384]{2,1,0:T(1,128)}, u32[]{:S(2)}) copy-start(s32[1,1,384]{2,1,0:T(1,128)} %param.17) | copy-start | bytes 4612
  21.8 4.6 %copy-start.6 = (s32[1,1,384]{2,1,0:T(1,128)S(1)}, s32[1,1,384]{2,1,0:T(1,128)}, u32[]{:S(2)}) copy-start(s32[1,1,384]{2,1,0:T(1,128)} %param.18) | copy-start | bytes 4612
  21.8 5.9 %copy-start = (bf16[2048,128]{1,0:T(8,128)(2,1)S(1)}, bf16[2048,128]{1,0:T(8,128)(2,1)}, u32[]{:S(2)}) copy-start(bf16[2048,128]{1,0:T(8,128)(2,1)} %feat_hbm.1) | copy-start | bytes 1572868
  21.8 24.3 %all-to-all-start.1 = ((bf16[32,160,128]{2,1,0:T(8,128)(2,1)}), bf16[32,160,128]{2,1,0:T(8,128)(2,1)S(1)}, u32[]{:S(2)}, u32[]{:S(2)}) async-start(bf16[32,160,128]{2,1,0:T(8,128)(2,1)} %insert_hubs.1), calls=%async_computation.1 | async-start | bytes 2621440 | tf_op jit(solution)/shard_map/all_to_all | solution.py:617
  53.6 9.6 %collective-permute-start = (bf16[4,128,128]{2,1,0:T(8,128)(2,1)S(1)}, bf16[4,128,128]{2,1,0:T(8,128)(2,1)S(1)}, u32[]{:S(2)}, u32[]{:S(2)}) collective-permute-start(bf16[4,128,128]{2,1,0:T(8,128)(2,1)S(1)} %get-tuple-element.22.after_ref), channel_id=1, source_target_pairs={{0,32},{32,64},{64,96},{96,0},{1,33},{33,65},{65,97},{97,1},{2,34}... | collective-permute-start | bytes 393224 | tf_op jit(solution)/shard_map/ppermute | solution.py:609
  54.3 8.9 %collective-permute-start.1 = (bf16[4,128,128]{2,1,0:T(8,128)(2,1)S(1)}, bf16[4,128,128]{2,1,0:T(8,128)(2,1)S(1)}, u32[]{:S(2)}, u32[]{:S(2)}) collective-permute-start(bf16[4,128,128]{2,1,0:T(8,128)(2,1)S(1)} %get-tuple-element.24), channel_id=1, source_target_pairs={{0,64},{32,96},{64,0},{96,32},{1,65},{33,97},{65,1},{97,33},{2,66}... | collective-permute-start | bytes 393224 | tf_op jit(solution)/shard_map/ppermute | solution.py:609
  57.0 16.0 %copy-start.1 = (bf16[2048,256]{1,0:T(8,128)(2,1)S(1)}, bf16[2048,256]{1,0:T(8,128)(2,1)}, u32[]{:S(2)}) copy-start(bf16[2048,256]{1,0:T(8,128)(2,1)} %cot_ref.1) | copy-start | bytes 3145732
  57.0 16.0 %copy-start.2 = (bf16[128,256]{1,0:T(8,128)(2,1)S(1)}, bf16[128,256]{1,0:T(8,128)(2,1)}, u32[]{:S(2)}) copy-start(bf16[128,256]{1,0:T(8,128)(2,1)} %w_ref.1) | copy-start | bytes 196612
  57.0 16.0 %copy-start.4 = (f32[256]{0:T(256)S(1)}, f32[256]{0:T(256)}, u32[]{:S(2)}) copy-start(f32[256]{0:T(256)} %param.12) | copy-start | bytes 3076
  57.0 6.3 %collective-permute-start.2 = (bf16[4,128,128]{2,1,0:T(8,128)(2,1)S(1)}, bf16[4,128,128]{2,1,0:T(8,128)(2,1)S(1)}, u32[]{:S(2)}, u32[]{:S(2)}) collective-permute-start(bf16[4,128,128]{2,1,0:T(8,128)(2,1)S(1)} %get-tuple-element.25), channel_id=1, source_target_pairs={{0,96},{32,0},{64,32},{96,64},{1,97},{33,1},{65,33},{97,65},{2,98}... | collective-permute-start | bytes 393224 | tf_op jit(solution)/shard_map/ppermute | solution.py:609
  63.4 5.1 %collective-permute-start.3 = (bf16[4,128,128]{2,1,0:T(8,128)(2,1)S(1)}, bf16[4,128,128]{2,1,0:T(8,128)(2,1)S(1)}, u32[]{:S(2)}, u32[]{:S(2)}) collective-permute-start(bf16[4,128,128]{2,1,0:T(8,128)(2,1)S(1)} %sum_quarter.1.z0), channel_id=1, source_target_pairs={{0,32},{32,64},{64,96},{96,0},{1,33},{33,65},{65,97},{97,1},{2,34}... | collective-permute-start | bytes 393224 | tf_op jit(solution)/shard_map/ppermute | solution.py:609
  64.6 8.4 %collective-permute-start.4 = (bf16[4,128,128]{2,1,0:T(8,128)(2,1)S(1)}, bf16[4,128,128]{2,1,0:T(8,128)(2,1)S(1)}, u32[]{:S(2)}, u32[]{:S(2)}) collective-permute-start(bf16[4,128,128]{2,1,0:T(8,128)(2,1)S(1)} %sum_quarter.1.z0), channel_id=1, source_target_pairs={{0,64},{32,96},{64,0},{96,32},{1,65},{33,97},{65,1},{97,33},{2,66}... | collective-permute-start | bytes 393224 | tf_op jit(solution)/shard_map/ppermute | solution.py:609
  67.2 5.8 %collective-permute-start.5 = (bf16[4,128,128]{2,1,0:T(8,128)(2,1)S(1)}, bf16[4,128,128]{2,1,0:T(8,128)(2,1)S(1)}, u32[]{:S(2)}, u32[]{:S(2)}) collective-permute-start(bf16[4,128,128]{2,1,0:T(8,128)(2,1)S(1)} %sum_quarter.1.z0), channel_id=1, source_target_pairs={{0,96},{32,0},{64,32},{96,64},{1,97},{33,1},{65,33},{97,65},{2,98}... | collective-permute-start | bytes 393224 | tf_op jit(solution)/shard_map/ppermute | solution.py:609
  83.3 30.9 %all-to-all-start.2 = ((bf16[128,48,128]{2,1,0:T(8,128)(2,1)}), bf16[128,48,128]{2,1,0:T(8,128)(2,1)S(1)}, u32[]{:S(2)}, u32[]{:S(2)}) async-start(bf16[128,48,128]{2,1,0:T(8,128)(2,1)} %bitcast.7), calls=%async_computation.2 | async-start | bytes 3145728 | tf_op jit(solution)/shard_map/all_to_all | solution.py:617
  93.5 26.4 %copy-start.3 = (s32[1,32,128]{2,1,0:T(8,128)S(1)}, s32[1,32,128]{2,1,0:T(8,128)}, u32[]{:S(2)}) copy-start(s32[1,32,128]{2,1,0:T(8,128)} %param.14) | copy-start | bytes 49156
  93.5 26.4 %collective-permute-start.6 = (bf16[16,32,128]{2,1,0:T(8,128)(2,1)S(1)}, bf16[16,32,128]{2,1,0:T(8,128)(2,1)S(1)}, u32[]{:S(2)}, u32[]{:S(2)}) collective-permute-start(bf16[16,32,128]{2,1,0:T(8,128)(2,1)S(1)} %get-tuple-element.32), channel_id=1, source_target_pairs={{0,32},{32,64},{64,96},{96,0},{1,33},{33,65},{65,97},{97,1},{2,34}... | collective-permute-start | bytes 393224 | tf_op jit(solution)/shard_map/ppermute | solution.py:609
  94.9 25.0 %collective-permute-start.7 = (bf16[16,32,128]{2,1,0:T(8,128)(2,1)S(1)}, bf16[16,32,128]{2,1,0:T(8,128)(2,1)S(1)}, u32[]{:S(2)}, u32[]{:S(2)}) collective-permute-start(bf16[16,32,128]{2,1,0:T(8,128)(2,1)S(1)} %get-tuple-element.33), channel_id=1, source_target_pairs={{0,64},{32,96},{64,0},{96,32},{1,65},{33,97},{65,1},{97,33},{2,66}... | collective-permute-start | bytes 393224 | tf_op jit(solution)/shard_map/ppermute | solution.py:609
  97.4 22.5 %collective-permute-start.8 = (bf16[16,32,128]{2,1,0:T(8,128)(2,1)S(1)}, bf16[16,32,128]{2,1,0:T(8,128)(2,1)S(1)}, u32[]{:S(2)}, u32[]{:S(2)}) collective-permute-start(bf16[16,32,128]{2,1,0:T(8,128)(2,1)S(1)} %get-tuple-element.34), channel_id=1, source_target_pairs={{0,96},{32,0},{64,32},{96,64},{1,97},{33,1},{65,33},{97,65},{2,98}... | collective-permute-start | bytes 393224 | tf_op jit(solution)/shard_map/ppermute | solution.py:609
  115.2 20.4 %all-to-all-start.3 = ((bf16[128,16,128]{2,1,0:T(8,128)(2,1)}), bf16[128,16,128]{2,1,0:T(8,128)(2,1)S(1)}, u32[]{:S(2)}, u32[]{:S(2)}) async-start(bf16[128,16,128]{2,1,0:T(8,128)(2,1)} %broadcast_in_dim.2), calls=%async_computation.3 | async-start | bytes 1048576 | tf_op jit(solution)/shard_map/all_to_all | solution.py:617
  123.0 9.1 %collective-permute-start.9 = (bf16[16,32,128]{2,1,0:T(8,128)(2,1)S(1)}, bf16[16,32,128]{2,1,0:T(8,128)(2,1)S(1)}, u32[]{:S(2)}, u32[]{:S(2)}) collective-permute-start(bf16[16,32,128]{2,1,0:T(8,128)(2,1)S(1)} %scatter_rows.1.m0), channel_id=1, source_target_pairs={{0,32},{32,64},{64,96},{96,0},{1,33},{33,65},{65,97},{97,1},{2,34}... | collective-permute-start | bytes 393224 | tf_op jit(solution)/shard_map/ppermute | solution.py:609
  124.5 11.0 %collective-permute-start.10 = (bf16[16,32,128]{2,1,0:T(8,128)(2,1)S(1)}, bf16[16,32,128]{2,1,0:T(8,128)(2,1)S(1)}, u32[]{:S(2)}, u32[]{:S(2)}) collective-permute-start(bf16[16,32,128]{2,1,0:T(8,128)(2,1)S(1)} %scatter_rows.1.m0), channel_id=1, source_target_pairs={{0,64},{32,96},{64,0},{96,32},{1,65},{33,97},{65,1},{97,33},{2,66}... | collective-permute-start | bytes 393224 | tf_op jit(solution)/shard_map/ppermute | solution.py:609
  127.1 8.5 %collective-permute-start.11 = (bf16[16,32,128]{2,1,0:T(8,128)(2,1)S(1)}, bf16[16,32,128]{2,1,0:T(8,128)(2,1)S(1)}, u32[]{:S(2)}, u32[]{:S(2)}) collective-permute-start(bf16[16,32,128]{2,1,0:T(8,128)(2,1)S(1)} %scatter_rows.1.m0), channel_id=1, source_target_pairs={{0,96},{32,0},{64,32},{96,64},{1,97},{33,1},{65,33},{97,65},{2,98}... | collective-permute-start | bytes 393224 | tf_op jit(solution)/shard_map/ppermute | solution.py:609

commit v6 on v5

--- a/solution.py
+++ b/solution.py
@@ -153,7 +153,7 @@
     )(dst, src)
 
 
-AHEAD = 3
+AHEAD = 6
 
 
 def keep(tiles, buckets):
@@ -567,6 +567,26 @@
     )(counts, rows, received, own, a, b, c)
 
 
+def piece_kernel(recv_ref, out_ref):
+    sums = [recv_ref[n, pl.ds(FQ, 16), :].astype(F32) for n in range(4)]
+    for n in range(4, N_REP * N_DOM):
+        sums[n % 4] = sums[n % 4] + recv_ref[n, pl.ds(FQ, 16), :].astype(F32)
+    piece = ((sums[0] + sums[1]) + (sums[2] + sums[3])).astype(BF16)
+    for n in range(N_REP * N_DOM):
+        out_ref[n] = piece
+
+
+def sum_piece(received):
+    return pl.pallas_call(
+        piece_kernel,
+        out_shape=jax.ShapeDtypeStruct((N_REP * N_DOM, 16, BLK), BF16),
+        in_specs=[VM],
+        out_specs=VM,
+        compiler_params=PARAMS,
+        name="sum_piece",
+    )(received)
+
+
 def final_kernel(place_ref, hub_ref, m0, m1, m2, m3, shared_ref, gx_ref, gw_ref, blocks, *, scale):
     rep = place_ref[0]
     for k, ref in enumerate((m0, m1, m2, m3)):
@@ -656,8 +676,7 @@
     own, s1, s2, s3 = backward_near(bwd, place, ys, stored)
     a, b, c = turn(s1, 1), turn(s2, 2), turn(s3, 3)
 
-    piece = jnp.sum(returned[:, FQ:, :].astype(F32), axis=0).astype(BF16)
-    shared = swap(jnp.broadcast_to(piece[None], (N_REP * N_DOM, 16, BLK)), ("rep", "dom"))
+    shared = swap(sum_piece(returned), ("rep", "dom"))
     part = scatter_rows(send_count, rows, returned, own, a, b, c)
     grad_x, grad_w = finish(place, hub_blocks, around(part), shared, 1.0 / math.sqrt(ROWS * N_DOM))
     return (output, grad_x, grad_w)

time: 138 us -> 139 us (level)
  starting transfers between devices: 45 us -> 47.3 us
    all_to_all x4, starting transfers between devices: 24.8 us -> 27.8 us  [swap(): return lax.all_to_all(value, axes, split_axis=0, concat_axis=0, tiled=True)]
  transfers between devices with their start and end apart: 16 -> 16, of which waited for: 8 -> 8; matrix products, arithmetic and copies ran while one was open for 1% -> 0% of each run, Pallas kernels for 16% -> 17%
where the time goes in v6:
time: 139 us; the launch traced here: 138 us
  starting transfers between devices  47.3 us (34%)
  waiting for transfers between devices  45.3 us (33%)
  Pallas kernels  44.5 us (32%)
    all_to_all x4, waiting for transfers between devices, swap(): return lax.all_to_all(value, axes, split_axis=0, concat_axis=0, tiled=True)  33.5 us
    all_to_all x4, starting transfers between devices, swap(): return lax.all_to_all(value, axes, split_axis=0, concat_axis=0, tiled=True)  27.8 us
    ppermute x12, starting transfers between devices, turn(): lax.ppermute(value, 'rep', [(i, (i + k) % N_REP) for i in range(N_REP)])  19.5 us
    ppermute x12, waiting for transfers between devices, turn(): lax.ppermute(value, 'rep', [(i, (i + k) % N_REP) for i in range(N_REP)])  11.7 us
    pallas_call x1, Pallas kernels, forward_far(): pl.pallas_call(forward_far_kernel, out_shape=[jax.ShapeDtypeStruct(quarte...  6.48 us
    pallas_call x1, Pallas kernels, backward_far(): pl.pallas_call(backward_far_kernel, out_shape=jax.ShapeDtypeStruct((N_REP...  6.39 us
    pallas_call x1, Pallas kernels, gather_rows(): pl.pallas_call(gather_kernel, out_shape=jax.ShapeDtypeStruct((N_DOM, BLK...  5.93 us
    pallas_call x1, Pallas kernels, hold_tiles(): pl.pallas_call(hold_kernel, out_shape=pltpu.VMEM((TILES, BLK, BLK), BF16)...  4.58 us
  transfers between devices with their start and end apart: 16, of which 8 were waited for; matrix products, arithmetic and copies ran while one was open for 0% of the time, Pallas kernels for 17%

profile of v6, /device:TPU:1, one launch (start us, length us, event | category | flops | bytes accessed | tf_op | source)
XLA Modules:
  0.0 138.1 jit_solution(1941363713743971981)
XLA Ops:
  0.6 0.1 pad_add_fusion.place_ref.rep_ref
  0.7 1.9 %pick_hubs.1 = bf16[8,128,128]{2,1,0:T(8,128)(2,1)} custom-call(s32[2]{0:T(128)S(1)} %pad_add_fusion.place_ref.rep_ref, s32[8]{0:T(128)} %hub_ref.3, bf16[16,128,128]{2,1,0:T(8,128)(2,1)} %bitcast.10), custom_call_target="tpu_custom_call" | custom-call | tf_op jit(solution)/shard_map/pick_hubs/pallas_call | solution.py:283
  2.6 9.4 %all-to-all-start = ((bf16[32,32,128]{2,1,0:T(8,128)(2,1)}), bf16[32,32,128]{2,1,0:T(8,128)(2,1)S(1)}, u32[]{:S(2)}, u32[]{:S(2)}) async-start(bf16[32,32,128]{2,1,0:T(8,128)(2,1)} %bitcast.4), calls=%async_computation | async-start | bytes 524288 | tf_op jit(solution)/shard_map/all_to_all | solution.py:637
  12.0 5.9 %gather_rows.1.listed_ref = bf16[32,160,128]{2,1,0:T(8,128)(2,1)} custom-call(s32[32,128]{1,0:T(8,128)} %bitcast.14, s32[1,32]{1,0:T(1,128)} %count_ref.3, bf16[2048,128]{1,0:T(8,128)(2,1)} %feat_hbm.1), custom_call_target="tpu_custom_call" | custom-call | flops 4000000000 | bytes 2000000 | tf_op jit(solution)/shard_map/gather_rows/pallas_call | solution.py:252
  18.0 3.0 %all-to-all-done.spread_ref = bf16[32,32,128]{2,1,0:T(8,128)(2,1)S(1)} async-done(((bf16[32,32,128]{2,1,0:T(8,128)(2,1)}), bf16[32,32,128]{2,1,0:T(8,128)(2,1)S(1)}, u32[]{:S(2)}, u32[]{:S(2)}) %all-to-all-start) | async-done | bytes 262176 | tf_op jit(solution)/shard_map/all_to_all | solution.py:637
  21.0 0.8 insert_hubs.1
  21.8 0.0 copy-start.5
  21.9 0.0 copy-start.6
  21.9 0.0 copy-start
  21.9 4.5 %all-to-all-start.1 = ((bf16[32,160,128]{2,1,0:T(8,128)(2,1)}), bf16[32,160,128]{2,1,0:T(8,128)(2,1)S(1)}, u32[]{:S(2)}, u32[]{:S(2)}) async-start(bf16[32,160,128]{2,1,0:T(8,128)(2,1)} %insert_hubs.1), calls=%async_computation.1 | async-start | bytes 2621440 | tf_op jit(solution)/shard_map/all_to_all | solution.py:637
  26.5 1.3 order_tiles.1
  27.8 3.8 %forward_near.1.near_ref = f32[16,128,128]{2,1,0:T(8,128)S(1)} custom-call(s32[4,4,128]{2,1,0:T(4,128)S(1)} %get-tuple-element.20.plan_ref, bf16[16,128,128]{2,1,0:T(8,128)(2,1)S(1)} %bitcast.11, bf16[384,128,128]{2,1,0:T(8,128)(2,1)} %bitcast.17), custom_call_target="tpu_custom_call" | custom-call | flops 1000000000 | bytes 4000000 | tf_op jit(solution)/shard_map/forward_near/pallas_call | solution.py:355
  31.5 14.6 %all-to-all-done.1.recv_ref = bf16[32,160,128]{2,1,0:T(8,128)(2,1)S(1)} async-done(((bf16[32,160,128]{2,1,0:T(8,128)(2,1)}), bf16[32,160,128]{2,1,0:T(8,128)(2,1)S(1)}, u32[]{:S(2)}, u32[]{:S(2)}) %all-to-all-start.1) | async-done | bytes 1310752 | tf_op jit(solution)/shard_map/all_to_all | solution.py:637
  46.2 6.5 %forward_far.1 = (f32[4,128,128]{2,1,0:T(8,128)S(1)}, bf16[4,128,128]{2,1,0:T(8,128)(2,1)S(1)}, bf16[4,128,128]{2,1,0:T(8,128)(2,1)S(1)}, bf16[4,128,128]{2,1,0:T(8,128)(2,1)S(1)}) custom-call(s32[4,4,128]{2,1,0:T(4,128)S(1)} %get-tuple-element.20.plan_ref, s32[2]{0:T(128)S(1)} %pad_add_fusion.place_ref.rep_ref, f32[16,128,128]{2,1,0:T(8,128)S(1)} %forward_near.1.near_ref, ...), custom_call_target="tpu_custom_call" | custom-call | flops 4000000000 | bytes 12000000 | tf_op jit(solution)/shard_map/forward_far/pallas_call | solution.py:369
  52.7 1.4 collective-permute-start
  54.0 2.6 %collective-permute-start.1 = (bf16[4,128,128]{2,1,0:T(8,128)(2,1)S(1)}, bf16[4,128,128]{2,1,0:T(8,128)(2,1)S(1)}, u32[]{:S(2)}, u32[]{:S(2)}) collective-permute-start(bf16[4,128,128]{2,1,0:T(8,128)(2,1)S(1)} %get-tuple-element.24), channel_id=1, source_target_pairs={{0,64},{32,96},{64,0},{96,32},{1,65},{33,97},{65,1},{97,33},{2,66}... | collective-permute-start | bytes 393224 | tf_op jit(solution)/shard_map/ppermute | solution.py:629
  56.7 1.1 collective-permute-start.2
  57.8 4.6 %hold_tiles.1.w_ref = bf16[384,128,128]{2,1,0:T(8,128)(2,1)S(1)} custom-call(bf16[384,128,128]{2,1,0:T(8,128)(2,1)} %bitcast.19, bf16[4,128,128]{2,1,0:T(8,128)(2,1)S(1)} %get-tuple-element.22.after_ref), custom_call_target="tpu_custom_call" | custom-call | bytes 13000000 | tf_op jit(solution)/shard_map/hold_tiles/pallas_call | solution.py:449
  62.4 0.0 collective-permute-done.a_ref
  62.4 0.3 collective-permute-done.1.b_ref
  62.7 0.0 collective-permute-done.2.c_ref
  62.7 0.1 sum_quarter.1.z0
  62.7 1.0 collective-permute-start.3
  63.8 2.3 %collective-permute-start.4 = (bf16[4,128,128]{2,1,0:T(8,128)(2,1)S(1)}, bf16[4,128,128]{2,1,0:T(8,128)(2,1)S(1)}, u32[]{:S(2)}, u32[]{:S(2)}) collective-permute-start(bf16[4,128,128]{2,1,0:T(8,128)(2,1)S(1)} %sum_quarter.1.z0), channel_id=1, source_target_pairs={{0,64},{32,96},{64,0},{96,32},{1,65},{33,97},{65,1},{97,33},{2,66}... | collective-permute-start | bytes 393224 | tf_op jit(solution)/shard_map/ppermute | solution.py:629
  66.0 1.0 collective-permute-start.5
  67.0 0.9 collective-permute-done.3.z1
  67.8 3.1 %collective-permute-done.4.z2 = bf16[4,128,128]{2,1,0:T(8,128)(2,1)S(1)} collective-permute-done((bf16[4,128,128]{2,1,0:T(8,128)(2,1)S(1)}, bf16[4,128,128]{2,1,0:T(8,128)(2,1)S(1)}, u32[]{:S(2)}, u32[]{:S(2)}) %collective-permute-start.4) | collective-permute-done | bytes 131104 | tf_op jit(solution)/shard_map/ppermute | solution.py:629
  70.9 0.0 collective-permute-done.5.z3
  71.0 3.4 %middle.1 = (bf16[2048,256]{1,0:T(8,128)(2,1)}, bf16[17,128,128]{2,1,0:T(8,128)(2,1)S(1)}, bf16[32,16,128]{2,1,0:T(8,128)(2,1)S(1)}) custom-call(s32[2]{0:T(128)S(1)} %pad_add_fusion.place_ref.rep_ref, bf16[4,128,128]{2,1,0:T(8,128)(2,1)S(1)} %sum_quarter.1.z0, bf16[4,128,128]{2,1,0:T(8,128)(2,1)S(1)} %collective-permute-done.3.z1, ...), custom_call_target="tpu_custom_call" | custom-call | flops 5000000000 | bytes 3000000 | tf_op jit(solution)/shard_map/middle/pallas_call | solution.py:426
  74.4 6.4 %backward_far.1 = bf16[4,32,48,128]{3,2,1,0:T(8,128)(2,1)} custom-call(s32[4,4,128]{2,1,0:T(4,128)S(1)} %get-tuple-element.27.plan_ref, bf16[17,128,128]{2,1,0:T(8,128)(2,1)S(1)} %get-tuple-element.28.ys, bf16[32,16,128]{2,1,0:T(8,128)(2,1)S(1)} %get-tuple-element.29.gw_ref, bf16[384,128,128]{2,1,0:T(8,128)(2,1)S(1)} %hold_tiles.1.w_ref), custom_call_target="tpu_custom_call" | custom-call | flops 4000000000 | bytes 14000000 | tf_op jit(solution)/shard_map/backward_far/pallas_call | solution.py:484
  80.8 9.2 %all-to-all-start.2 = ((bf16[128,48,128]{2,1,0:T(8,128)(2,1)}), bf16[128,48,128]{2,1,0:T(8,128)(2,1)S(1)}, u32[]{:S(2)}, u32[]{:S(2)}) async-start(bf16[128,48,128]{2,1,0:T(8,128)(2,1)} %bitcast.7), calls=%async_computation.2 | async-start | bytes 3145728 | tf_op jit(solution)/shard_map/all_to_all | solution.py:637
  90.0 3.8 %backward_near.1 = (f32[16,32,128]{2,1,0:T(8,128)S(1)}, bf16[16,32,128]{2,1,0:T(8,128)(2,1)S(1)}, bf16[16,32,128]{2,1,0:T(8,128)(2,1)S(1)}, bf16[16,32,128]{2,1,0:T(8,128)(2,1)S(1)}) custom-call(s32[4,4,128]{2,1,0:T(4,128)S(1)} %get-tuple-element.27.plan_ref, s32[2]{0:T(128)S(1)} %pad_add_fusion.place_ref.rep_ref, ...), custom_call_target="tpu_custom_call" | custom-call | flops 1000000000 | bytes 14000000 | tf_op jit(solution)/shard_map/backward_near/pallas_call | solution.py:513
  93.8 1.8 %collective-permute-start.6 = (bf16[16,32,128]{2,1,0:T(8,128)(2,1)S(1)}, bf16[16,32,128]{2,1,0:T(8,128)(2,1)S(1)}, u32[]{:S(2)}, u32[]{:S(2)}) collective-permute-start(bf16[16,32,128]{2,1,0:T(8,128)(2,1)S(1)} %get-tuple-element.32), channel_id=1, source_target_pairs={{0,32},{32,64},{64,96},{96,0},{1,33},{33,65},{65,97},{97,1},{2,34}... | collective-permute-start | bytes 393224 | tf_op jit(solution)/shard_map/ppermute | solution.py:629
  95.6 2.2 %collective-permute-start.7 = (bf16[16,32,128]{2,1,0:T(8,128)(2,1)S(1)}, bf16[16,32,128]{2,1,0:T(8,128)(2,1)S(1)}, u32[]{:S(2)}, u32[]{:S(2)}) collective-permute-start(bf16[16,32,128]{2,1,0:T(8,128)(2,1)S(1)} %get-tuple-element.33), channel_id=1, source_target_pairs={{0,64},{32,96},{64,0},{96,32},{1,65},{33,97},{65,1},{97,33},{2,66}... | collective-permute-start | bytes 393224 | tf_op jit(solution)/shard_map/ppermute | solution.py:629
  97.8 1.0 collective-permute-start.8
  98.8 15.8 %all-to-all-done.2.recv_ref = bf16[128,48,128]{2,1,0:T(8,128)(2,1)S(1)} async-done(((bf16[128,48,128]{2,1,0:T(8,128)(2,1)}), bf16[128,48,128]{2,1,0:T(8,128)(2,1)S(1)}, u32[]{:S(2)}, u32[]{:S(2)}) %all-to-all-start.2) | async-done | bytes 1572896 | tf_op jit(solution)/shard_map/all_to_all | solution.py:637
  114.7 0.9 sum_piece.1
  115.6 4.7 %all-to-all-start.3 = ((bf16[128,16,128]{2,1,0:T(8,128)(2,1)}), bf16[128,16,128]{2,1,0:T(8,128)(2,1)S(1)}, u32[]{:S(2)}, u32[]{:S(2)}) async-start(bf16[128,16,128]{2,1,0:T(8,128)(2,1)} %sum_piece.1), calls=%async_computation.3 | async-start | bytes 1048576 | tf_op jit(solution)/shard_map/all_to_all | solution.py:637
  120.2 0.0 collective-permute-done.6.a_ref
  120.3 0.0 collective-permute-done.7.b_ref
  120.3 3.1 %scatter_rows.1.m0 = bf16[16,32,128]{2,1,0:T(8,128)(2,1)S(1)} custom-call(s32[1,32]{1,0:T(1,128)} %count_ref.3, s32[32,128]{1,0:T(8,128)S(1)} %bitcast.15, bf16[128,48,128]{2,1,0:T(8,128)(2,1)S(1)} %all-to-all-done.2.recv_ref, f32[16,32,128]{2,1,0:T(8,128)S(1)} %get-tuple-element.31.own_ref, bf16[16,32,128]{2,1,0:T(8,128)(2,1)S(1)} %collective-permute-done.6.a_ref, ...), custom_call_target="tpu_custom_call" | custom-call | flops 4000000000 | bytes 4000000 | tf_op jit(solution)/shard_map/scatter_rows/pallas_call | solution.py:558
  123.4 1.5 %collective-permute-start.9 = (bf16[16,32,128]{2,1,0:T(8,128)(2,1)S(1)}, bf16[16,32,128]{2,1,0:T(8,128)(2,1)S(1)}, u32[]{:S(2)}, u32[]{:S(2)}) collective-permute-start(bf16[16,32,128]{2,1,0:T(8,128)(2,1)S(1)} %scatter_rows.1.m0), channel_id=1, source_target_pairs={{0,32},{32,64},{64,96},{96,0},{1,33},{33,65},{65,97},{97,1},{2,34}... | collective-permute-start | bytes 393224 | tf_op jit(solution)/shard_map/ppermute | solution.py:629
  124.9 2.5 %collective-permute-start.10 = (bf16[16,32,128]{2,1,0:T(8,128)(2,1)S(1)}, bf16[16,32,128]{2,1,0:T(8,128)(2,1)S(1)}, u32[]{:S(2)}, u32[]{:S(2)}) collective-permute-start(bf16[16,32,128]{2,1,0:T(8,128)(2,1)S(1)} %scatter_rows.1.m0), channel_id=1, source_target_pairs={{0,64},{32,96},{64,0},{96,32},{1,65},{33,97},{65,1},{97,33},{2,66}... | collective-permute-start | bytes 393224 | tf_op jit(solution)/shard_map/ppermute | solution.py:629
  127.4 1.1 collective-permute-start.11
  128.5 4.0 %collective-permute-done.9.m1 = bf16[16,32,128]{2,1,0:T(8,128)(2,1)S(1)} collective-permute-done((bf16[16,32,128]{2,1,0:T(8,128)(2,1)S(1)}, bf16[16,32,128]{2,1,0:T(8,128)(2,1)S(1)}, u32[]{:S(2)}, u32[]{:S(2)}) %collective-permute-start.9) | collective-permute-done | bytes 131104 | tf_op jit(solution)/shard_map/ppermute | solution.py:629
  132.5 3.4 %collective-permute-done.10.m2 = bf16[16,32,128]{2,1,0:T(8,128)(2,1)S(1)} collective-permute-done((bf16[16,32,128]{2,1,0:T(8,128)(2,1)S(1)}, bf16[16,32,128]{2,1,0:T(8,128)(2,1)S(1)}, u32[]{:S(2)}, u32[]{:S(2)}) %collective-permute-start.10) | collective-permute-done | bytes 131104 | tf_op jit(solution)/shard_map/ppermute | solution.py:629
  136.0 0.0 collective-permute-done.11.m3
  136.0 2.1 %finish.1 = (f32[2048,128]{1,0:T(8,128)}, f32[128,256]{1,0:T(8,128)}) custom-call(s32[2]{0:T(128)S(1)} %pad_add_fusion.place_ref.rep_ref, s32[8]{0:T(128)} %hub_ref.3, bf16[16,32,128]{2,1,0:T(8,128)(2,1)S(1)} %scatter_rows.1.m0, bf16[16,32,128]{2,1,0:T(8,128)(2,1)S(1)} %collective-permute-done.9.m1, bf16[16,32,128]{2,1,0:T(8,128)(2,1)S(1)} %collective-permute-done.10.m2, ...), custom_call_target="tpu_custom_call" | custom-call | tf_op jit(solution)/shard_map/finish/pallas_call | solution.py:614
  (15 shorter events, 0.1 us)
Async XLA Ops:
  2.6 18.4 %all-to-all-start = ((bf16[32,32,128]{2,1,0:T(8,128)(2,1)}), bf16[32,32,128]{2,1,0:T(8,128)(2,1)S(1)}, u32[]{:S(2)}, u32[]{:S(2)}) async-start(bf16[32,32,128]{2,1,0:T(8,128)(2,1)} %bitcast.4), calls=%async_computation | async-start | bytes 524288 | tf_op jit(solution)/shard_map/all_to_all | solution.py:637
  21.8 4.6 %copy-start.5 = (s32[1,1,384]{2,1,0:T(1,128)S(1)}, s32[1,1,384]{2,1,0:T(1,128)}, u32[]{:S(2)}) copy-start(s32[1,1,384]{2,1,0:T(1,128)} %param.17) | copy-start | bytes 4612
  21.9 4.6 %copy-start.6 = (s32[1,1,384]{2,1,0:T(1,128)S(1)}, s32[1,1,384]{2,1,0:T(1,128)}, u32[]{:S(2)}) copy-start(s32[1,1,384]{2,1,0:T(1,128)} %param.18) | copy-start | bytes 4612
  21.9 5.9 %copy-start = (bf16[2048,128]{1,0:T(8,128)(2,1)S(1)}, bf16[2048,128]{1,0:T(8,128)(2,1)}, u32[]{:S(2)}) copy-start(bf16[2048,128]{1,0:T(8,128)(2,1)} %feat_hbm.1) | copy-start | bytes 1572868
  21.9 24.3 %all-to-all-start.1 = ((bf16[32,160,128]{2,1,0:T(8,128)(2,1)}), bf16[32,160,128]{2,1,0:T(8,128)(2,1)S(1)}, u32[]{:S(2)}, u32[]{:S(2)}) async-start(bf16[32,160,128]{2,1,0:T(8,128)(2,1)} %insert_hubs.1), calls=%async_computation.1 | async-start | bytes 2621440 | tf_op jit(solution)/shard_map/all_to_all | solution.py:637
  52.7 9.7 %collective-permute-start = (bf16[4,128,128]{2,1,0:T(8,128)(2,1)S(1)}, bf16[4,128,128]{2,1,0:T(8,128)(2,1)S(1)}, u32[]{:S(2)}, u32[]{:S(2)}) collective-permute-start(bf16[4,128,128]{2,1,0:T(8,128)(2,1)S(1)} %get-tuple-element.22.after_ref), channel_id=1, source_target_pairs={{0,32},{32,64},{64,96},{96,0},{1,33},{33,65},{65,97},{97,1},{2,34}... | collective-permute-start | bytes 393224 | tf_op jit(solution)/shard_map/ppermute | solution.py:629
  54.0 8.6 %collective-permute-start.1 = (bf16[4,128,128]{2,1,0:T(8,128)(2,1)S(1)}, bf16[4,128,128]{2,1,0:T(8,128)(2,1)S(1)}, u32[]{:S(2)}, u32[]{:S(2)}) collective-permute-start(bf16[4,128,128]{2,1,0:T(8,128)(2,1)S(1)} %get-tuple-element.24), channel_id=1, source_target_pairs={{0,64},{32,96},{64,0},{96,32},{1,65},{33,97},{65,1},{97,33},{2,66}... | collective-permute-start | bytes 393224 | tf_op jit(solution)/shard_map/ppermute | solution.py:629
  56.7 14.3 %copy-start.1 = (bf16[2048,256]{1,0:T(8,128)(2,1)S(1)}, bf16[2048,256]{1,0:T(8,128)(2,1)}, u32[]{:S(2)}) copy-start(bf16[2048,256]{1,0:T(8,128)(2,1)} %cot_ref.1) | copy-start | bytes 3145732
  56.7 14.3 %copy-start.2 = (bf16[128,256]{1,0:T(8,128)(2,1)S(1)}, bf16[128,256]{1,0:T(8,128)(2,1)}, u32[]{:S(2)}) copy-start(bf16[128,256]{1,0:T(8,128)(2,1)} %w_ref.1) | copy-start | bytes 196612
  56.7 14.3 %copy-start.4 = (f32[256]{0:T(256)S(1)}, f32[256]{0:T(256)}, u32[]{:S(2)}) copy-start(f32[256]{0:T(256)} %param.12) | copy-start | bytes 3076
  56.7 6.0 %collective-permute-start.2 = (bf16[4,128,128]{2,1,0:T(8,128)(2,1)S(1)}, bf16[4,128,128]{2,1,0:T(8,128)(2,1)S(1)}, u32[]{:S(2)}, u32[]{:S(2)}) collective-permute-start(bf16[4,128,128]{2,1,0:T(8,128)(2,1)S(1)} %get-tuple-element.25), channel_id=1, source_target_pairs={{0,96},{32,0},{64,32},{96,64},{1,97},{33,1},{65,33},{97,65},{2,98}... | collective-permute-start | bytes 393224 | tf_op jit(solution)/shard_map/ppermute | solution.py:629
  62.7 5.1 %collective-permute-start.3 = (bf16[4,128,128]{2,1,0:T(8,128)(2,1)S(1)}, bf16[4,128,128]{2,1,0:T(8,128)(2,1)S(1)}, u32[]{:S(2)}, u32[]{:S(2)}) collective-permute-start(bf16[4,128,128]{2,1,0:T(8,128)(2,1)S(1)} %sum_quarter.1.z0), channel_id=1, source_target_pairs={{0,32},{32,64},{64,96},{96,0},{1,33},{33,65},{65,97},{97,1},{2,34}... | collective-permute-start | bytes 393224 | tf_op jit(solution)/shard_map/ppermute | solution.py:629
  63.8 7.2 %collective-permute-start.4 = (bf16[4,128,128]{2,1,0:T(8,128)(2,1)S(1)}, bf16[4,128,128]{2,1,0:T(8,128)(2,1)S(1)}, u32[]{:S(2)}, u32[]{:S(2)}) collective-permute-start(bf16[4,128,128]{2,1,0:T(8,128)(2,1)S(1)} %sum_quarter.1.z0), channel_id=1, source_target_pairs={{0,64},{32,96},{64,0},{96,32},{1,65},{33,97},{65,1},{97,33},{2,66}... | collective-permute-start | bytes 393224 | tf_op jit(solution)/shard_map/ppermute | solution.py:629
  66.0 4.9 %collective-permute-start.5 = (bf16[4,128,128]{2,1,0:T(8,128)(2,1)S(1)}, bf16[4,128,128]{2,1,0:T(8,128)(2,1)S(1)}, u32[]{:S(2)}, u32[]{:S(2)}) collective-permute-start(bf16[4,128,128]{2,1,0:T(8,128)(2,1)S(1)} %sum_quarter.1.z0), channel_id=1, source_target_pairs={{0,96},{32,0},{64,32},{96,64},{1,97},{33,1},{65,33},{97,65},{2,98}... | collective-permute-start | bytes 393224 | tf_op jit(solution)/shard_map/ppermute | solution.py:629
  80.8 33.9 %all-to-all-start.2 = ((bf16[128,48,128]{2,1,0:T(8,128)(2,1)}), bf16[128,48,128]{2,1,0:T(8,128)(2,1)S(1)}, u32[]{:S(2)}, u32[]{:S(2)}) async-start(bf16[128,48,128]{2,1,0:T(8,128)(2,1)} %bitcast.7), calls=%async_computation.2 | async-start | bytes 3145728 | tf_op jit(solution)/shard_map/all_to_all | solution.py:637
  93.8 26.4 %collective-permute-start.6 = (bf16[16,32,128]{2,1,0:T(8,128)(2,1)S(1)}, bf16[16,32,128]{2,1,0:T(8,128)(2,1)S(1)}, u32[]{:S(2)}, u32[]{:S(2)}) collective-permute-start(bf16[16,32,128]{2,1,0:T(8,128)(2,1)S(1)} %get-tuple-element.32), channel_id=1, source_target_pairs={{0,32},{32,64},{64,96},{96,0},{1,33},{33,65},{65,97},{97,1},{2,34}... | collective-permute-start | bytes 393224 | tf_op jit(solution)/shard_map/ppermute | solution.py:629
  95.6 24.7 %collective-permute-start.7 = (bf16[16,32,128]{2,1,0:T(8,128)(2,1)S(1)}, bf16[16,32,128]{2,1,0:T(8,128)(2,1)S(1)}, u32[]{:S(2)}, u32[]{:S(2)}) collective-permute-start(bf16[16,32,128]{2,1,0:T(8,128)(2,1)S(1)} %get-tuple-element.33), channel_id=1, source_target_pairs={{0,64},{32,96},{64,0},{96,32},{1,65},{33,97},{65,1},{97,33},{2,66}... | collective-permute-start | bytes 393224 | tf_op jit(solution)/shard_map/ppermute | solution.py:629
  97.8 22.5 %copy-start.3 = (s32[1,32,128]{2,1,0:T(8,128)S(1)}, s32[1,32,128]{2,1,0:T(8,128)}, u32[]{:S(2)}) copy-start(s32[1,32,128]{2,1,0:T(8,128)} %param.14) | copy-start | bytes 49156
  97.8 22.4 %collective-permute-start.8 = (bf16[16,32,128]{2,1,0:T(8,128)(2,1)S(1)}, bf16[16,32,128]{2,1,0:T(8,128)(2,1)S(1)}, u32[]{:S(2)}, u32[]{:S(2)}) collective-permute-start(bf16[16,32,128]{2,1,0:T(8,128)(2,1)S(1)} %get-tuple-element.34), channel_id=1, source_target_pairs={{0,96},{32,0},{64,32},{96,64},{1,97},{33,1},{65,33},{97,65},{2,98}... | collective-permute-start | bytes 393224 | tf_op jit(solution)/shard_map/ppermute | solution.py:629
  115.6 20.4 %all-to-all-start.3 = ((bf16[128,16,128]{2,1,0:T(8,128)(2,1)}), bf16[128,16,128]{2,1,0:T(8,128)(2,1)S(1)}, u32[]{:S(2)}, u32[]{:S(2)}) async-start(bf16[128,16,128]{2,1,0:T(8,128)(2,1)} %sum_piece.1), calls=%async_computation.3 | async-start | bytes 1048576 | tf_op jit(solution)/shard_map/all_to_all | solution.py:637
  123.4 9.2 %collective-permute-start.9 = (bf16[16,32,128]{2,1,0:T(8,128)(2,1)S(1)}, bf16[16,32,128]{2,1,0:T(8,128)(2,1)S(1)}, u32[]{:S(2)}, u32[]{:S(2)}) collective-permute-start(bf16[16,32,128]{2,1,0:T(8,128)(2,1)S(1)} %scatter_rows.1.m0), channel_id=1, source_target_pairs={{0,32},{32,64},{64,96},{96,0},{1,33},{33,65},{65,97},{97,1},{2,34}... | collective-permute-start | bytes 393224 | tf_op jit(solution)/shard_map/ppermute | solution.py:629
  124.9 11.1 %collective-permute-start.10 = (bf16[16,32,128]{2,1,0:T(8,128)(2,1)S(1)}, bf16[16,32,128]{2,1,0:T(8,128)(2,1)S(1)}, u32[]{:S(2)}, u32[]{:S(2)}) collective-permute-start(bf16[16,32,128]{2,1,0:T(8,128)(2,1)S(1)} %scatter_rows.1.m0), channel_id=1, source_target_pairs={{0,64},{32,96},{64,0},{96,32},{1,65},{33,97},{65,1},{97,33},{2,66}... | collective-permute-start | bytes 393224 | tf_op jit(solution)/shard_map/ppermute | solution.py:629
  127.4 8.6 %collective-permute-start.11 = (bf16[16,32,128]{2,1,0:T(8,128)(2,1)S(1)}, bf16[16,32,128]{2,1,0:T(8,128)(2,1)S(1)}, u32[]{:S(2)}, u32[]{:S(2)}) collective-permute-start(bf16[16,32,128]{2,1,0:T(8,128)(2,1)S(1)} %scatter_rows.1.m0), channel_id=1, source_target_pairs={{0,96},{32,0},{64,32},{96,64},{1,97},{33,1},{65,33},{97,65},{2,98}... | collective-permute-start | bytes 393224 | tf_op jit(solution)/shard_map/ppermute | solution.py:629

commit v7 on v6

--- a/solution.py
+++ b/solution.py
@@ -466,9 +466,10 @@
     return product
 
 
-def backward_far_kernel(plan_ref, ys, gw_ref, w_ref, msg_ref, acc):
+def backward_far_kernel(plan_ref, ys, gw_ref, w_ref, msg_hbm, acc, msg_ref, stored):
     acc[...] = jnp.zeros_like(acc)
     run_class(plan_ref, 0, w_ref, None, None, backward_product(ys), acc)
+    stores = []
     for q in range(N_REP):
         msg_ref[q, :, pl.ds(0, FQ), :] = acc[pl.ds(0, REMOTE), pl.ds(q * FQ, FQ), :].astype(BF16)
         for m in range(16):
@@ -478,6 +479,10 @@
                 msg_ref[q, 2 * m + 1, pl.ds(FQ, 16), :] = gw_ref[q * 8 + m]
             else:
                 msg_ref[q, 2 * m + 1, pl.ds(FQ, 16), :] = jnp.zeros((16, BLK), BF16)
+        stores.append(pltpu.make_async_copy(msg_ref.at[q], msg_hbm.at[q], stored.at[q]))
+        stores[-1].start()
+    for store in stores:
+        store.wait()
 
 
 def backward_far(plan, ys, gw, weights):
@@ -485,8 +490,12 @@
         backward_far_kernel,
         out_shape=jax.ShapeDtypeStruct((N_REP, N_DOM, MSG, BLK), BF16),
         in_specs=[SM] + [VM] * 3,
-        out_specs=VM,
-        scratch_shapes=[pltpu.VMEM((REMOTE + HUBS, FIN, BLK), F32)],
+        out_specs=pl.BlockSpec(memory_space=pl.ANY),
+        scratch_shapes=[
+            pltpu.VMEM((REMOTE + HUBS, FIN, BLK), F32),
+            pltpu.VMEM((N_REP, N_DOM, MSG, BLK), BF16),
+            pltpu.SemaphoreType.DMA((N_REP,)),
+        ],
         compiler_params=TILE_PARAMS,
         cost_estimate=pl.CostEstimate(flops=4 * 10**9, bytes_accessed=14 * 10**6, transcendentals=0),
         name="backward_far",

time: 139 us -> 138 us (level)
  no operation moved by 1% of the time
where the time goes in v7:
time: 138 us; the launch traced here: 137 us
  starting transfers between devices  46.4 us (34%)
  Pallas kernels  44.9 us (33%)
  waiting for transfers between devices  44.9 us (33%)
    all_to_all x4, waiting for transfers between devices, swap(): return lax.all_to_all(value, axes, split_axis=0, concat_axis=0, tiled=True)  33.5 us
    all_to_all x4, starting transfers between devices, swap(): return lax.all_to_all(value, axes, split_axis=0, concat_axis=0, tiled=True)  26.4 us
    ppermute x12, starting transfers between devices, turn(): lax.ppermute(value, 'rep', [(i, (i + k) % N_REP) for i in range(N_REP)])  20 us
    ppermute x12, waiting for transfers between devices, turn(): lax.ppermute(value, 'rep', [(i, (i + k) % N_REP) for i in range(N_REP)])  11.3 us
    pallas_call x1, Pallas kernels, backward_far(): pl.pallas_call(backward_far_kernel, out_shape=jax.ShapeDtypeStruct((N_REP...  6.77 us
    pallas_call x1, Pallas kernels, forward_far(): pl.pallas_call(forward_far_kernel, out_shape=[jax.ShapeDtypeStruct(quarte...  6.48 us
    pallas_call x1, Pallas kernels, gather_rows(): pl.pallas_call(gather_kernel, out_shape=jax.ShapeDtypeStruct((N_DOM, BLK...  5.93 us
    pallas_call x1, Pallas kernels, hold_tiles(): pl.pallas_call(hold_kernel, out_shape=pltpu.VMEM((TILES, BLK, BLK), BF16)...  4.58 us
  transfers between devices with their start and end apart: 16, of which 8 were waited for; matrix products, arithmetic and copies ran while one was open for 0% of the time, Pallas kernels for 17%

profile of v7, /device:TPU:1, one launch (start us, length us, event | category | flops | bytes accessed | tf_op | source)
XLA Modules:
  0.0 137.2 jit_solution(13142831729630124681)
XLA Ops:
  0.6 0.1 pad_add_fusion.place_ref.rep_ref
  0.7 1.9 %pick_hubs.1 = bf16[8,128,128]{2,1,0:T(8,128)(2,1)} custom-call(s32[2]{0:T(128)S(1)} %pad_add_fusion.place_ref.rep_ref, s32[8]{0:T(128)} %hub_ref.3, bf16[16,128,128]{2,1,0:T(8,128)(2,1)} %bitcast.10), custom_call_target="tpu_custom_call" | custom-call | tf_op jit(solution)/shard_map/pick_hubs/pallas_call | solution.py:283
  2.6 9.4 %all-to-all-start = ((bf16[32,32,128]{2,1,0:T(8,128)(2,1)}), bf16[32,32,128]{2,1,0:T(8,128)(2,1)S(1)}, u32[]{:S(2)}, u32[]{:S(2)}) async-start(bf16[32,32,128]{2,1,0:T(8,128)(2,1)} %bitcast.4), calls=%async_computation | async-start | bytes 524288 | tf_op jit(solution)/shard_map/all_to_all | solution.py:646
  12.0 5.9 %gather_rows.1.listed_ref = bf16[32,160,128]{2,1,0:T(8,128)(2,1)} custom-call(s32[32,128]{1,0:T(8,128)} %bitcast.14, s32[1,32]{1,0:T(1,128)} %count_ref.3, bf16[2048,128]{1,0:T(8,128)(2,1)} %feat_hbm.1), custom_call_target="tpu_custom_call" | custom-call | flops 4000000000 | bytes 2000000 | tf_op jit(solution)/shard_map/gather_rows/pallas_call | solution.py:252
  18.0 3.0 %all-to-all-done.spread_ref = bf16[32,32,128]{2,1,0:T(8,128)(2,1)S(1)} async-done(((bf16[32,32,128]{2,1,0:T(8,128)(2,1)}), bf16[32,32,128]{2,1,0:T(8,128)(2,1)S(1)}, u32[]{:S(2)}, u32[]{:S(2)}) %all-to-all-start) | async-done | bytes 262176 | tf_op jit(solution)/shard_map/all_to_all | solution.py:646
  21.0 0.8 insert_hubs.1
  21.8 0.0 copy-start.5
  21.9 0.0 copy-start.6
  21.9 0.0 copy-start
  21.9 4.5 %all-to-all-start.1 = ((bf16[32,160,128]{2,1,0:T(8,128)(2,1)}), bf16[32,160,128]{2,1,0:T(8,128)(2,1)S(1)}, u32[]{:S(2)}, u32[]{:S(2)}) async-start(bf16[32,160,128]{2,1,0:T(8,128)(2,1)} %insert_hubs.1), calls=%async_computation.1 | async-start | bytes 2621440 | tf_op jit(solution)/shard_map/all_to_all | solution.py:646
  26.5 1.3 order_tiles.1
  27.8 3.8 %forward_near.1.near_ref = f32[16,128,128]{2,1,0:T(8,128)S(1)} custom-call(s32[4,4,128]{2,1,0:T(4,128)S(1)} %get-tuple-element.20.plan_ref, bf16[16,128,128]{2,1,0:T(8,128)(2,1)S(1)} %bitcast.11, bf16[384,128,128]{2,1,0:T(8,128)(2,1)} %bitcast.17), custom_call_target="tpu_custom_call" | custom-call | flops 1000000000 | bytes 4000000 | tf_op jit(solution)/shard_map/forward_near/pallas_call | solution.py:355
  31.5 14.6 %all-to-all-done.1.recv_ref = bf16[32,160,128]{2,1,0:T(8,128)(2,1)S(1)} async-done(((bf16[32,160,128]{2,1,0:T(8,128)(2,1)}), bf16[32,160,128]{2,1,0:T(8,128)(2,1)S(1)}, u32[]{:S(2)}, u32[]{:S(2)}) %all-to-all-start.1) | async-done | bytes 1310752 | tf_op jit(solution)/shard_map/all_to_all | solution.py:646
  46.2 6.5 %forward_far.1 = (f32[4,128,128]{2,1,0:T(8,128)S(1)}, bf16[4,128,128]{2,1,0:T(8,128)(2,1)S(1)}, bf16[4,128,128]{2,1,0:T(8,128)(2,1)S(1)}, bf16[4,128,128]{2,1,0:T(8,128)(2,1)S(1)}) custom-call(s32[4,4,128]{2,1,0:T(4,128)S(1)} %get-tuple-element.20.plan_ref, s32[2]{0:T(128)S(1)} %pad_add_fusion.place_ref.rep_ref, f32[16,128,128]{2,1,0:T(8,128)S(1)} %forward_near.1.near_ref, ...), custom_call_target="tpu_custom_call" | custom-call | flops 4000000000 | bytes 12000000 | tf_op jit(solution)/shard_map/forward_far/pallas_call | solution.py:369
  52.7 1.9 %collective-permute-start = (bf16[4,128,128]{2,1,0:T(8,128)(2,1)S(1)}, bf16[4,128,128]{2,1,0:T(8,128)(2,1)S(1)}, u32[]{:S(2)}, u32[]{:S(2)}) collective-permute-start(bf16[4,128,128]{2,1,0:T(8,128)(2,1)S(1)} %get-tuple-element.22.after_ref), channel_id=1, source_target_pairs={{0,32},{32,64},{64,96},{96,0},{1,33},{33,65},{65,97},{97,1},{2,34}... | collective-permute-start | bytes 393224 | tf_op jit(solution)/shard_map/ppermute | solution.py:638
  54.6 2.0 %collective-permute-start.1 = (bf16[4,128,128]{2,1,0:T(8,128)(2,1)S(1)}, bf16[4,128,128]{2,1,0:T(8,128)(2,1)S(1)}, u32[]{:S(2)}, u32[]{:S(2)}) collective-permute-start(bf16[4,128,128]{2,1,0:T(8,128)(2,1)S(1)} %get-tuple-element.24), channel_id=1, source_target_pairs={{0,64},{32,96},{64,0},{96,32},{1,65},{33,97},{65,1},{97,33},{2,66}... | collective-permute-start | bytes 393224 | tf_op jit(solution)/shard_map/ppermute | solution.py:638
  56.7 1.2 collective-permute-start.2
  57.9 4.6 %hold_tiles.1.w_ref = bf16[384,128,128]{2,1,0:T(8,128)(2,1)S(1)} custom-call(bf16[384,128,128]{2,1,0:T(8,128)(2,1)} %bitcast.19, bf16[4,128,128]{2,1,0:T(8,128)(2,1)S(1)} %get-tuple-element.22.after_ref), custom_call_target="tpu_custom_call" | custom-call | bytes 13000000 | tf_op jit(solution)/shard_map/hold_tiles/pallas_call | solution.py:449
  62.5 0.0 collective-permute-done.a_ref
  62.5 0.0 collective-permute-done.1.b_ref
  62.5 0.0 collective-permute-done.2.c_ref
  62.5 0.1 sum_quarter.1.z0
  62.6 1.1 collective-permute-start.3
  63.6 2.4 %collective-permute-start.4 = (bf16[4,128,128]{2,1,0:T(8,128)(2,1)S(1)}, bf16[4,128,128]{2,1,0:T(8,128)(2,1)S(1)}, u32[]{:S(2)}, u32[]{:S(2)}) collective-permute-start(bf16[4,128,128]{2,1,0:T(8,128)(2,1)S(1)} %sum_quarter.1.z0), channel_id=1, source_target_pairs={{0,64},{32,96},{64,0},{96,32},{1,65},{33,97},{65,1},{97,33},{2,66}... | collective-permute-start | bytes 393224 | tf_op jit(solution)/shard_map/ppermute | solution.py:638
  66.0 1.1 collective-permute-start.5
  67.2 0.5 collective-permute-done.3.z1
  67.7 3.3 %collective-permute-done.4.z2 = bf16[4,128,128]{2,1,0:T(8,128)(2,1)S(1)} collective-permute-done((bf16[4,128,128]{2,1,0:T(8,128)(2,1)S(1)}, bf16[4,128,128]{2,1,0:T(8,128)(2,1)S(1)}, u32[]{:S(2)}, u32[]{:S(2)}) %collective-permute-start.4) | collective-permute-done | bytes 131104 | tf_op jit(solution)/shard_map/ppermute | solution.py:638
  71.0 0.1 collective-permute-done.5.z3
  71.1 3.4 %middle.1 = (bf16[2048,256]{1,0:T(8,128)(2,1)}, bf16[17,128,128]{2,1,0:T(8,128)(2,1)S(1)}, bf16[32,16,128]{2,1,0:T(8,128)(2,1)S(1)}) custom-call(s32[2]{0:T(128)S(1)} %pad_add_fusion.place_ref.rep_ref, bf16[4,128,128]{2,1,0:T(8,128)(2,1)S(1)} %sum_quarter.1.z0, bf16[4,128,128]{2,1,0:T(8,128)(2,1)S(1)} %collective-permute-done.3.z1, ...), custom_call_target="tpu_custom_call" | custom-call | flops 5000000000 | bytes 3000000 | tf_op jit(solution)/shard_map/middle/pallas_call | solution.py:426
  74.5 6.8 %backward_far.1 = bf16[4,32,48,128]{3,2,1,0:T(8,128)(2,1)} custom-call(s32[4,4,128]{2,1,0:T(4,128)S(1)} %get-tuple-element.27.plan_ref, bf16[17,128,128]{2,1,0:T(8,128)(2,1)S(1)} %get-tuple-element.28.ys, bf16[32,16,128]{2,1,0:T(8,128)(2,1)S(1)} %get-tuple-element.29.gw_ref, bf16[384,128,128]{2,1,0:T(8,128)(2,1)S(1)} %hold_tiles.1.w_ref), custom_call_target="tpu_custom_call" | custom-call | flops 4000000000 | bytes 14000000 | tf_op jit(solution)/shard_map/backward_far/pallas_call | solution.py:489
  81.3 7.8 %all-to-all-start.2 = ((bf16[128,48,128]{2,1,0:T(8,128)(2,1)}), bf16[128,48,128]{2,1,0:T(8,128)(2,1)S(1)}, u32[]{:S(2)}, u32[]{:S(2)}) async-start(bf16[128,48,128]{2,1,0:T(8,128)(2,1)} %bitcast.7), calls=%async_computation.2 | async-start | bytes 3145728 | tf_op jit(solution)/shard_map/all_to_all | solution.py:646
  89.1 3.8 %backward_near.1 = (f32[16,32,128]{2,1,0:T(8,128)S(1)}, bf16[16,32,128]{2,1,0:T(8,128)(2,1)S(1)}, bf16[16,32,128]{2,1,0:T(8,128)(2,1)S(1)}, bf16[16,32,128]{2,1,0:T(8,128)(2,1)S(1)}) custom-call(s32[4,4,128]{2,1,0:T(4,128)S(1)} %get-tuple-element.27.plan_ref, s32[2]{0:T(128)S(1)} %pad_add_fusion.place_ref.rep_ref, ...), custom_call_target="tpu_custom_call" | custom-call | flops 1000000000 | bytes 14000000 | tf_op jit(solution)/shard_map/backward_near/pallas_call | solution.py:522
  92.9 1.5 %collective-permute-start.6 = (bf16[16,32,128]{2,1,0:T(8,128)(2,1)S(1)}, bf16[16,32,128]{2,1,0:T(8,128)(2,1)S(1)}, u32[]{:S(2)}, u32[]{:S(2)}) collective-permute-start(bf16[16,32,128]{2,1,0:T(8,128)(2,1)S(1)} %get-tuple-element.32), channel_id=1, source_target_pairs={{0,32},{32,64},{64,96},{96,0},{1,33},{33,65},{65,97},{97,1},{2,34}... | collective-permute-start | bytes 393224 | tf_op jit(solution)/shard_map/ppermute | solution.py:638
  94.4 2.4 %collective-permute-start.7 = (bf16[16,32,128]{2,1,0:T(8,128)(2,1)S(1)}, bf16[16,32,128]{2,1,0:T(8,128)(2,1)S(1)}, u32[]{:S(2)}, u32[]{:S(2)}) collective-permute-start(bf16[16,32,128]{2,1,0:T(8,128)(2,1)S(1)} %get-tuple-element.33), channel_id=1, source_target_pairs={{0,64},{32,96},{64,0},{96,32},{1,65},{33,97},{65,1},{97,33},{2,66}... | collective-permute-start | bytes 393224 | tf_op jit(solution)/shard_map/ppermute | solution.py:638
  96.9 1.1 collective-permute-start.8
  98.0 15.8 %all-to-all-done.2.recv_ref = bf16[128,48,128]{2,1,0:T(8,128)(2,1)S(1)} async-done(((bf16[128,48,128]{2,1,0:T(8,128)(2,1)}), bf16[128,48,128]{2,1,0:T(8,128)(2,1)S(1)}, u32[]{:S(2)}, u32[]{:S(2)}) %all-to-all-start.2) | async-done | bytes 1572896 | tf_op jit(solution)/shard_map/all_to_all | solution.py:646
  113.8 0.9 sum_piece.1
  114.7 4.7 %all-to-all-start.3 = ((bf16[128,16,128]{2,1,0:T(8,128)(2,1)}), bf16[128,16,128]{2,1,0:T(8,128)(2,1)S(1)}, u32[]{:S(2)}, u32[]{:S(2)}) async-start(bf16[128,16,128]{2,1,0:T(8,128)(2,1)} %sum_piece.1), calls=%async_computation.3 | async-start | bytes 1048576 | tf_op jit(solution)/shard_map/all_to_all | solution.py:646
  119.4 0.0 collective-permute-done.6.a_ref
  119.4 0.0 collective-permute-done.7.b_ref
  119.4 3.1 %scatter_rows.1.m0 = bf16[16,32,128]{2,1,0:T(8,128)(2,1)S(1)} custom-call(s32[1,32]{1,0:T(1,128)} %count_ref.3, s32[32,128]{1,0:T(8,128)S(1)} %bitcast.15, bf16[128,48,128]{2,1,0:T(8,128)(2,1)S(1)} %all-to-all-done.2.recv_ref, f32[16,32,128]{2,1,0:T(8,128)S(1)} %get-tuple-element.31.own_ref, bf16[16,32,128]{2,1,0:T(8,128)(2,1)S(1)} %collective-permute-done.6.a_ref, ...), custom_call_target="tpu_custom_call" | custom-call | flops 4000000000 | bytes 4000000 | tf_op jit(solution)/shard_map/scatter_rows/pallas_call | solution.py:567
  122.5 1.5 %collective-permute-start.9 = (bf16[16,32,128]{2,1,0:T(8,128)(2,1)S(1)}, bf16[16,32,128]{2,1,0:T(8,128)(2,1)S(1)}, u32[]{:S(2)}, u32[]{:S(2)}) collective-permute-start(bf16[16,32,128]{2,1,0:T(8,128)(2,1)S(1)} %scatter_rows.1.m0), channel_id=1, source_target_pairs={{0,32},{32,64},{64,96},{96,0},{1,33},{33,65},{65,97},{97,1},{2,34}... | collective-permute-start | bytes 393224 | tf_op jit(solution)/shard_map/ppermute | solution.py:638
  124.0 2.5 %collective-permute-start.10 = (bf16[16,32,128]{2,1,0:T(8,128)(2,1)S(1)}, bf16[16,32,128]{2,1,0:T(8,128)(2,1)S(1)}, u32[]{:S(2)}, u32[]{:S(2)}) collective-permute-start(bf16[16,32,128]{2,1,0:T(8,128)(2,1)S(1)} %scatter_rows.1.m0), channel_id=1, source_target_pairs={{0,64},{32,96},{64,0},{96,32},{1,65},{33,97},{65,1},{97,33},{2,66}... | collective-permute-start | bytes 393224 | tf_op jit(solution)/shard_map/ppermute | solution.py:638
  126.5 1.1 collective-permute-start.11
  127.7 4.0 %collective-permute-done.9.m1 = bf16[16,32,128]{2,1,0:T(8,128)(2,1)S(1)} collective-permute-done((bf16[16,32,128]{2,1,0:T(8,128)(2,1)S(1)}, bf16[16,32,128]{2,1,0:T(8,128)(2,1)S(1)}, u32[]{:S(2)}, u32[]{:S(2)}) %collective-permute-start.9) | collective-permute-done | bytes 131104 | tf_op jit(solution)/shard_map/ppermute | solution.py:638
  131.7 3.4 %collective-permute-done.10.m2 = bf16[16,32,128]{2,1,0:T(8,128)(2,1)S(1)} collective-permute-done((bf16[16,32,128]{2,1,0:T(8,128)(2,1)S(1)}, bf16[16,32,128]{2,1,0:T(8,128)(2,1)S(1)}, u32[]{:S(2)}, u32[]{:S(2)}) %collective-permute-start.10) | collective-permute-done | bytes 131104 | tf_op jit(solution)/shard_map/ppermute | solution.py:638
  135.1 0.0 all-to-all-done.3.shared_ref
  135.1 2.1 %finish.1 = (f32[2048,128]{1,0:T(8,128)}, f32[128,256]{1,0:T(8,128)}) custom-call(s32[2]{0:T(128)S(1)} %pad_add_fusion.place_ref.rep_ref, s32[8]{0:T(128)} %hub_ref.3, bf16[16,32,128]{2,1,0:T(8,128)(2,1)S(1)} %scatter_rows.1.m0, bf16[16,32,128]{2,1,0:T(8,128)(2,1)S(1)} %collective-permute-done.9.m1, bf16[16,32,128]{2,1,0:T(8,128)(2,1)S(1)} %collective-permute-done.10.m2, ...), custom_call_target="tpu_custom_call" | custom-call | tf_op jit(solution)/shard_map/finish/pallas_call | solution.py:623
  (15 shorter events, 0.1 us)
Async XLA Ops:
  2.6 18.4 %all-to-all-start = ((bf16[32,32,128]{2,1,0:T(8,128)(2,1)}), bf16[32,32,128]{2,1,0:T(8,128)(2,1)S(1)}, u32[]{:S(2)}, u32[]{:S(2)}) async-start(bf16[32,32,128]{2,1,0:T(8,128)(2,1)} %bitcast.4), calls=%async_computation | async-start | bytes 524288 | tf_op jit(solution)/shard_map/all_to_all | solution.py:646
  21.8 4.6 %copy-start.5 = (s32[1,1,384]{2,1,0:T(1,128)S(1)}, s32[1,1,384]{2,1,0:T(1,128)}, u32[]{:S(2)}) copy-start(s32[1,1,384]{2,1,0:T(1,128)} %param.17) | copy-start | bytes 4612
  21.9 4.6 %copy-start.6 = (s32[1,1,384]{2,1,0:T(1,128)S(1)}, s32[1,1,384]{2,1,0:T(1,128)}, u32[]{:S(2)}) copy-start(s32[1,1,384]{2,1,0:T(1,128)} %param.18) | copy-start | bytes 4612
  21.9 5.9 %copy-start = (bf16[2048,128]{1,0:T(8,128)(2,1)S(1)}, bf16[2048,128]{1,0:T(8,128)(2,1)}, u32[]{:S(2)}) copy-start(bf16[2048,128]{1,0:T(8,128)(2,1)} %feat_hbm.1) | copy-start | bytes 1572868
  21.9 24.3 %all-to-all-start.1 = ((bf16[32,160,128]{2,1,0:T(8,128)(2,1)}), bf16[32,160,128]{2,1,0:T(8,128)(2,1)S(1)}, u32[]{:S(2)}, u32[]{:S(2)}) async-start(bf16[32,160,128]{2,1,0:T(8,128)(2,1)} %insert_hubs.1), calls=%async_computation.1 | async-start | bytes 2621440 | tf_op jit(solution)/shard_map/all_to_all | solution.py:646
  52.7 9.8 %collective-permute-start = (bf16[4,128,128]{2,1,0:T(8,128)(2,1)S(1)}, bf16[4,128,128]{2,1,0:T(8,128)(2,1)S(1)}, u32[]{:S(2)}, u32[]{:S(2)}) collective-permute-start(bf16[4,128,128]{2,1,0:T(8,128)(2,1)S(1)} %get-tuple-element.22.after_ref), channel_id=1, source_target_pairs={{0,32},{32,64},{64,96},{96,0},{1,33},{33,65},{65,97},{97,1},{2,34}... | collective-permute-start | bytes 393224 | tf_op jit(solution)/shard_map/ppermute | solution.py:638
  54.6 7.8 %collective-permute-start.1 = (bf16[4,128,128]{2,1,0:T(8,128)(2,1)S(1)}, bf16[4,128,128]{2,1,0:T(8,128)(2,1)S(1)}, u32[]{:S(2)}, u32[]{:S(2)}) collective-permute-start(bf16[4,128,128]{2,1,0:T(8,128)(2,1)S(1)} %get-tuple-element.24), channel_id=1, source_target_pairs={{0,64},{32,96},{64,0},{96,32},{1,65},{33,97},{65,1},{97,33},{2,66}... | collective-permute-start | bytes 393224 | tf_op jit(solution)/shard_map/ppermute | solution.py:638
  56.7 14.4 %copy-start.1 = (bf16[2048,256]{1,0:T(8,128)(2,1)S(1)}, bf16[2048,256]{1,0:T(8,128)(2,1)}, u32[]{:S(2)}) copy-start(bf16[2048,256]{1,0:T(8,128)(2,1)} %cot_ref.1) | copy-start | bytes 3145732
  56.7 14.4 %copy-start.2 = (bf16[128,256]{1,0:T(8,128)(2,1)S(1)}, bf16[128,256]{1,0:T(8,128)(2,1)}, u32[]{:S(2)}) copy-start(bf16[128,256]{1,0:T(8,128)(2,1)} %w_ref.1) | copy-start | bytes 196612
  56.7 14.4 %copy-start.4 = (f32[256]{0:T(256)S(1)}, f32[256]{0:T(256)}, u32[]{:S(2)}) copy-start(f32[256]{0:T(256)} %param.12) | copy-start | bytes 3076
  56.7 5.8 %collective-permute-start.2 = (bf16[4,128,128]{2,1,0:T(8,128)(2,1)S(1)}, bf16[4,128,128]{2,1,0:T(8,128)(2,1)S(1)}, u32[]{:S(2)}, u32[]{:S(2)}) collective-permute-start(bf16[4,128,128]{2,1,0:T(8,128)(2,1)S(1)} %get-tuple-element.25), channel_id=1, source_target_pairs={{0,96},{32,0},{64,32},{96,64},{1,97},{33,1},{65,33},{97,65},{2,98}... | collective-permute-start | bytes 393224 | tf_op jit(solution)/shard_map/ppermute | solution.py:638
  62.6 5.1 %collective-permute-start.3 = (bf16[4,128,128]{2,1,0:T(8,128)(2,1)S(1)}, bf16[4,128,128]{2,1,0:T(8,128)(2,1)S(1)}, u32[]{:S(2)}, u32[]{:S(2)}) collective-permute-start(bf16[4,128,128]{2,1,0:T(8,128)(2,1)S(1)} %sum_quarter.1.z0), channel_id=1, source_target_pairs={{0,32},{32,64},{64,96},{96,0},{1,33},{33,65},{65,97},{97,1},{2,34}... | collective-permute-start | bytes 393224 | tf_op jit(solution)/shard_map/ppermute | solution.py:638
  63.6 7.3 %collective-permute-start.4 = (bf16[4,128,128]{2,1,0:T(8,128)(2,1)S(1)}, bf16[4,128,128]{2,1,0:T(8,128)(2,1)S(1)}, u32[]{:S(2)}, u32[]{:S(2)}) collective-permute-start(bf16[4,128,128]{2,1,0:T(8,128)(2,1)S(1)} %sum_quarter.1.z0), channel_id=1, source_target_pairs={{0,64},{32,96},{64,0},{96,32},{1,65},{33,97},{65,1},{97,33},{2,66}... | collective-permute-start | bytes 393224 | tf_op jit(solution)/shard_map/ppermute | solution.py:638
  66.0 5.0 %collective-permute-start.5 = (bf16[4,128,128]{2,1,0:T(8,128)(2,1)S(1)}, bf16[4,128,128]{2,1,0:T(8,128)(2,1)S(1)}, u32[]{:S(2)}, u32[]{:S(2)}) collective-permute-start(bf16[4,128,128]{2,1,0:T(8,128)(2,1)S(1)} %sum_quarter.1.z0), channel_id=1, source_target_pairs={{0,96},{32,0},{64,32},{96,64},{1,97},{33,1},{65,33},{97,65},{2,98}... | collective-permute-start | bytes 393224 | tf_op jit(solution)/shard_map/ppermute | solution.py:638
  81.3 32.5 %all-to-all-start.2 = ((bf16[128,48,128]{2,1,0:T(8,128)(2,1)}), bf16[128,48,128]{2,1,0:T(8,128)(2,1)S(1)}, u32[]{:S(2)}, u32[]{:S(2)}) async-start(bf16[128,48,128]{2,1,0:T(8,128)(2,1)} %bitcast.7), calls=%async_computation.2 | async-start | bytes 3145728 | tf_op jit(solution)/shard_map/all_to_all | solution.py:646
  92.9 26.4 %collective-permute-start.6 = (bf16[16,32,128]{2,1,0:T(8,128)(2,1)S(1)}, bf16[16,32,128]{2,1,0:T(8,128)(2,1)S(1)}, u32[]{:S(2)}, u32[]{:S(2)}) collective-permute-start(bf16[16,32,128]{2,1,0:T(8,128)(2,1)S(1)} %get-tuple-element.32), channel_id=1, source_target_pairs={{0,32},{32,64},{64,96},{96,0},{1,33},{33,65},{65,97},{97,1},{2,34}... | collective-permute-start | bytes 393224 | tf_op jit(solution)/shard_map/ppermute | solution.py:638
  94.4 24.9 %collective-permute-start.7 = (bf16[16,32,128]{2,1,0:T(8,128)(2,1)S(1)}, bf16[16,32,128]{2,1,0:T(8,128)(2,1)S(1)}, u32[]{:S(2)}, u32[]{:S(2)}) collective-permute-start(bf16[16,32,128]{2,1,0:T(8,128)(2,1)S(1)} %get-tuple-element.33), channel_id=1, source_target_pairs={{0,64},{32,96},{64,0},{96,32},{1,65},{33,97},{65,1},{97,33},{2,66}... | collective-permute-start | bytes 393224 | tf_op jit(solution)/shard_map/ppermute | solution.py:638
  96.9 22.5 %copy-start.3 = (s32[1,32,128]{2,1,0:T(8,128)S(1)}, s32[1,32,128]{2,1,0:T(8,128)}, u32[]{:S(2)}) copy-start(s32[1,32,128]{2,1,0:T(8,128)} %param.14) | copy-start | bytes 49156
  96.9 22.5 %collective-permute-start.8 = (bf16[16,32,128]{2,1,0:T(8,128)(2,1)S(1)}, bf16[16,32,128]{2,1,0:T(8,128)(2,1)S(1)}, u32[]{:S(2)}, u32[]{:S(2)}) collective-permute-start(bf16[16,32,128]{2,1,0:T(8,128)(2,1)S(1)} %get-tuple-element.34), channel_id=1, source_target_pairs={{0,96},{32,0},{64,32},{96,64},{1,97},{33,1},{65,33},{97,65},{2,98}... | collective-permute-start | bytes 393224 | tf_op jit(solution)/shard_map/ppermute | solution.py:638
  114.7 20.4 %all-to-all-start.3 = ((bf16[128,16,128]{2,1,0:T(8,128)(2,1)}), bf16[128,16,128]{2,1,0:T(8,128)(2,1)S(1)}, u32[]{:S(2)}, u32[]{:S(2)}) async-start(bf16[128,16,128]{2,1,0:T(8,128)(2,1)} %sum_piece.1), calls=%async_computation.3 | async-start | bytes 1048576 | tf_op jit(solution)/shard_map/all_to_all | solution.py:646
  122.5 9.2 %collective-permute-start.9 = (bf16[16,32,128]{2,1,0:T(8,128)(2,1)S(1)}, bf16[16,32,128]{2,1,0:T(8,128)(2,1)S(1)}, u32[]{:S(2)}, u32[]{:S(2)}) collective-permute-start(bf16[16,32,128]{2,1,0:T(8,128)(2,1)S(1)} %scatter_rows.1.m0), channel_id=1, source_target_pairs={{0,32},{32,64},{64,96},{96,0},{1,33},{33,65},{65,97},{97,1},{2,34}... | collective-permute-start | bytes 393224 | tf_op jit(solution)/shard_map/ppermute | solution.py:638
  124.0 11.1 %collective-permute-start.10 = (bf16[16,32,128]{2,1,0:T(8,128)(2,1)S(1)}, bf16[16,32,128]{2,1,0:T(8,128)(2,1)S(1)}, u32[]{:S(2)}, u32[]{:S(2)}) collective-permute-start(bf16[16,32,128]{2,1,0:T(8,128)(2,1)S(1)} %scatter_rows.1.m0), channel_id=1, source_target_pairs={{0,64},{32,96},{64,0},{96,32},{1,65},{33,97},{65,1},{97,33},{2,66}... | collective-permute-start | bytes 393224 | tf_op jit(solution)/shard_map/ppermute | solution.py:638
  126.5 8.6 %collective-permute-start.11 = (bf16[16,32,128]{2,1,0:T(8,128)(2,1)S(1)}, bf16[16,32,128]{2,1,0:T(8,128)(2,1)S(1)}, u32[]{:S(2)}, u32[]{:S(2)}) collective-permute-start(bf16[16,32,128]{2,1,0:T(8,128)(2,1)S(1)} %scatter_rows.1.m0), channel_id=1, source_target_pairs={{0,96},{32,0},{64,32},{96,64},{1,97},{33,1},{65,33},{97,65},{2,98}... | collective-permute-start | bytes 393224 | tf_op jit(solution)/shard_map/ppermute | solution.py:638
